TPU v7x, 32 devices: a whole 2x2x4 slice. The times are simulated.
32 devices in a mesh: grp: 2 (over core), seq: 4 (over z), head: 4 (over y, x).
Axes of the slice: x: 2, y: 2, z: 4, core: 2. Of those that a mesh axis runs over, the one named last changes fastest.
Arguments:
- queries: bfloat16 [768, 64, 128], P('seq', ('grp', 'head')), may hold values from -6 to 6
- keys: bfloat16 [768, 64, 128], P('seq', ('grp', 'head')), may hold values from -6 to 6
- values: bfloat16 [768, 64, 128], P('seq', ('grp', 'head')), may hold values from -6 to 6
- documents: int32 [768], P('seq'), may hold values from 0 to 3, never falling along the last dimension, each value on 1 to 576 neighbouring positions
- feature_map: float32 [64, 128, 128], P(('grp', 'head')), may hold values from -8 to 8
Outputs:
- teacher_out: bfloat16 [768, 64, 128], P('seq', ('grp', 'head'))
- student_out: bfloat16 [768, 64, 128], P('seq', ('grp', 'head'))
- loss: float32 [], replicated
- feature_grad: float32 [64, 128, 128], P(('grp', 'head'))
All inputs are finite; a program needn't handle non-finite values.
Results may differ from a plain program's by a relative error of at most 0.006.
Values may be sent and summed in bfloat16 or wider, within the bound.
No kernel may reach another device: no remote copies, remote signals or barrier semaphores. Data moves between devices by JAX's collectives and lax.ppermute only.
A program may use at most 192 MiB of HBM per device.

v0:
```python
import jax
import jax.numpy as jnp
from jax import lax
from jax.sharding import PartitionSpec as P

WINDOW = 64


exact_mode = lax.Precision.HIGHEST
masked_value = -1e30


def passed_along(block, axis, distance):
    devices = range(lax.axis_size(axis))
    route = [(i - distance, i) for i in devices if i - distance in devices]
    return lax.ppermute(block, axis, route)


def features(inputs, weights):
    logits = jnp.einsum("rhd,hdf->rhf", inputs, weights, precision=exact_mode)
    return jnp.concatenate(
        [jax.nn.softmax(logits, axis=-1), jax.nn.softmax(-logits, axis=-1)], axis=-1
    )


def join_up(earlier, later):
    merged_tag = jnp.maximum(earlier[0], later[0])
    early_keep = (earlier[0] == merged_tag).astype(earlier[1].dtype)
    late_keep = (later[0] == merged_tag).astype(later[1].dtype)
    return (
        merged_tag,
        early_keep * earlier[1] + late_keep * later[1],
        early_keep * earlier[2] + late_keep * later[2],
    )


def join_down(earlier, later):
    merged_tag = jnp.minimum(earlier[0], later[0])
    early_keep = (earlier[0] == merged_tag).astype(earlier[1].dtype)
    late_keep = (later[0] == merged_tag).astype(later[1].dtype)
    return (
        merged_tag,
        early_keep * earlier[1] + late_keep * later[1],
        early_keep * earlier[2] + late_keep * later[2],
    )


def body(queries, keys, values, documents, feature_map):
    tok_rows, head_count, head_width = queries.shape
    half_feat = feature_map.shape[2] // 2
    score_scale = head_width ** (-0.5)
    seq_place = lax.axis_index("seq")
    seq_count = lax.axis_size("seq")
    first_row = seq_place * tok_rows
    doc_float = documents.astype(jnp.float32)
    doc_marks = (documents + 1).astype(jnp.bfloat16)
    query_pos = first_row + jnp.arange(tok_rows)

    def attend(carried, portion):
        key_piece, value_piece, mark_piece = portion
        key_pos = jnp.arange(key_piece.shape[0])
        same_doc = mark_piece.astype(jnp.float32)[None, :] - 1.0 == doc_float[:, None]
        allowed = (same_doc & (key_pos[None, :] <= query_pos[:, None]))[:, None, :]
        scores = (
            jnp.einsum("ihd,jhd->ihj", queries, key_piece, preferred_element_type=jnp.float32)
            * score_scale
        )
        scores = jnp.where(allowed, scores, masked_value)
        row_max, totals, numerator = carried
        new_max = jnp.maximum(row_max, jnp.max(scores, axis=-1))
        probabilities = jnp.where(allowed, jnp.exp(scores - new_max[:, :, None]), 0.0)
        totals = jnp.sum(probabilities, axis=-1)
        numerator = jnp.einsum(
            "ihj,jhd->ihd",
            probabilities.astype(jnp.bfloat16),
            value_piece,
            preferred_element_type=jnp.float32,
        )
        return (new_max, totals, numerator)

    start_carry = (
        jnp.full((tok_rows, head_count), masked_value, jnp.float32),
        jnp.zeros((tok_rows, head_count), jnp.float32),
        jnp.zeros((tok_rows, head_count, head_width), jnp.float32),
    )
    portion = (
        lax.all_gather(keys, "seq", axis=0, tiled=True),
        lax.all_gather(values, "seq", axis=0, tiled=True),
        lax.all_gather(doc_marks, "seq", axis=0, tiled=True),
    )
    touches = (jnp.int32(0) < first_row + tok_rows) & (
        portion[2][-1].astype(jnp.float32) - 1.0 >= doc_float[0]
    )

    def compute_update(held_carry):
        return attend(held_carry, portion)

    def keep_carry(held_carry):
        return held_carry

    row_max, totals, numerator = lax.cond(touches, compute_update, keep_carry, start_carry)
    teacher_out = (numerator / totals[:, :, None]).astype(jnp.bfloat16)
    target = teacher_out.astype(jnp.float32)
    halo_keys, halo_values, halo_marks = passed_along(
        (keys[tok_rows - WINDOW :], values[tok_rows - WINDOW :], doc_marks[tok_rows - WINDOW :]),
        "seq",
        1,
    )
    key_joined = jnp.concatenate([halo_keys, keys], axis=0)
    key_float = key_joined.astype(jnp.float32)
    value_float = jnp.concatenate([halo_values, values], axis=0).astype(jnp.float32)
    doc_all = jnp.concatenate([halo_marks.astype(jnp.float32) - 1.0, doc_float], axis=0)
    query_float = queries.astype(jnp.float32)
    distance = jnp.arange(tok_rows)[:, None] + WINDOW - jnp.arange(tok_rows + WINDOW)[None, :]
    same_doc = doc_float[:, None] == doc_all[None, :]
    in_window = same_doc & (distance >= 0) & (distance < WINDOW)
    beyond = same_doc & (distance >= WINDOW)
    scores = (
        jnp.einsum("ihd,jhd->hij", queries, key_joined, preferred_element_type=jnp.float32)
        * score_scale
    )
    window_row = jnp.max(jnp.where(in_window[None], scores, masked_value), axis=-1, keepdims=True)
    window_weight = jnp.where(in_window[None], jnp.exp(scores - window_row), 0.0)
    elem_keys = key_float[:tok_rows]
    elem_values = value_float[:tok_rows]
    elem_docs = doc_all[:tok_rows]
    elem_tag = elem_docs[tok_rows - 1]
    in_tail = (elem_docs == elem_tag).astype(jnp.float32)

    def element(weights):
        masked_feat = features(elem_keys, weights[:, :, half_feat:]) * in_tail[:, None, None]
        return (
            jnp.einsum("jhf,jhd->hfd", masked_feat, elem_values, precision=exact_mode),
            jnp.sum(masked_feat, axis=0),
        )

    (elem_state, elem_norm), element_pullback = jax.vjp(element, feature_map)
    blank_state = jnp.zeros_like(elem_state)
    blank_norm = jnp.zeros_like(elem_norm)
    forward_blank = (jnp.float32(-2.0), blank_state, blank_norm)

    def relay_step(turn_index, carried):
        arrived = passed_along(join_up(carried, (elem_tag, elem_state, elem_norm)), "seq", 1)
        return jax.tree.map(
            lambda received, blank_entry: jnp.where(seq_place == 0, blank_entry, received),
            arrived,
            forward_blank,
        )

    tag_in, state_in, norm_in = lax.fori_loop(0, seq_count - 1, relay_step, forward_blank)
    uses_state = (doc_float == tag_in).astype(jnp.float32)[:, None]
    normaliser = 1.0 / (tok_rows * seq_count * head_count * lax.axis_size(("grp", "head")))

    def local_loss(weights, state, norm):
        query_feat = features(query_float, weights[:, :, :half_feat])
        key_feat = features(key_float, weights[:, :, half_feat:])
        linear = jnp.where(
            beyond[None],
            jnp.einsum("ihf,jhf->hij", query_feat, key_feat, precision=exact_mode),
            0.0,
        )
        weight = window_weight + linear
        numer_sum = jnp.einsum("hij,jhd->ihd", weight, value_float, precision=exact_mode)
        numer_sum = numer_sum + uses_state[:, :, None] * jnp.einsum(
            "ihf,hfd->ihd", query_feat, state, precision=exact_mode
        )
        denominator = jnp.sum(weight, axis=-1).T + uses_state * jnp.einsum(
            "ihf,hf->ih", query_feat, norm, precision=exact_mode
        )
        output = numer_sum / denominator[:, :, None]
        return (jnp.sum(jnp.square(output - target)) * normaliser, output)

    local_part, local_pullback, output = jax.vjp(
        local_loss, feature_map, state_in, norm_in, has_aux=True
    )
    grad_direct, grad_state, grad_norm = local_pullback(jnp.ones_like(local_part))
    backward_blank = (jnp.float32(1000000000.0), blank_state, blank_norm)

    def return_step(turn_index, carried):
        arrived = passed_along(join_down(carried, (tag_in, grad_state, grad_norm)), "seq", -1)
        return jax.tree.map(
            lambda received, blank_entry: jnp.where(
                seq_place == seq_count - 1, blank_entry, received
            ),
            arrived,
            backward_blank,
        )

    back_tag, carried_state, carried_norm = lax.fori_loop(
        0, seq_count - 1, return_step, backward_blank
    )
    total_grad = grad_direct + element_pullback((carried_state, carried_norm))[0]
    feature_grad = lax.psum(total_grad, "seq")
    loss_total = lax.psum(local_part, ("grp", "seq", "head"))
    return (teacher_out, output.astype(jnp.bfloat16), loss_total, feature_grad)


def solution(mesh):
    in_specs = (
        P("seq", ("grp", "head"), None),
        P("seq", ("grp", "head"), None),
        P("seq", ("grp", "head"), None),
        P("seq"),
        P(("grp", "head"), None, None),
    )
    out_specs = (
        P("seq", ("grp", "head"), None),
        P("seq", ("grp", "head"), None),
        P(),
        P(("grp", "head"), None, None),
    )
    return jax.shard_map(body, mesh=mesh, in_specs=in_specs, out_specs=out_specs, check_vma=False)
```

profile of v0, /device:TPU:0, one launch (start us, length us, event | category | flops | bytes accessed | tf_op | source)
XLA Modules:
  0.0 273.3 jit_solution(8016053413023378515)
XLA Ops:
  7.2 1.9 copy.35
  10.5 5.5 %collective-permute-start.7 = (bf16[64]{0:T(256)(128)(2,1)}, bf16[64]{0:T(256)(128)(2,1)}, u32[]{:S(2)}, u32[]{:S(2)}) collective-permute-start(bf16[64]{0:T(256)(128)(2,1)} %slice.39), channel_id=1, source_target_pairs={{0,4},{4,8},{8,12},{1,5},{5,9},{9,13},{2,6},{6,10},{10,14},{3,7},{... | collective-permute-start | bytes 392 | tf_op jit(solution)/shard_map/ppermute | solution.py:16
  17.5 3.5 %collective-permute-start.8 = (bf16[64,8,128]{2,0,1:T(8,128)(2,1)}, bf16[64,8,128]{2,0,1:T(8,128)(2,1)}, u32[]{:S(2)}, u32[]{:S(2)}) collective-permute-start(bf16[64,8,128]{2,0,1:T(8,128)(2,1)} %slice.48), channel_id=1, source_target_pairs={{0,4},{4,8},{8,12},{1,5},{5,9},{9,13},{2,6},{6,10},{10,14},{3,7},{... | collective-permute-start | bytes 393224 | tf_op jit(solution)/shard_map/ppermute | solution.py:16
  23.5 3.5 %collective-permute-start.6 = (bf16[64,8,128]{2,0,1:T(8,128)(2,1)}, bf16[64,8,128]{2,0,1:T(8,128)(2,1)}, u32[]{:S(2)}, u32[]{:S(2)}) collective-permute-start(bf16[64,8,128]{2,0,1:T(8,128)(2,1)} %slice.47), channel_id=1, source_target_pairs={{0,4},{4,8},{8,12},{1,5},{5,9},{9,13},{2,6},{6,10},{10,14},{3,7},{... | collective-permute-start | bytes 393224 | tf_op jit(solution)/shard_map/ppermute | solution.py:16
  32.4 8.7 %all-reduce.3 = bf16[768]{0:T(1024)(128)(2,1)S(1)} all-reduce(bf16[768]{0:T(1024)(128)(2,1)S(1)} %dynamic-update-slice), channel_id=1, replica_groups=mesh['grp'=2,'seq'=4,'head'=4] {'seq'}, use_global_device_ids=true, to_apply=%add.3 | all-reduce | flops 768 | bytes 3072
  58.7 3.2 %fusion.48 = f32[8,192,256]{2,1,0:T(8,128)} fusion(f32[256,8,64]{0,2,1:T(8,128)S(1)} %get-tuple-element.370, f32[256,8,64]{0,2,1:T(8,128)S(1)} %get-tuple-element.371, f32[192,8,64]{0,2,1:T(8,128)S(1)} %get-tuple-element.372, f32[192,8,64]{0,2,1:T(8,128)S(1)} %get-tuple-element.373), kind=kOutput, calls=%fused_computation.75 | convolution fusion | flops 604438528 | bytes 3407872 | tf_op jit(solution)/shard_map/jvp(ihf,jhf->hij)/dot_general | solution.py:159
  61.9 70.8 %while.34 = (s32[]{:T(128)}, f32[]{:T(128)}, f32[8,128,128]{2,1,0:T(8,128)S(1)}, f32[8,128]{1,0:T(8,128)S(1)}, f32[]{:T(128)}, /*index=5*/pred[]{:T(512)}, f32[8...) while((s32[]{:T(128)}, f32[]{:T(128)}, ...), condition=%wide.region_19.20_spmd.clone, body=%wide.region_18.19_spmd.clone.sunk | while | flops 660489 | bytes 4755783 | solution.py:150
  63.1 4.4 %collective-permute-start.1 = (f32[8,128,128]{2,1,0:T(8,128)S(1)}, f32[8,128,128]{2,1,0:T(8,128)}, u32[]{:S(2)}, u32[]{:S(2)}) collective-permute-start(f32[8,128,128]{2,1,0:T(8,128)S(1)} %fusion.172), channel_id=1, source_target_pairs={{0,4},{4,8},{8,12},{1,5},{5,9},{9,13},{2,6},{6,10},{10,14},{3,7},{... | collective-permute-start | bytes 1572872 | tf_op jit(solution)/shard_map/while/body/eval_jaxpr/ppermute | solution.py:16
  67.5 1.9 collective-permute-start.2
  69.4 19.6 %collective-permute-start = (f32[]{:T(128)}, f32[]{:T(128)}, u32[]{:S(2)}, u32[]{:S(2)}) collective-permute-start(f32[]{:T(128)} %max.7), channel_id=1, source_target_pairs={{0,4},{4,8},{8,12},{1,5},{5,9},{9,13},{2,6},{6,10},{10,14},{3,7},{... | collective-permute-start | bytes 20 | tf_op jit(solution)/shard_map/while/body/eval_jaxpr/ppermute | solution.py:16
  91.0 11.8 %collective-permute-start.1 = (f32[8,128,128]{2,1,0:T(8,128)S(1)}, f32[8,128,128]{2,1,0:T(8,128)}, u32[]{:S(2)}, u32[]{:S(2)}) collective-permute-start(f32[8,128,128]{2,1,0:T(8,128)S(1)} %fusion.172), channel_id=1, source_target_pairs={{0,4},{4,8},{8,12},{1,5},{5,9},{9,13},{2,6},{6,10},{10,14},{3,7},{... | collective-permute-start | bytes 1572872 | tf_op jit(solution)/shard_map/while/body/eval_jaxpr/ppermute | solution.py:16
  102.9 7.5 %collective-permute-start.2 = (f32[8,128]{1,0:T(8,128)S(1)}, f32[8,128]{1,0:T(8,128)S(1)}, u32[]{:S(2)}, u32[]{:S(2)}) collective-permute-start(f32[8,128]{1,0:T(8,128)S(1)} %fusion.173), channel_id=1, source_target_pairs={{0,4},{4,8},{8,12},{1,5},{5,9},{9,13},{2,6},{6,10},{10,14},{3,7},{... | collective-permute-start | bytes 12296 | tf_op jit(solution)/shard_map/while/body/eval_jaxpr/ppermute | solution.py:16
  110.4 5.6 %collective-permute-start = (f32[]{:T(128)}, f32[]{:T(128)}, u32[]{:S(2)}, u32[]{:S(2)}) collective-permute-start(f32[]{:T(128)} %max.7), channel_id=1, source_target_pairs={{0,4},{4,8},{8,12},{1,5},{5,9},{9,13},{2,6},{6,10},{10,14},{3,7},{... | collective-permute-start | bytes 20 | tf_op jit(solution)/shard_map/while/body/eval_jaxpr/ppermute | solution.py:16
  118.1 5.9 %collective-permute-start.1 = (f32[8,128,128]{2,1,0:T(8,128)S(1)}, f32[8,128,128]{2,1,0:T(8,128)}, u32[]{:S(2)}, u32[]{:S(2)}) collective-permute-start(f32[8,128,128]{2,1,0:T(8,128)S(1)} %fusion.172), channel_id=1, source_target_pairs={{0,4},{4,8},{8,12},{1,5},{5,9},{9,13},{2,6},{6,10},{10,14},{3,7},{... | collective-permute-start | bytes 1572872 | tf_op jit(solution)/shard_map/while/body/eval_jaxpr/ppermute | solution.py:16
  124.0 2.3 collective-permute-start.2
  126.3 5.6 %collective-permute-start = (f32[]{:T(128)}, f32[]{:T(128)}, u32[]{:S(2)}, u32[]{:S(2)}) collective-permute-start(f32[]{:T(128)} %max.7), channel_id=1, source_target_pairs={{0,4},{4,8},{8,12},{1,5},{5,9},{9,13},{2,6},{6,10},{10,14},{3,7},{... | collective-permute-start | bytes 20 | tf_op jit(solution)/shard_map/while/body/eval_jaxpr/ppermute | solution.py:16
  138.2 2.0 fusion.149
  140.2 2.7 convolution_multiply_fusion.1
  143.0 6.4 %conditional.1 = (f32[192,8]{0,1:T(8,128)S(1)}, f32[192,8,128]{2,0,1:T(8,128)S(1)}) conditional(s32[]{:T(128)} %convert_element_type.63, () %tuple.40, (bf16[768]{0:T(1024)(128)(2,1)S(1)}, f32[192]{0:T(256)S(1)}, s32[]{:T(128)}, s32[192]{0:T(256)S(1)}, bf16[768,8,128]{2,0,1:T(8,128)(2,1)}, /*index=5*/bf16[192,8,128]{2,1,0:T(8,128)(2,1)S(1)}, ...), branch_computations={%region_0.0_spmd, %region_1.4_spmd} | conditional | flops 619757760 | bytes 25410096 | solution.py:101
  143.4 2.6 fusion
  146.1 1.8 fusion.6
  149.4 4.0 %multiply_reduce_fusion = (f32[192,8]{0,1:T(8,128)S(1)}, f32[]{:T(128)}, bf16[192,8,128]{2,0,1:T(8,128)(2,1)S(1)}, bf16[192,8,128]{2,0,1:T(8,128)(2,1)}, f32[192,8,128]{2,0,1:T(8,128)S(1)}) fusion(f32[192,8]{0,1:T(8,128)S(1)} %get-tuple-element.344, f32[192,8]{0,1:T(8,128)S(1)} %get-tuple-element.345, f32[192,8,128]{2,0,1:T(8,128)S(1)} %get-tuple-element.220, ...), kind=kOutput, calls=%fused_computation.83 | convolution fusion | flops 606337536 | bytes 5267460 | tf_op jit(solution)/shard_map/jvp(hij,jhd->ihd)/dot_general | solution.py:163
  154.1 2.1 fusion.51
  157.8 2.3 convolution_bitcast_fusion
  160.1 2.9 %fusion.47 = f32[8,192,128]{1,2,0:T(8,128)} fusion(f32[8,192,256]{2,1,0:T(8,128)S(1)} %add_select_fusion, f32[256,8,64]{0,2,1:T(8,128)S(1)} %copy-done.4, f32[256,8,64]{0,2,1:T(8,128)S(1)} %copy-done.6), kind=kOutput, calls=%fused_computation.74 | convolution fusion | flops 604241920 | bytes 3407872 | tf_op jit(solution)/shard_map/transpose(jvp(ihf,jhf->hij))/dot_general | solution.py:159
  163.8 47.9 %while.35 = (s32[]{:T(128)}, f32[]{:T(128)}, f32[8,128,128]{2,1,0:T(8,128)S(1)}, f32[8,128]{1,0:T(8,128)S(1)}, f32[]{:T(128)}, /*index=5*/pred[]{:T(512)}, f32[8...) while((s32[]{:T(128)}, f32[]{:T(128)}, ...), condition=%wide.region_29.30_spmd.clone, body=%wide.region_28.29_spmd.clone.sunk | while | flops 660489 | bytes 4755783 | solution.py:189
  167.9 13.8 %collective-permute-done.3 = f32[]{:T(128)} collective-permute-done((f32[]{:T(128)}, f32[]{:T(128)}, u32[]{:S(2)}, u32[]{:S(2)}) %collective-permute-start.3) | collective-permute-done | bytes 36 | tf_op jit(solution)/shard_map/while/body/eval_jaxpr/ppermute | solution.py:16
  186.4 12.5 %collective-permute-done.3 = f32[]{:T(128)} collective-permute-done((f32[]{:T(128)}, f32[]{:T(128)}, u32[]{:S(2)}, u32[]{:S(2)}) %collective-permute-start.3) | collective-permute-done | bytes 36 | tf_op jit(solution)/shard_map/while/body/eval_jaxpr/ppermute | solution.py:16
  203.7 7.2 %collective-permute-done.3 = f32[]{:T(128)} collective-permute-done((f32[]{:T(128)}, f32[]{:T(128)}, u32[]{:S(2)}, u32[]{:S(2)}) %collective-permute-start.3) | collective-permute-done | bytes 36 | tf_op jit(solution)/shard_map/while/body/eval_jaxpr/ppermute | solution.py:16
  214.9 1.8 fusion.33
  222.2 40.6 %psum.14 = f32[]{:T(128)} all-reduce(f32[]{:T(128)S(6)} %mul.316), channel_id=1, replica_groups=mesh['grp'=2,'seq'=4,'head'=4] {'grp','seq','head'}, use_global_device_ids=true, to_apply=%region_22.23 | all-reduce | flops 1 | bytes 8 | tf_op jit(solution)/shard_map/psum | solution.py:194
  264.8 2.0 copy.59
  (257 shorter events, 58.5 us)
Async XLA Ops:
  7.2 13.9 %copy-start.23 = (bf16[192,8,128]{2,1,0:T(8,128)(2,1)S(1)}, bf16[192,8,128]{2,1,0:T(8,128)(2,1)}, u32[]{:S(2)}) copy-start(bf16[192,8,128]{2,1,0:T(8,128)(2,1)} %param.13) | copy-start | bytes 1179652
  7.2 20.5 %copy-start.20 = (bf16[192,8,128]{2,1,0:T(8,128)(2,1)S(1)}, bf16[192,8,128]{2,1,0:T(8,128)(2,1)}, u32[]{:S(2)}) copy-start(bf16[192,8,128]{2,1,0:T(8,128)(2,1)} %param.11) | copy-start | bytes 1179652
  7.2 20.4 %copy-start.7 = (f32[8,128,128]{2,1,0:T(8,128)S(1)}, f32[8,128,128]{2,1,0:T(8,128)}, u32[]{:S(2)}) copy-start(f32[8,128,128]{2,1,0:T(8,128)} %param.15) | copy-start | bytes 1572868
  7.2 135.7 %all-gather.3.cloned.1.call-start = ((), (), s32[]{:S(2)}) async-start(), calls=%async_computation | async-start | bytes 1966080 | tf_op jit(solution)/shard_map/all_gather | solution.py:87
  9.2 133.8 %all-gather.5.cloned.1.call-start = ((), (), s32[]{:S(2)}) async-start(), calls=%async_computation.1 | async-start | bytes 1966080 | tf_op jit(solution)/shard_map/all_gather | solution.py:88
  10.0 20.5 %copy-start.50 = (f32[192]{0:T(256)}, f32[192]{0:T(256)S(1)}, u32[]{:S(2)}) copy-start(f32[192]{0:T(256)S(1)} %get-tuple-element.354) | copy-start | bytes 2308
  10.5 34.2 %collective-permute-start.7 = (bf16[64]{0:T(256)(128)(2,1)}, bf16[64]{0:T(256)(128)(2,1)}, u32[]{:S(2)}, u32[]{:S(2)}) collective-permute-start(bf16[64]{0:T(256)(128)(2,1)} %slice.39), channel_id=1, source_target_pairs={{0,4},{4,8},{8,12},{1,5},{5,9},{9,13},{2,6},{6,10},{10,14},{3,7},{... | collective-permute-start | bytes 392 | tf_op jit(solution)/shard_map/ppermute | solution.py:16
  17.5 30.7 %collective-permute-start.8 = (bf16[64,8,128]{2,0,1:T(8,128)(2,1)}, bf16[64,8,128]{2,0,1:T(8,128)(2,1)}, u32[]{:S(2)}, u32[]{:S(2)}) collective-permute-start(bf16[64,8,128]{2,0,1:T(8,128)(2,1)} %slice.48), channel_id=1, source_target_pairs={{0,4},{4,8},{8,12},{1,5},{5,9},{9,13},{2,6},{6,10},{10,14},{3,7},{... | collective-permute-start | bytes 393224 | tf_op jit(solution)/shard_map/ppermute | solution.py:16
  21.9 242.8 %all-reduce.6.cloned.1.call-start = ((), (), s32[]{:S(2)}) async-start(), calls=%async_computation.2 | async-start | bytes 1048576 | tf_op jit(solution)/shard_map/psum | solution.py:193
  23.5 32.4 %collective-permute-start.6 = (bf16[64,8,128]{2,0,1:T(8,128)(2,1)}, bf16[64,8,128]{2,0,1:T(8,128)(2,1)}, u32[]{:S(2)}, u32[]{:S(2)}) collective-permute-start(bf16[64,8,128]{2,0,1:T(8,128)(2,1)} %slice.47), channel_id=1, source_target_pairs={{0,4},{4,8},{8,12},{1,5},{5,9},{9,13},{2,6},{6,10},{10,14},{3,7},{... | collective-permute-start | bytes 393224 | tf_op jit(solution)/shard_map/ppermute | solution.py:16
  29.4 15.2 %copy-start.8 = (f32[192,8,64]{0,2,1:T(8,128)}, f32[192,8,64]{0,2,1:T(8,128)S(1)}, u32[]{:S(2)}) copy-start(f32[192,8,64]{0,2,1:T(8,128)S(1)} %get-tuple-element.362) | copy-start | bytes 1179652
  29.5 15.2 %copy-start.32 = (f32[192,8]{0,1:T(8,128)}, f32[192,8]{0,1:T(8,128)S(1)}, u32[]{:S(2)}) copy-start(f32[192,8]{0,1:T(8,128)S(1)} %get-tuple-element.361) | copy-start | bytes 18436
  30.4 13.1 %copy-start.34 = (f32[192,8]{0,1:T(8,128)}, f32[192,8]{0,1:T(8,128)S(1)}, u32[]{:S(2)}) copy-start(f32[192,8]{0,1:T(8,128)S(1)} %get-tuple-element.359) | copy-start | bytes 18436
  63.1 26.6 %collective-permute-start.1 = (f32[8,128,128]{2,1,0:T(8,128)S(1)}, f32[8,128,128]{2,1,0:T(8,128)}, u32[]{:S(2)}, u32[]{:S(2)}) collective-permute-start(f32[8,128,128]{2,1,0:T(8,128)S(1)} %fusion.172), channel_id=1, source_target_pairs={{0,4},{4,8},{8,12},{1,5},{5,9},{9,13},{2,6},{6,10},{10,14},{3,7},{... | collective-permute-start | bytes 1572872 | tf_op jit(solution)/shard_map/while/body/eval_jaxpr/ppermute | solution.py:16
  67.5 22.2 %collective-permute-start.2 = (f32[8,128]{1,0:T(8,128)S(1)}, f32[8,128]{1,0:T(8,128)S(1)}, u32[]{:S(2)}, u32[]{:S(2)}) collective-permute-start(f32[8,128]{1,0:T(8,128)S(1)} %fusion.173), channel_id=1, source_target_pairs={{0,4},{4,8},{8,12},{1,5},{5,9},{9,13},{2,6},{6,10},{10,14},{3,7},{... | collective-permute-start | bytes 12296 | tf_op jit(solution)/shard_map/while/body/eval_jaxpr/ppermute | solution.py:16
  69.4 19.6 %collective-permute-start = (f32[]{:T(128)}, f32[]{:T(128)}, u32[]{:S(2)}, u32[]{:S(2)}) collective-permute-start(f32[]{:T(128)} %max.7), channel_id=1, source_target_pairs={{0,4},{4,8},{8,12},{1,5},{5,9},{9,13},{2,6},{6,10},{10,14},{3,7},{... | collective-permute-start | bytes 20 | tf_op jit(solution)/shard_map/while/body/eval_jaxpr/ppermute | solution.py:16
  91.0 25.7 %collective-permute-start.1 = (f32[8,128,128]{2,1,0:T(8,128)S(1)}, f32[8,128,128]{2,1,0:T(8,128)}, u32[]{:S(2)}, u32[]{:S(2)}) collective-permute-start(f32[8,128,128]{2,1,0:T(8,128)S(1)} %fusion.172), channel_id=1, source_target_pairs={{0,4},{4,8},{8,12},{1,5},{5,9},{9,13},{2,6},{6,10},{10,14},{3,7},{... | collective-permute-start | bytes 1572872 | tf_op jit(solution)/shard_map/while/body/eval_jaxpr/ppermute | solution.py:16
  102.9 13.9 %collective-permute-start.2 = (f32[8,128]{1,0:T(8,128)S(1)}, f32[8,128]{1,0:T(8,128)S(1)}, u32[]{:S(2)}, u32[]{:S(2)}) collective-permute-start(f32[8,128]{1,0:T(8,128)S(1)} %fusion.173), channel_id=1, source_target_pairs={{0,4},{4,8},{8,12},{1,5},{5,9},{9,13},{2,6},{6,10},{10,14},{3,7},{... | collective-permute-start | bytes 12296 | tf_op jit(solution)/shard_map/while/body/eval_jaxpr/ppermute | solution.py:16
  110.4 5.6 %collective-permute-start = (f32[]{:T(128)}, f32[]{:T(128)}, u32[]{:S(2)}, u32[]{:S(2)}) collective-permute-start(f32[]{:T(128)} %max.7), channel_id=1, source_target_pairs={{0,4},{4,8},{8,12},{1,5},{5,9},{9,13},{2,6},{6,10},{10,14},{3,7},{... | collective-permute-start | bytes 20 | tf_op jit(solution)/shard_map/while/body/eval_jaxpr/ppermute | solution.py:16
  118.1 14.6 %collective-permute-start.1 = (f32[8,128,128]{2,1,0:T(8,128)S(1)}, f32[8,128,128]{2,1,0:T(8,128)}, u32[]{:S(2)}, u32[]{:S(2)}) collective-permute-start(f32[8,128,128]{2,1,0:T(8,128)S(1)} %fusion.172), channel_id=1, source_target_pairs={{0,4},{4,8},{8,12},{1,5},{5,9},{9,13},{2,6},{6,10},{10,14},{3,7},{... | collective-permute-start | bytes 1572872 | tf_op jit(solution)/shard_map/while/body/eval_jaxpr/ppermute | solution.py:16
  124.0 8.7 %collective-permute-start.2 = (f32[8,128]{1,0:T(8,128)S(1)}, f32[8,128]{1,0:T(8,128)S(1)}, u32[]{:S(2)}, u32[]{:S(2)}) collective-permute-start(f32[8,128]{1,0:T(8,128)S(1)} %fusion.173), channel_id=1, source_target_pairs={{0,4},{4,8},{8,12},{1,5},{5,9},{9,13},{2,6},{6,10},{10,14},{3,7},{... | collective-permute-start | bytes 12296 | tf_op jit(solution)/shard_map/while/body/eval_jaxpr/ppermute | solution.py:16
  126.3 5.6 %collective-permute-start = (f32[]{:T(128)}, f32[]{:T(128)}, u32[]{:S(2)}, u32[]{:S(2)}) collective-permute-start(f32[]{:T(128)} %max.7), channel_id=1, source_target_pairs={{0,4},{4,8},{8,12},{1,5},{5,9},{9,13},{2,6},{6,10},{10,14},{3,7},{... | collective-permute-start | bytes 20 | tf_op jit(solution)/shard_map/while/body/eval_jaxpr/ppermute | solution.py:16
  163.9 18.4 %collective-permute-start.4 = (f32[8,128,128]{2,1,0:T(8,128)S(1)}, f32[8,128,128]{2,1,0:T(8,128)S(1)}, u32[]{:S(2)}, u32[]{:S(2)}) collective-permute-start(f32[8,128,128]{2,1,0:T(8,128)S(1)} %fusion.174), channel_id=1, source_target_pairs={{4,0},{8,4},{12,8},{5,1},{9,5},{13,9},{6,2},{10,6},{14,10},{7,3},{... | collective-permute-start | bytes 1572872 | tf_op jit(solution)/shard_map/while/body/eval_jaxpr/ppermute | solution.py:16
  165.3 17.1 %collective-permute-start.5 = (f32[8,128]{1,0:T(8,128)S(1)}, f32[8,128]{1,0:T(8,128)S(1)}, u32[]{:S(2)}, u32[]{:S(2)}) collective-permute-start(f32[8,128]{1,0:T(8,128)S(1)} %fusion.175), channel_id=1, source_target_pairs={{4,0},{8,4},{12,8},{5,1},{9,5},{13,9},{6,2},{10,6},{14,10},{7,3},{... | collective-permute-start | bytes 12296 | tf_op jit(solution)/shard_map/while/body/eval_jaxpr/ppermute | solution.py:16
  166.6 15.1 %collective-permute-start.3 = (f32[]{:T(128)}, f32[]{:T(128)}, u32[]{:S(2)}, u32[]{:S(2)}) collective-permute-start(f32[]{:T(128)} %min.7), channel_id=1, source_target_pairs={{4,0},{8,4},{12,8},{5,1},{9,5},{13,9},{6,2},{10,6},{14,10},{7,3},{... | collective-permute-start | bytes 20 | tf_op jit(solution)/shard_map/while/body/eval_jaxpr/ppermute | solution.py:16
  182.5 17.1 %collective-permute-start.4 = (f32[8,128,128]{2,1,0:T(8,128)S(1)}, f32[8,128,128]{2,1,0:T(8,128)S(1)}, u32[]{:S(2)}, u32[]{:S(2)}) collective-permute-start(f32[8,128,128]{2,1,0:T(8,128)S(1)} %fusion.174), channel_id=1, source_target_pairs={{4,0},{8,4},{12,8},{5,1},{9,5},{13,9},{6,2},{10,6},{14,10},{7,3},{... | collective-permute-start | bytes 1572872 | tf_op jit(solution)/shard_map/while/body/eval_jaxpr/ppermute | solution.py:16
  183.8 15.8 %collective-permute-start.5 = (f32[8,128]{1,0:T(8,128)S(1)}, f32[8,128]{1,0:T(8,128)S(1)}, u32[]{:S(2)}, u32[]{:S(2)}) collective-permute-start(f32[8,128]{1,0:T(8,128)S(1)} %fusion.175), channel_id=1, source_target_pairs={{4,0},{8,4},{12,8},{5,1},{9,5},{13,9},{6,2},{10,6},{14,10},{7,3},{... | collective-permute-start | bytes 12296 | tf_op jit(solution)/shard_map/while/body/eval_jaxpr/ppermute | solution.py:16
  185.1 13.8 %collective-permute-start.3 = (f32[]{:T(128)}, f32[]{:T(128)}, u32[]{:S(2)}, u32[]{:S(2)}) collective-permute-start(f32[]{:T(128)} %min.7), channel_id=1, source_target_pairs={{4,0},{8,4},{12,8},{5,1},{9,5},{13,9},{6,2},{10,6},{14,10},{7,3},{... | collective-permute-start | bytes 20 | tf_op jit(solution)/shard_map/while/body/eval_jaxpr/ppermute | solution.py:16
  199.8 11.8 %collective-permute-start.4 = (f32[8,128,128]{2,1,0:T(8,128)S(1)}, f32[8,128,128]{2,1,0:T(8,128)S(1)}, u32[]{:S(2)}, u32[]{:S(2)}) collective-permute-start(f32[8,128,128]{2,1,0:T(8,128)S(1)} %fusion.174), channel_id=1, source_target_pairs={{4,0},{8,4},{12,8},{5,1},{9,5},{13,9},{6,2},{10,6},{14,10},{7,3},{... | collective-permute-start | bytes 1572872 | tf_op jit(solution)/shard_map/while/body/eval_jaxpr/ppermute | solution.py:16
  201.1 10.5 %collective-permute-start.5 = (f32[8,128]{1,0:T(8,128)S(1)}, f32[8,128]{1,0:T(8,128)S(1)}, u32[]{:S(2)}, u32[]{:S(2)}) collective-permute-start(f32[8,128]{1,0:T(8,128)S(1)} %fusion.175), channel_id=1, source_target_pairs={{4,0},{8,4},{12,8},{5,1},{9,5},{13,9},{6,2},{10,6},{14,10},{7,3},{... | collective-permute-start | bytes 12296 | tf_op jit(solution)/shard_map/while/body/eval_jaxpr/ppermute | solution.py:16
  202.4 8.5 %collective-permute-start.3 = (f32[]{:T(128)}, f32[]{:T(128)}, u32[]{:S(2)}, u32[]{:S(2)}) collective-permute-start(f32[]{:T(128)} %min.7), channel_id=1, source_target_pairs={{4,0},{8,4},{12,8},{5,1},{9,5},{13,9},{6,2},{10,6},{14,10},{7,3},{... | collective-permute-start | bytes 20 | tf_op jit(solution)/shard_map/while/body/eval_jaxpr/ppermute | solution.py:16
  220.7 43.1 %copy-start.26 = (bf16[192,8,128]{2,0,1:T(8,128)(2,1)S(1)}, bf16[192,8,128]{2,0,1:T(8,128)(2,1)}, u32[]{:S(2)}) copy-start(bf16[192,8,128]{2,0,1:T(8,128)(2,1)} %get-tuple-element.348) | copy-start | bytes 1179652
  (55 other events, 145.1 us)
Sparse Core Ops, SparseCore 0:
  10.2 41.6 all-gather.2
  54.0 51.4 all-gather.4
  221.7 38.3 all-reduce.5
where the time goes:
time: 275 us; the launch traced here: 273 us
  starting transfers between devices  89.1 us (32%)
  blocking collectives  49.3 us (18%)
  matrix products  35 us (13%)
  waiting for transfers between devices  33.6 us (12%)
  other arithmetic  22.5 us (8%)
  local copies, waits for them, and re-layouts  18.5 us (7%)
  between operations  17.1 us (6%)
  loops' own time  8.25 us (3%)
    ppermute x21, starting transfers between devices, passed_along(): return lax.ppermute(block, axis, route)  89 us
    psum x1, blocking collectives, body(): loss_total = lax.psum(local_part, ('grp', 'seq', 'head'))  40.6 us
    ppermute x21, waiting for transfers between devices, passed_along(): return lax.ppermute(block, axis, route)  33.5 us
    unnamed x134, local copies, waits for them, and re-layouts  12.5 us
    unnamed x1, blocking collectives  8.74 us
    dot_general x3, matrix products, local_loss(): jnp.einsum('ihf,jhf->hij', query_feat, key_feat, precision=exact_mode)  8.36 us
    dot_general x3, matrix products, local_loss(): jnp.einsum('ihf,hfd->ihd', query_feat, state, precision=exact_mode)  6.7 us
    another operation x1, loops' own time, body(): lax.fori_loop(0, seq_count - 1, relay_step, forward_blank)  5.64 us
  transfers between devices with their start and end apart: 24, of which 3 were waited for; matrix products, arithmetic and copies ran while one was open for 15% of the time, Pallas kernels for 0%

commit v1 on v0

--- a/solution.py
+++ b/solution.py
@@ -1,9 +1,19 @@
+import functools
+import math
+
 import jax
 import jax.numpy as jnp
 from jax import lax
+from jax.experimental import pallas as pl
+from jax.experimental.pallas import tpu as pltpu
 from jax.sharding import PartitionSpec as P
 
 WINDOW = 64
+DOC_VALUES = 4
+LANES = 128
+META_ROWS = 16
+BLOCK = 256
+LOG2E = math.log2(math.e)
 
 
 exact_mode = lax.Precision.HIGHEST
@@ -45,7 +55,7 @@
     )
 
 
-def body(queries, keys, values, documents, feature_map):
+def relay_body(queries, keys, values, documents, feature_map):
     tok_rows, head_count, head_width = queries.shape
     half_feat = feature_map.shape[2] // 2
     score_scale = head_width ** (-0.5)
@@ -195,6 +205,315 @@
     return (teacher_out, output.astype(jnp.bfloat16), loss_total, feature_grad)
 
 
+def turned(block, axis, distance):
+    count = lax.axis_size(axis)
+    return lax.ppermute(block, axis, [(i, (i + distance) % count) for i in range(count)])
+
+
+def crossed(block, axis, mask):
+    count = lax.axis_size(axis)
+    return lax.ppermute(block, axis, [(i, i ^ mask) for i in range(count)])
+
+
+def summed_over(block, axis):
+    count = lax.axis_size(axis)
+    if count == 1:
+        return block
+    if count == 2:
+        return block + crossed(block, axis, 1)
+    if count == 4:
+        return (block + crossed(block, axis, 2)) + (
+            crossed(block, axis, 1) + crossed(block, axis, 3)
+        )
+    return lax.psum(block, axis)
+
+
+def fits_split(tok_rows, head_count, head_width, feat, seq_count):
+    return (
+        head_count % seq_count == 0
+        and head_count % 8 == 0
+        and tok_rows % 16 == 0
+        and tok_rows <= 256
+        and tok_rows * seq_count <= 1536
+        and (tok_rows * seq_count) % BLOCK == 0
+        and head_width == LANES
+        and feat == LANES
+    )
+
+
+def dot_nn(a, b):
+    return jnp.dot(a, b, preferred_element_type=jnp.float32)
+
+
+def dot_nt(a, b):
+    return lax.dot_general(a, b, (((1,), (1,)), ((), ())), preferred_element_type=jnp.float32)
+
+
+def dot_tn(a, b):
+    return lax.dot_general(a, b, (((0,), (0,)), ((), ())), preferred_element_type=jnp.float32)
+
+
+def place_of(shift, seq_count):
+    return lax.rem(lax.axis_index("seq") + (seq_count - shift), seq_count)
+
+
+def pack_kernel(seq_count, per_place, chunk, q_ref, k_ref, v_ref, doc_ref, *rest):
+    outs, wide = rest[:seq_count], rest[seq_count]
+    rows = doc_ref.shape[1]
+    heads = seq_count * per_place
+    docs = doc_ref[...]
+    meta_row = lax.broadcasted_iota(jnp.int32, (META_ROWS, LANES), 0)
+    meta = jnp.zeros((META_ROWS, LANES), jnp.float32)
+    for value in range(DOC_VALUES - 1):
+        amount = jnp.sum((docs <= value).astype(jnp.float32), axis=1, keepdims=True)
+        meta = jnp.where(meta_row == value, amount, meta)
+    for n, ref in enumerate((q_ref, k_ref, v_ref)):
+        wide[n] = ref[...].astype(jnp.float32)
+    for shift, out in enumerate(outs):
+        head = lax.rem(lax.axis_index("seq") + shift, seq_count) * per_place + chunk
+        for n in range(3):
+            out[n * rows : (n + 1) * rows, :] = wide[
+                n, pl.ds(head, rows, stride=heads), :
+            ].astype(jnp.bfloat16)
+        out[3 * rows :, :] = meta.astype(jnp.bfloat16)
+
+
+def half_sums(array, ones_block):
+    high = array.astype(jnp.bfloat16)
+    low = (array - high.astype(jnp.float32)).astype(jnp.bfloat16)
+    return dot_nn(high, ones_block) + dot_nn(low, ones_block)
+
+
+def signed_features(inputs, weights, ones_block, left):
+    first = weights.astype(jnp.bfloat16)
+    left_over = weights - first.astype(jnp.float32)
+    second = left_over.astype(jnp.bfloat16)
+    third = (left_over - second.astype(jnp.float32)).astype(jnp.bfloat16)
+    logits = dot_nn(inputs, first) + dot_nn(inputs, second) + dot_nn(inputs, third)
+    left_most = jnp.max(jnp.where(left, logits, -jnp.inf), axis=1, keepdims=True)
+    right_most = jnp.max(jnp.where(left, -jnp.inf, logits), axis=1, keepdims=True)
+    raised = jnp.exp2((logits - jnp.where(left, left_most, right_most)) * LOG2E)
+    return raised / half_sums(raised, ones_block)
+
+
+def head_kernel(seq_count, per_place, chunk, score_scale, normaliser, *refs):
+    pieces, map_ref = refs[:seq_count], refs[seq_count]
+    outs = refs[seq_count + 1 : 2 * seq_count + 1]
+    loss_ref = refs[2 * seq_count + 1]
+    q_s, k_s, v_s, t_s, s_s, qf_s, kf_s, qb_s, kb_s, dq_s, dk_s = refs[2 * seq_count + 2 :]
+    total = q_s.shape[0]
+    rows = total // seq_count
+    exponent = score_scale * LOG2E
+
+    counts = jnp.zeros((META_ROWS, LANES), jnp.float32)
+    for shift, piece in enumerate(pieces):
+        first = pl.multiple_of(place_of(shift, seq_count) * rows, 16)
+        q_s[pl.ds(first, rows), :] = piece[:rows, :]
+        k_s[pl.ds(first, rows), :] = piece[rows : 2 * rows, :]
+        v_s[pl.ds(first, rows), :LANES] = piece[2 * rows : 3 * rows, :]
+        counts = counts + piece[3 * rows :, :].astype(jnp.float32)
+    v_s[:, LANES:] = jnp.ones((total, LANES), jnp.bfloat16)
+    bounds = counts.astype(jnp.int32)
+
+    lane = lax.broadcasted_iota(jnp.int32, (1, LANES), 1)
+    left = lane < LANES // 2
+    block_row = lax.broadcasted_iota(jnp.int32, (LANES, LANES), 0)
+    block_col = lax.broadcasted_iota(jnp.int32, (LANES, LANES), 1)
+    ones_block = ((block_row < LANES // 2) == (block_col < LANES // 2)).astype(jnp.bfloat16)
+
+    weights = map_ref[lax.axis_index("seq") * per_place + chunk]
+    rolled = pltpu.roll(weights, LANES // 2, 1)
+    q_feat = signed_features(q_s[...], jnp.where(left, weights, -rolled), ones_block, left)
+    k_feat = signed_features(k_s[...], jnp.where(left, rolled, -weights), ones_block, left)
+    qf_s[...] = q_feat
+    kf_s[...] = k_feat
+    qb_s[...] = q_feat.astype(jnp.bfloat16)
+    kb_s[...] = k_feat.astype(jnp.bfloat16)
+    dk_s[...] = jnp.zeros_like(dk_s)
+    loss = jnp.zeros((8, LANES), jnp.float32)
+
+    for first in range(0, total, BLOCK):
+        last = first + BLOCK
+        near = max(0, first - LANES)
+        place = lax.broadcasted_iota(jnp.int32, (BLOCK, LANES), 0) + first
+        start = jnp.zeros((BLOCK, LANES), jnp.int32)
+        for value in range(DOC_VALUES - 1):
+            bound = bounds[value : value + 1, :]
+            start = jnp.maximum(start, jnp.where(bound <= place, bound, 0))
+        row = place[:, :1]
+        col = lax.broadcasted_iota(jnp.int32, (BLOCK, last), 1)
+        visible = (col <= row) & (col >= start[:, :1])
+        far = (col <= row - WINDOW) & (col >= start[:, :1])
+        window = visible[:, near:] & (col[:, near:] > row - WINDOW)
+        scores = dot_nt(q_s[first:last, :], k_s[:last, :])
+        shown = jnp.where(visible, scores, masked_value)
+        raised = jnp.exp2((shown - jnp.max(shown, axis=1, keepdims=True)) * exponent)
+        numer = dot_nn(raised.astype(jnp.bfloat16), v_s[:last, :LANES])
+        teacher = (numer / jnp.sum(raised, axis=1, keepdims=True)).astype(jnp.bfloat16)
+        t_s[first:last, :] = teacher
+
+        shown = jnp.where(window, scores[:, near:], masked_value)
+        raised = jnp.exp2((shown - jnp.max(shown, axis=1, keepdims=True)) * exponent)
+        linear = dot_nt(qb_s[first:last, :], kb_s[:last, :])
+        weight = jnp.where(far[:, near:], linear[:, near:], raised)
+        if near:
+            weight = jnp.concatenate(
+                [jnp.where(far[:, :near], linear[:, :near], 0.0), weight], axis=1
+            )
+        sums = dot_nn(weight.astype(jnp.bfloat16), v_s[:last, :])
+        inverse = 1.0 / sums[:, LANES:]
+        output = sums[:, :LANES] * inverse
+        s_s[first:last, :] = output.astype(jnp.bfloat16)
+        error = output - teacher.astype(jnp.float32)
+        loss = loss + jnp.sum((error * error).reshape(BLOCK // 8, 8, LANES), axis=0)
+
+        slope = error * (2.0 * normaliser)
+        slope_numer = slope * inverse
+        slope_denom = -jnp.sum(slope * output, axis=1, keepdims=True) * inverse
+        high = slope_denom.astype(jnp.bfloat16).astype(jnp.float32)
+        extra = jnp.where(lane == 0, high, jnp.where(lane == 1, slope_denom - high, 0.0))
+        slopes = jnp.concatenate(
+            [slope_numer.astype(jnp.bfloat16), extra.astype(jnp.bfloat16)], axis=1
+        )
+        slope_weight = jnp.where(far, dot_nt(slopes, v_s[:last, :]), 0.0).astype(jnp.bfloat16)
+        dq_s[first:last, :] = dot_nn(slope_weight, kb_s[:last, :])
+        dk_s[:last, :] += dot_tn(slope_weight, qb_s[first:last, :])
+
+    def logits_slope(feat, slope):
+        product = feat * slope
+        return (product - feat * half_sums(product, ones_block)).astype(jnp.bfloat16)
+
+    from_q = dot_tn(q_s[...], logits_slope(qf_s[...], dq_s[...]))
+    from_k = dot_tn(k_s[...], logits_slope(kf_s[...], dk_s[...]))
+    grad = jnp.where(
+        left,
+        from_q - pltpu.roll(from_q, LANES // 2, 1),
+        pltpu.roll(from_k, LANES // 2, 1) - from_k,
+    ).astype(jnp.bfloat16)
+    for shift, out in enumerate(outs):
+        first = lax.rem(lax.axis_index("seq") + shift, seq_count) * rows
+        first = pl.multiple_of(first, 16)
+        out[:rows, :] = t_s[pl.ds(first, rows), :]
+        out[rows : 2 * rows, :] = s_s[pl.ds(first, rows), :]
+        out[2 * rows :, :] = grad
+    loss_ref[...] = loss * normaliser
+
+
+def unpack_kernel(seq_count, per_place, *refs):
+    pieces = refs[: seq_count * per_place]
+    t_ref, s_ref, grad_ref, t_wide, s_wide = refs[seq_count * per_place :]
+    heads = seq_count * per_place
+    rows = t_ref.shape[0] // heads
+    for chunk in range(per_place):
+        for shift in range(seq_count):
+            piece = pieces[chunk * seq_count + shift]
+            head = place_of(shift, seq_count) * per_place + chunk
+            t_wide[pl.ds(head, rows, stride=heads), :] = piece[:rows, :].astype(jnp.float32)
+            s_wide[pl.ds(head, rows, stride=heads), :] = piece[rows : 2 * rows, :].astype(
+                jnp.float32
+            )
+            grad_ref[head] = piece[2 * rows :, :].astype(jnp.float32)
+    t_ref[...] = t_wide[...].astype(jnp.bfloat16)
+    s_ref[...] = s_wide[...].astype(jnp.bfloat16)
+
+
+def kernel_call(kernel, out_shape, scratch_shapes, flops, moved, name):
+    return pl.pallas_call(
+        kernel,
+        out_shape=out_shape,
+        scratch_shapes=scratch_shapes,
+        compiler_params=pltpu.CompilerParams(vmem_limit_bytes=48 * 1024 * 1024),
+        cost_estimate=pl.CostEstimate(flops=flops, bytes_accessed=moved, transcendentals=0),
+        name=name,
+    )
+
+
+def split_body(queries, keys, values, documents, feature_map):
+    tok_rows, head_count, head_width = queries.shape
+    seq_count = lax.axis_size("seq")
+    per_place = head_count // seq_count
+    total = tok_rows * seq_count
+    score_scale = head_width ** (-0.5)
+    normaliser = 1.0 / (total * head_count * lax.axis_size(("grp", "head")))
+    flat = [a.reshape(tok_rows * head_count, head_width) for a in (queries, keys, values)]
+    docs = documents.reshape(1, tok_rows)
+    sent_rows = 3 * tok_rows + META_ROWS
+    back_rows = 2 * tok_rows + head_width
+    bf16, f32 = jnp.bfloat16, jnp.float32
+
+    held = []
+    for chunk in range(per_place):
+        packed = kernel_call(
+            functools.partial(pack_kernel, seq_count, per_place, chunk),
+            [jax.ShapeDtypeStruct((sent_rows, LANES), bf16)] * seq_count,
+            [pltpu.VMEM((3, tok_rows * head_count, LANES), f32)],
+            0,
+            12 * tok_rows * head_count * LANES,
+            "pack",
+        )(*flat, docs)
+        held.append(
+            [packed[0]] + [turned(packed[d], "seq", d) for d in range(1, seq_count)]
+        )
+
+    returned = []
+    loss = jnp.zeros((8, LANES), f32)
+    for chunk in range(per_place):
+        *packed, part = kernel_call(
+            functools.partial(
+                head_kernel, seq_count, per_place, chunk, score_scale, normaliser
+            ),
+            [jax.ShapeDtypeStruct((back_rows, LANES), bf16)] * seq_count
+            + [jax.ShapeDtypeStruct((8, LANES), f32)],
+            [
+                pltpu.VMEM((total, LANES), bf16),
+                pltpu.VMEM((total, LANES), bf16),
+                pltpu.VMEM((total, 2 * LANES), bf16),
+                pltpu.VMEM((total, LANES), bf16),
+                pltpu.VMEM((total, LANES), bf16),
+                pltpu.VMEM((total, LANES), f32),
+                pltpu.VMEM((total, LANES), f32),
+                pltpu.VMEM((total, LANES), bf16),
+                pltpu.VMEM((total, LANES), bf16),
+                pltpu.VMEM((total, LANES), f32),
+                pltpu.VMEM((total, LANES), f32),
+            ],
+            14 * total * total * LANES,
+            16 * total * LANES,
+            "one_head",
+        )(*held[chunk], feature_map)
+        returned += [packed[0]] + [turned(packed[d], "seq", d) for d in range(1, seq_count)]
+        loss = loss + part
+
+    loss = jnp.full((8, LANES), jnp.sum(loss), f32)
+    for axis in ("grp", "head", "seq"):
+        loss = summed_over(loss, axis)
+    teacher_out, student_out, feature_grad = kernel_call(
+        functools.partial(unpack_kernel, seq_count, per_place),
+        [
+            jax.ShapeDtypeStruct((tok_rows * head_count, LANES), bf16),
+            jax.ShapeDtypeStruct((tok_rows * head_count, LANES), bf16),
+            jax.ShapeDtypeStruct(feature_map.shape, f32),
+        ],
+        [pltpu.VMEM((tok_rows * head_count, LANES), f32)] * 2,
+        0,
+        12 * tok_rows * head_count * LANES,
+        "unpack",
+    )(*returned)
+    return (
+        teacher_out.reshape(queries.shape),
+        student_out.reshape(queries.shape),
+        loss[0, 0],
+        feature_grad,
+    )
+
+
+def body(queries, keys, values, documents, feature_map):
+    tok_rows, head_count, head_width = queries.shape
+    if fits_split(tok_rows, head_count, head_width, feature_map.shape[2], lax.axis_size("seq")):
+        return split_body(queries, keys, values, documents, feature_map)
+    return relay_body(queries, keys, values, documents, feature_map)
+
+
 def solution(mesh):
     in_specs = (
         P("seq", ("grp", "head"), None),

time: 275 us -> 77.2 us (0.28)
  starting transfers between devices: 89.1 us -> 32.1 us
  blocking collectives: 49.3 us -> 0 us
  matrix products: 35 us -> 0 us
  other arithmetic: 22.5 us -> 1.91 us
  between operations: 17.1 us -> 0.73 us
  Pallas kernels: 0 us -> 13.9 us
  local copies, waits for them, and re-layouts: 18.5 us -> 4.82 us
  waiting for transfers between devices: 33.6 us -> 23.5 us
  loops' own time: 8.25 us -> 0 us
    ppermute x21 -> x19, starting transfers between devices: 89 us -> 32.1 us  [the longest x12 23 us: turned(): lax.ppermute(block, axis, [(i, (i + distance) % count) for i in range(cou...]
    psum x1 -> x0, blocking collectives: 40.6 us -> none  [body(): loss_total = lax.psum(local_part, ('grp', 'seq', 'head'))]
    dot_general x21 -> x0, matrix products: 35 us -> none  [the longest x3 8.36 us: local_loss(): jnp.einsum('ihf,jhf->hij', query_feat, key_feat, precision=exact_mode)]
    pallas_call x0 -> x5, Pallas kernels: none -> 13.9 us  [the longest x2 11.6 us: split_body(): kernel_call(functools.partial(head_kernel, seq_count, per_place, chunk, s...]
    ppermute x21 -> x19, waiting for transfers between devices: 33.5 us -> 23.5 us  [the longest x12 22.3 us: turned(): lax.ppermute(block, axis, [(i, (i + distance) % count) for i in range(cou...]
    unnamed x134 -> x10, local copies, waits for them, and re-layouts: 12.5 us -> 3.66 us
    unnamed x1 -> x0, blocking collectives: 8.74 us -> none
    another operation x3 -> x0, loops' own time: 8.25 us -> none  [the longest x1 5.64 us: body(): lax.fori_loop(0, seq_count - 1, relay_step, forward_blank)]
  transfers between devices with their start and end apart: 24 -> 19, of which waited for: 3 -> 8; matrix products, arithmetic and copies ran while one was open for 15% -> 2% of each run, Pallas kernels for 0% -> 8%
where the time goes in v1:
time: 77.2 us; the launch traced here: 76.9 us
  starting transfers between devices  32.1 us (42%)
  waiting for transfers between devices  23.5 us (30%)
  Pallas kernels  13.9 us (18%)
  local copies, waits for them, and re-layouts  4.82 us (6%)
  other arithmetic  1.91 us (2%)
    ppermute x12, starting transfers between devices, turned(): lax.ppermute(block, axis, [(i, (i + distance) % count) for i in range(cou...  23 us
    ppermute x12, waiting for transfers between devices, turned(): lax.ppermute(block, axis, [(i, (i + distance) % count) for i in range(cou...  22.3 us
    pallas_call x2, Pallas kernels, split_body(): kernel_call(functools.partial(head_kernel, seq_count, per_place, chunk, s...  11.6 us
    ppermute x7, starting transfers between devices, crossed(): return lax.ppermute(block, axis, [(i, i ^ mask) for i in range(count)])  9.04 us
    unnamed x10, local copies, waits for them, and re-layouts  3.66 us
  transfers between devices with their start and end apart: 19, of which 8 were waited for; matrix products, arithmetic and copies ran while one was open for 2% of the time, Pallas kernels for 8%

profile of v1, /device:TPU:0, one launch (start us, length us, event | category | flops | bytes accessed | tf_op | source)
XLA Modules:
  0.0 76.9 jit_solution(7046825895903174573)
XLA Ops:
  0.6 0.7 copy-done.3
  1.3 1.0 %copy-done = bf16[192,8,128]{2,1,0:T(8,128)(2,1)S(1)} copy-done((bf16[192,8,128]{2,1,0:T(8,128)(2,1)S(1)}, bf16[192,8,128]{2,1,0:T(8,128)(2,1)}, u32[]{:S(2)}) %copy-start) | copy-done | bytes 393240
  2.3 1.0 %copy-done.1 = bf16[192,8,128]{2,1,0:T(8,128)(2,1)S(1)} copy-done((bf16[192,8,128]{2,1,0:T(8,128)(2,1)S(1)}, bf16[192,8,128]{2,1,0:T(8,128)(2,1)}, u32[]{:S(2)}) %copy-start.1) | copy-done | bytes 393240
  3.3 1.0 %copy-done.2 = bf16[192,8,128]{2,1,0:T(8,128)(2,1)S(1)} copy-done((bf16[192,8,128]{2,1,0:T(8,128)(2,1)S(1)}, bf16[192,8,128]{2,1,0:T(8,128)(2,1)}, u32[]{:S(2)}) %copy-start.2) | copy-done | bytes 393240
  4.8 3.1 %collective-permute-start.6 = (bf16[592,128]{1,0:T(8,128)(2,1)S(1)}, bf16[592,128]{1,0:T(8,128)(2,1)S(1)}, u32[]{:S(2)}, u32[]{:S(2)}) collective-permute-start(bf16[592,128]{1,0:T(8,128)(2,1)S(1)} %get-tuple-element.34), channel_id=1, source_target_pairs={{0,4},{4,8},{8,12},{12,0},{1,5},{5,9},{9,13},{13,1},{2,6},{6,10},{... | collective-permute-start | bytes 454664 | tf_op jit(solution)/shard_map/ppermute | solution.py:210
  7.8 2.6 %collective-permute-start.7 = (bf16[592,128]{1,0:T(8,128)(2,1)S(1)}, bf16[592,128]{1,0:T(8,128)(2,1)S(1)}, u32[]{:S(2)}, u32[]{:S(2)}) collective-permute-start(bf16[592,128]{1,0:T(8,128)(2,1)S(1)} %get-tuple-element.35), channel_id=1, source_target_pairs={{0,8},{4,12},{8,0},{12,4},{1,9},{5,13},{9,1},{13,5},{2,10},{6,14},... | collective-permute-start | bytes 454664 | tf_op jit(solution)/shard_map/ppermute | solution.py:210
  10.4 1.3 %collective-permute-start.8 = (bf16[592,128]{1,0:T(8,128)(2,1)S(1)}, bf16[592,128]{1,0:T(8,128)(2,1)S(1)}, u32[]{:S(2)}, u32[]{:S(2)}) collective-permute-start(bf16[592,128]{1,0:T(8,128)(2,1)S(1)} %get-tuple-element.36), channel_id=1, source_target_pairs={{0,12},{4,0},{8,4},{12,8},{1,13},{5,1},{9,5},{13,9},{2,14},{6,2},{... | collective-permute-start | bytes 454664 | tf_op jit(solution)/shard_map/ppermute | solution.py:210
  12.3 0.7 collective-permute-start
  13.3 1.4 %collective-permute-done.6.refs_1_ = bf16[592,128]{1,0:T(8,128)(2,1)S(1)} collective-permute-done((bf16[592,128]{1,0:T(8,128)(2,1)S(1)}, bf16[592,128]{1,0:T(8,128)(2,1)S(1)}, u32[]{:S(2)}, u32[]{:S(2)}) %collective-permute-start.6) | collective-permute-done | bytes 151584 | tf_op jit(solution)/shard_map/ppermute | solution.py:210
  14.7 2.5 %collective-permute-start.2 = (bf16[592,128]{1,0:T(8,128)(2,1)S(1)}, bf16[592,128]{1,0:T(8,128)(2,1)S(1)}, u32[]{:S(2)}, u32[]{:S(2)}) collective-permute-start(bf16[592,128]{1,0:T(8,128)(2,1)S(1)} %get-tuple-element.28), channel_id=1, source_target_pairs={{0,12},{4,0},{8,4},{12,8},{1,13},{5,1},{9,5},{13,9},{2,14},{6,2},{... | collective-permute-start | bytes 454664 | tf_op jit(solution)/shard_map/ppermute | solution.py:210
  17.3 4.0 %collective-permute-done.7.refs_2_ = bf16[592,128]{1,0:T(8,128)(2,1)S(1)} collective-permute-done((bf16[592,128]{1,0:T(8,128)(2,1)S(1)}, bf16[592,128]{1,0:T(8,128)(2,1)S(1)}, u32[]{:S(2)}, u32[]{:S(2)}) %collective-permute-start.7) | collective-permute-done | bytes 151584 | tf_op jit(solution)/shard_map/ppermute | solution.py:210
  21.3 2.3 %collective-permute-done.8.refs_3_ = bf16[592,128]{1,0:T(8,128)(2,1)S(1)} collective-permute-done((bf16[592,128]{1,0:T(8,128)(2,1)S(1)}, bf16[592,128]{1,0:T(8,128)(2,1)S(1)}, u32[]{:S(2)}, u32[]{:S(2)}) %collective-permute-start.8) | collective-permute-done | bytes 151584 | tf_op jit(solution)/shard_map/ppermute | solution.py:210
  23.6 5.8 %one_head.3 = (bf16[512,128]{1,0:T(8,128)(2,1)S(1)}, bf16[512,128]{1,0:T(8,128)(2,1)S(1)}, bf16[512,128]{1,0:T(8,128)(2,1)S(1)}, bf16[512,128]{1,0:T(8,128)(2,1)S(1)}, f32[8,128]{1,0:T(8,128)S(1)}) custom-call(bf16[592,128]{1,0:T(8,128)(2,1)S(1)} %get-tuple-element.33.refs_0_, bf16[592,128]{1,0:T(8,128)(2,1)S(1)} %collective-permute-done.6.refs_1_, ...), custom_call_target="tpu_custom_call" | custom-call | flops 1056964608 | bytes 1572864 | tf_op jit(solution)/shard_map/one_head/pallas_call | solution.py:461
  29.5 4.0 %collective-permute-done.1.refs_2_ = bf16[592,128]{1,0:T(8,128)(2,1)S(1)} collective-permute-done((bf16[592,128]{1,0:T(8,128)(2,1)S(1)}, bf16[592,128]{1,0:T(8,128)(2,1)S(1)}, u32[]{:S(2)}, u32[]{:S(2)}) %collective-permute-start.1) | collective-permute-done | bytes 151584 | tf_op jit(solution)/shard_map/ppermute | solution.py:210
  33.4 5.8 %one_head.2 = (bf16[512,128]{1,0:T(8,128)(2,1)S(1)}, bf16[512,128]{1,0:T(8,128)(2,1)S(1)}, bf16[512,128]{1,0:T(8,128)(2,1)S(1)}, bf16[512,128]{1,0:T(8,128)(2,1)S(1)}, f32[8,128]{1,0:T(8,128)S(1)}) custom-call(bf16[592,128]{1,0:T(8,128)(2,1)S(1)} %get-tuple-element.25.refs_0_, bf16[592,128]{1,0:T(8,128)(2,1)S(1)} %collective-permute-done.refs_1_, ...), custom_call_target="tpu_custom_call" | custom-call | flops 1056964608 | bytes 1572864 | tf_op jit(solution)/shard_map/one_head/pallas_call | solution.py:461
  39.3 0.6 add_reduce_fusion
  39.9 0.6 broadcast_in_dim.3
  40.6 1.2 %collective-permute-done.12 = f32[8,128]{1,0:T(8,128)S(1)} collective-permute-done((f32[8,128]{1,0:T(8,128)S(1)}, f32[8,128]{1,0:T(8,128)S(1)}, u32[]{:S(2)}, u32[]{:S(2)}) %collective-permute-start.12) | collective-permute-done | bytes 4128 | tf_op jit(solution)/shard_map/ppermute | solution.py:215
  41.7 0.6 broadcast_add_fusion
  42.4 1.6 %collective-permute-start.14 = (f32[8,128]{1,0:T(8,128)S(1)}, f32[8,128]{1,0:T(8,128)S(1)}, u32[]{:S(2)}, u32[]{:S(2)}) collective-permute-start(f32[8,128]{1,0:T(8,128)S(1)} %broadcast_add_fusion), channel_id=1, source_target_pairs={{0,1},{1,0},{2,3},{3,2},{4,5},{5,4},{6,7},{7,6},{8,9},{9,8},{10,11... | collective-permute-start | bytes 12296 | tf_op jit(solution)/shard_map/ppermute | solution.py:215
  44.0 1.5 %collective-permute-start.15 = (f32[8,128]{1,0:T(8,128)S(1)}, f32[8,128]{1,0:T(8,128)S(1)}, u32[]{:S(2)}, u32[]{:S(2)}) collective-permute-start(f32[8,128]{1,0:T(8,128)S(1)} %broadcast_add_fusion), channel_id=1, source_target_pairs={{0,3},{1,2},{2,1},{3,0},{4,7},{5,6},{6,5},{7,4},{8,11},{9,10},{10,... | collective-permute-start | bytes 12296 | tf_op jit(solution)/shard_map/ppermute | solution.py:215
  46.0 3.7 %collective-permute-start.9 = (bf16[512,128]{1,0:T(8,128)(2,1)S(1)}, bf16[512,128]{1,0:T(8,128)(2,1)S(1)}, u32[]{:S(2)}, u32[]{:S(2)}) collective-permute-start(bf16[512,128]{1,0:T(8,128)(2,1)S(1)} %get-tuple-element.38), channel_id=1, source_target_pairs={{0,4},{4,8},{8,12},{12,0},{1,5},{5,9},{9,13},{13,1},{2,6},{6,10},{... | collective-permute-start | bytes 393224 | tf_op jit(solution)/shard_map/ppermute | solution.py:210
  49.7 0.7 add_add_fusion.1
  50.4 4.8 %collective-permute-start.18 = (f32[8,128]{1,0:T(8,128)S(1)}, f32[8,128]{1,0:T(8,128)S(1)}, u32[]{:S(2)}, u32[]{:S(2)}) collective-permute-start(f32[8,128]{1,0:T(8,128)S(1)} %add_add_fusion.1), channel_id=1, source_target_pairs={{0,12},{4,8},{8,4},{12,0},{1,13},{5,9},{9,5},{13,1},{2,14},{6,10},... | collective-permute-start | bytes 12296 | tf_op jit(solution)/shard_map/ppermute | solution.py:215
  55.1 0.6 collective-permute-start.16
  55.8 2.3 %collective-permute-start.10 = (bf16[512,128]{1,0:T(8,128)(2,1)S(1)}, bf16[512,128]{1,0:T(8,128)(2,1)S(1)}, u32[]{:S(2)}, u32[]{:S(2)}) collective-permute-start(bf16[512,128]{1,0:T(8,128)(2,1)S(1)} %get-tuple-element.39), channel_id=1, source_target_pairs={{0,8},{4,12},{8,0},{12,4},{1,9},{5,13},{9,1},{13,5},{2,10},{6,14},... | collective-permute-start | bytes 393224 | tf_op jit(solution)/shard_map/ppermute | solution.py:210
  58.1 2.5 %collective-permute-start.11 = (bf16[512,128]{1,0:T(8,128)(2,1)S(1)}, bf16[512,128]{1,0:T(8,128)(2,1)S(1)}, u32[]{:S(2)}, u32[]{:S(2)}) collective-permute-start(bf16[512,128]{1,0:T(8,128)(2,1)S(1)} %get-tuple-element.40), channel_id=1, source_target_pairs={{0,12},{4,0},{8,4},{12,8},{1,13},{5,1},{9,5},{13,9},{2,14},{6,2},{... | collective-permute-start | bytes 393224 | tf_op jit(solution)/shard_map/ppermute | solution.py:210
  60.6 1.0 %collective-permute-start.4 = (bf16[512,128]{1,0:T(8,128)(2,1)S(1)}, bf16[512,128]{1,0:T(8,128)(2,1)S(1)}, u32[]{:S(2)}, u32[]{:S(2)}) collective-permute-start(bf16[512,128]{1,0:T(8,128)(2,1)S(1)} %get-tuple-element.31), channel_id=1, source_target_pairs={{0,8},{4,12},{8,0},{12,4},{1,9},{5,13},{9,1},{13,5},{2,10},{6,14},... | collective-permute-start | bytes 393224 | tf_op jit(solution)/shard_map/ppermute | solution.py:210
  61.6 2.9 %collective-permute-start.5 = (bf16[512,128]{1,0:T(8,128)(2,1)S(1)}, bf16[512,128]{1,0:T(8,128)(2,1)S(1)}, u32[]{:S(2)}, u32[]{:S(2)}) collective-permute-start(bf16[512,128]{1,0:T(8,128)(2,1)S(1)} %get-tuple-element.32), channel_id=1, source_target_pairs={{0,12},{4,0},{8,4},{12,8},{1,13},{5,1},{9,5},{13,9},{2,14},{6,2},{... | collective-permute-start | bytes 393224 | tf_op jit(solution)/shard_map/ppermute | solution.py:210
  65.0 3.8 %collective-permute-done.10.refs_6_ = bf16[512,128]{1,0:T(8,128)(2,1)S(1)} collective-permute-done((bf16[512,128]{1,0:T(8,128)(2,1)S(1)}, bf16[512,128]{1,0:T(8,128)(2,1)S(1)}, u32[]{:S(2)}, u32[]{:S(2)}) %collective-permute-start.10) | collective-permute-done | bytes 131104 | tf_op jit(solution)/shard_map/ppermute | solution.py:210
  68.9 6.7 %collective-permute-done.4.refs_2_ = bf16[512,128]{1,0:T(8,128)(2,1)S(1)} collective-permute-done((bf16[512,128]{1,0:T(8,128)(2,1)S(1)}, bf16[512,128]{1,0:T(8,128)(2,1)S(1)}, u32[]{:S(2)}, u32[]{:S(2)}) %collective-permute-start.4) | collective-permute-done | bytes 131104 | tf_op jit(solution)/shard_map/ppermute | solution.py:210
  75.6 1.4 %unpack.1 = (bf16[1536,128]{1,0:T(8,128)(2,1)}, bf16[1536,128]{1,0:T(8,128)(2,1)}, f32[8,128,128]{2,1,0:T(8,128)}) custom-call(bf16[512,128]{1,0:T(8,128)(2,1)S(1)} %get-tuple-element.29.refs_0_, bf16[512,128]{1,0:T(8,128)(2,1)S(1)} %collective-permute-done.3.refs_1_, bf16[512,128]{1,0:T(8,128)(2,1)S(1)} %collective-permute-done.4.refs_2_, ...), custom_call_target="tpu_custom_call" | custom-call | bytes 2359296 | tf_op jit(solution)/shard_map/unpack/pallas_call | solution.py:490
  (27 shorter events, 2.5 us)
Async XLA Ops:
  0.6 0.7 copy-start.3
  1.3 1.0 %copy-start = (bf16[192,8,128]{2,1,0:T(8,128)(2,1)S(1)}, bf16[192,8,128]{2,1,0:T(8,128)(2,1)}, u32[]{:S(2)}) copy-start(bf16[192,8,128]{2,1,0:T(8,128)(2,1)} %param.5) | copy-start | bytes 1179652
  2.3 1.0 %copy-start.1 = (bf16[192,8,128]{2,1,0:T(8,128)(2,1)S(1)}, bf16[192,8,128]{2,1,0:T(8,128)(2,1)}, u32[]{:S(2)}) copy-start(bf16[192,8,128]{2,1,0:T(8,128)(2,1)} %param.6) | copy-start | bytes 1179652
  3.3 1.0 %copy-start.2 = (bf16[192,8,128]{2,1,0:T(8,128)(2,1)S(1)}, bf16[192,8,128]{2,1,0:T(8,128)(2,1)}, u32[]{:S(2)}) copy-start(bf16[192,8,128]{2,1,0:T(8,128)(2,1)} %param.7) | copy-start | bytes 1179652
  4.8 10.0 %collective-permute-start.6 = (bf16[592,128]{1,0:T(8,128)(2,1)S(1)}, bf16[592,128]{1,0:T(8,128)(2,1)S(1)}, u32[]{:S(2)}, u32[]{:S(2)}) collective-permute-start(bf16[592,128]{1,0:T(8,128)(2,1)S(1)} %get-tuple-element.34), channel_id=1, source_target_pairs={{0,4},{4,8},{8,12},{12,0},{1,5},{5,9},{9,13},{13,1},{2,6},{6,10},{... | collective-permute-start | bytes 454664 | tf_op jit(solution)/shard_map/ppermute | solution.py:210
  7.8 13.4 %collective-permute-start.7 = (bf16[592,128]{1,0:T(8,128)(2,1)S(1)}, bf16[592,128]{1,0:T(8,128)(2,1)S(1)}, u32[]{:S(2)}, u32[]{:S(2)}) collective-permute-start(bf16[592,128]{1,0:T(8,128)(2,1)S(1)} %get-tuple-element.35), channel_id=1, source_target_pairs={{0,8},{4,12},{8,0},{12,4},{1,9},{5,13},{9,1},{13,5},{2,10},{6,14},... | collective-permute-start | bytes 454664 | tf_op jit(solution)/shard_map/ppermute | solution.py:210
  10.4 13.2 %copy-start.4 = (f32[8,128,128]{2,1,0:T(8,128)S(1)}, f32[8,128,128]{2,1,0:T(8,128)}, u32[]{:S(2)}) copy-start(f32[8,128,128]{2,1,0:T(8,128)} %refs_4_.3) | copy-start | bytes 1572868
  10.4 13.2 %collective-permute-start.8 = (bf16[592,128]{1,0:T(8,128)(2,1)S(1)}, bf16[592,128]{1,0:T(8,128)(2,1)S(1)}, u32[]{:S(2)}, u32[]{:S(2)}) collective-permute-start(bf16[592,128]{1,0:T(8,128)(2,1)S(1)} %get-tuple-element.36), channel_id=1, source_target_pairs={{0,12},{4,0},{8,4},{12,8},{1,13},{5,1},{9,5},{13,9},{2,14},{6,2},{... | collective-permute-start | bytes 454664 | tf_op jit(solution)/shard_map/ppermute | solution.py:210
  12.3 17.2 %collective-permute-start = (bf16[592,128]{1,0:T(8,128)(2,1)S(1)}, bf16[592,128]{1,0:T(8,128)(2,1)S(1)}, u32[]{:S(2)}, u32[]{:S(2)}) collective-permute-start(bf16[592,128]{1,0:T(8,128)(2,1)S(1)} %get-tuple-element.26), channel_id=1, source_target_pairs={{0,4},{4,8},{8,12},{12,0},{1,5},{5,9},{9,13},{13,1},{2,6},{6,10},{... | collective-permute-start | bytes 454664 | tf_op jit(solution)/shard_map/ppermute | solution.py:210
  13.0 20.4 %collective-permute-start.1 = (bf16[592,128]{1,0:T(8,128)(2,1)S(1)}, bf16[592,128]{1,0:T(8,128)(2,1)S(1)}, u32[]{:S(2)}, u32[]{:S(2)}) collective-permute-start(bf16[592,128]{1,0:T(8,128)(2,1)S(1)} %get-tuple-element.27), channel_id=1, source_target_pairs={{0,8},{4,12},{8,0},{12,4},{1,9},{5,13},{9,1},{13,5},{2,10},{6,14},... | collective-permute-start | bytes 454664 | tf_op jit(solution)/shard_map/ppermute | solution.py:210
  14.7 18.7 %collective-permute-start.2 = (bf16[592,128]{1,0:T(8,128)(2,1)S(1)}, bf16[592,128]{1,0:T(8,128)(2,1)S(1)}, u32[]{:S(2)}, u32[]{:S(2)}) collective-permute-start(bf16[592,128]{1,0:T(8,128)(2,1)S(1)} %get-tuple-element.28), channel_id=1, source_target_pairs={{0,12},{4,0},{8,4},{12,8},{1,13},{5,1},{9,5},{13,9},{2,14},{6,2},{... | collective-permute-start | bytes 454664 | tf_op jit(solution)/shard_map/ppermute | solution.py:210
  40.5 1.2 %collective-permute-start.12 = (f32[8,128]{1,0:T(8,128)S(1)}, f32[8,128]{1,0:T(8,128)S(1)}, u32[]{:S(2)}, u32[]{:S(2)}) collective-permute-start(f32[8,128]{1,0:T(8,128)S(1)} %broadcast_in_dim.3), channel_id=1, source_target_pairs={{0,16},{16,0},{1,17},{17,1},{2,18},{18,2},{3,19},{19,3},{4,20},{20... | collective-permute-start | bytes 12296 | tf_op jit(solution)/shard_map/ppermute | solution.py:215
  42.4 7.3 %collective-permute-start.14 = (f32[8,128]{1,0:T(8,128)S(1)}, f32[8,128]{1,0:T(8,128)S(1)}, u32[]{:S(2)}, u32[]{:S(2)}) collective-permute-start(f32[8,128]{1,0:T(8,128)S(1)} %broadcast_add_fusion), channel_id=1, source_target_pairs={{0,1},{1,0},{2,3},{3,2},{4,5},{5,4},{6,7},{7,6},{8,9},{9,8},{10,11... | collective-permute-start | bytes 12296 | tf_op jit(solution)/shard_map/ppermute | solution.py:215
  44.0 5.7 %collective-permute-start.15 = (f32[8,128]{1,0:T(8,128)S(1)}, f32[8,128]{1,0:T(8,128)S(1)}, u32[]{:S(2)}, u32[]{:S(2)}) collective-permute-start(f32[8,128]{1,0:T(8,128)S(1)} %broadcast_add_fusion), channel_id=1, source_target_pairs={{0,3},{1,2},{2,1},{3,0},{4,7},{5,6},{6,5},{7,4},{8,11},{9,10},{10,... | collective-permute-start | bytes 12296 | tf_op jit(solution)/shard_map/ppermute | solution.py:215
  45.4 4.2 %collective-permute-start.13 = (f32[8,128]{1,0:T(8,128)S(1)}, f32[8,128]{1,0:T(8,128)S(1)}, u32[]{:S(2)}, u32[]{:S(2)}) collective-permute-start(f32[8,128]{1,0:T(8,128)S(1)} %broadcast_add_fusion), channel_id=1, source_target_pairs={{0,2},{1,3},{2,0},{3,1},{4,6},{5,7},{6,4},{7,5},{8,10},{9,11},{10,... | collective-permute-start | bytes 12296 | tf_op jit(solution)/shard_map/ppermute | solution.py:215
  46.0 15.7 %collective-permute-start.9 = (bf16[512,128]{1,0:T(8,128)(2,1)S(1)}, bf16[512,128]{1,0:T(8,128)(2,1)S(1)}, u32[]{:S(2)}, u32[]{:S(2)}) collective-permute-start(bf16[512,128]{1,0:T(8,128)(2,1)S(1)} %get-tuple-element.38), channel_id=1, source_target_pairs={{0,4},{4,8},{8,12},{12,0},{1,5},{5,9},{9,13},{13,1},{2,6},{6,10},{... | collective-permute-start | bytes 393224 | tf_op jit(solution)/shard_map/ppermute | solution.py:210
  50.4 7.7 %collective-permute-start.18 = (f32[8,128]{1,0:T(8,128)S(1)}, f32[8,128]{1,0:T(8,128)S(1)}, u32[]{:S(2)}, u32[]{:S(2)}) collective-permute-start(f32[8,128]{1,0:T(8,128)S(1)} %add_add_fusion.1), channel_id=1, source_target_pairs={{0,12},{4,8},{8,4},{12,0},{1,13},{5,9},{9,5},{13,1},{2,14},{6,10},... | collective-permute-start | bytes 12296 | tf_op jit(solution)/shard_map/ppermute | solution.py:215
  55.1 5.5 %collective-permute-start.17 = (f32[8,128]{1,0:T(8,128)S(1)}, f32[8,128]{1,0:T(8,128)S(1)}, u32[]{:S(2)}, u32[]{:S(2)}) collective-permute-start(f32[8,128]{1,0:T(8,128)S(1)} %add_add_fusion.1), channel_id=1, source_target_pairs={{0,4},{4,0},{8,12},{12,8},{1,5},{5,1},{9,13},{13,9},{2,6},{6,2},{1... | collective-permute-start | bytes 12296 | tf_op jit(solution)/shard_map/ppermute | solution.py:215
  55.1 5.5 %collective-permute-start.16 = (f32[8,128]{1,0:T(8,128)S(1)}, f32[8,128]{1,0:T(8,128)S(1)}, u32[]{:S(2)}, u32[]{:S(2)}) collective-permute-start(f32[8,128]{1,0:T(8,128)S(1)} %add_add_fusion.1), channel_id=1, source_target_pairs={{0,8},{4,12},{8,0},{12,4},{1,9},{5,13},{9,1},{13,5},{2,10},{6,14},... | collective-permute-start | bytes 12296 | tf_op jit(solution)/shard_map/ppermute | solution.py:215
  55.8 13.0 %collective-permute-start.10 = (bf16[512,128]{1,0:T(8,128)(2,1)S(1)}, bf16[512,128]{1,0:T(8,128)(2,1)S(1)}, u32[]{:S(2)}, u32[]{:S(2)}) collective-permute-start(bf16[512,128]{1,0:T(8,128)(2,1)S(1)} %get-tuple-element.39), channel_id=1, source_target_pairs={{0,8},{4,12},{8,0},{12,4},{1,9},{5,13},{9,1},{13,5},{2,10},{6,14},... | collective-permute-start | bytes 393224 | tf_op jit(solution)/shard_map/ppermute | solution.py:210
  58.1 10.7 %collective-permute-start.11 = (bf16[512,128]{1,0:T(8,128)(2,1)S(1)}, bf16[512,128]{1,0:T(8,128)(2,1)S(1)}, u32[]{:S(2)}, u32[]{:S(2)}) collective-permute-start(bf16[512,128]{1,0:T(8,128)(2,1)S(1)} %get-tuple-element.40), channel_id=1, source_target_pairs={{0,12},{4,0},{8,4},{12,8},{1,13},{5,1},{9,5},{13,9},{2,14},{6,2},{... | collective-permute-start | bytes 393224 | tf_op jit(solution)/shard_map/ppermute | solution.py:210
  60.6 8.3 %collective-permute-start.3 = (bf16[512,128]{1,0:T(8,128)(2,1)S(1)}, bf16[512,128]{1,0:T(8,128)(2,1)S(1)}, u32[]{:S(2)}, u32[]{:S(2)}) collective-permute-start(bf16[512,128]{1,0:T(8,128)(2,1)S(1)} %get-tuple-element.30), channel_id=1, source_target_pairs={{0,4},{4,8},{8,12},{12,0},{1,5},{5,9},{9,13},{13,1},{2,6},{6,10},{... | collective-permute-start | bytes 393224 | tf_op jit(solution)/shard_map/ppermute | solution.py:210
  60.6 15.0 %collective-permute-start.4 = (bf16[512,128]{1,0:T(8,128)(2,1)S(1)}, bf16[512,128]{1,0:T(8,128)(2,1)S(1)}, u32[]{:S(2)}, u32[]{:S(2)}) collective-permute-start(bf16[512,128]{1,0:T(8,128)(2,1)S(1)} %get-tuple-element.31), channel_id=1, source_target_pairs={{0,8},{4,12},{8,0},{12,4},{1,9},{5,13},{9,1},{13,5},{2,10},{6,14},... | collective-permute-start | bytes 393224 | tf_op jit(solution)/shard_map/ppermute | solution.py:210
  61.6 13.9 %collective-permute-start.5 = (bf16[512,128]{1,0:T(8,128)(2,1)S(1)}, bf16[512,128]{1,0:T(8,128)(2,1)S(1)}, u32[]{:S(2)}, u32[]{:S(2)}) collective-permute-start(bf16[512,128]{1,0:T(8,128)(2,1)S(1)} %get-tuple-element.32), channel_id=1, source_target_pairs={{0,12},{4,0},{8,4},{12,8},{1,13},{5,1},{9,5},{13,9},{2,14},{6,2},{... | collective-permute-start | bytes 393224 | tf_op jit(solution)/shard_map/ppermute | solution.py:210

commit v2 on v1

--- a/solution.py
+++ b/solution.py
@@ -14,6 +14,10 @@
 META_ROWS = 16
 BLOCK = 256
 LOG2E = math.log2(math.e)
+COPIES = 4
+
+PACK_VMEM = 62
+HEAD_COST = 6_000_000_000
 
 
 exact_mode = lax.Precision.HIGHEST
@@ -257,25 +261,46 @@
     return lax.rem(lax.axis_index("seq") + (seq_count - shift), seq_count)
 
 
-def pack_kernel(seq_count, per_place, chunk, q_ref, k_ref, v_ref, doc_ref, *rest):
-    outs, wide = rest[:seq_count], rest[seq_count]
+def pack_kernel(seq_count, per_place, q_ref, k_ref, v_ref, map_ref, doc_ref, *rest):
+    outs = rest[: seq_count * per_place]
+    own_map, narrow, wide, sems = rest[seq_count * per_place :]
     rows = doc_ref.shape[1]
     heads = seq_count * per_place
+    part = rows * heads // COPIES
+    copies = []
+    for n, ref in enumerate((q_ref, k_ref, v_ref)):
+        for piece in range(COPIES):
+            span = pl.ds(piece * part, part)
+            copies.append(
+                pltpu.make_async_copy(
+                    ref.at[span, :], narrow.at[n, span, :], sems.at[n * COPIES + piece]
+                )
+            )
+    own = pl.ds(lax.axis_index("seq") * per_place, per_place)
+    copies.append(pltpu.make_async_copy(map_ref.at[own], own_map, sems.at[3 * COPIES]))
+    for copy in copies:
+        copy.start()
     docs = doc_ref[...]
     meta_row = lax.broadcasted_iota(jnp.int32, (META_ROWS, LANES), 0)
     meta = jnp.zeros((META_ROWS, LANES), jnp.float32)
     for value in range(DOC_VALUES - 1):
         amount = jnp.sum((docs <= value).astype(jnp.float32), axis=1, keepdims=True)
         meta = jnp.where(meta_row == value, amount, meta)
-    for n, ref in enumerate((q_ref, k_ref, v_ref)):
-        wide[n] = ref[...].astype(jnp.float32)
-    for shift, out in enumerate(outs):
-        head = lax.rem(lax.axis_index("seq") + shift, seq_count) * per_place + chunk
-        for n in range(3):
-            out[n * rows : (n + 1) * rows, :] = wide[
-                n, pl.ds(head, rows, stride=heads), :
-            ].astype(jnp.bfloat16)
-        out[3 * rows :, :] = meta.astype(jnp.bfloat16)
+    for n in range(3):
+        for piece in range(COPIES):
+            copies[n * COPIES + piece].wait()
+            span = pl.ds(piece * part, part)
+            wide[n, span, :] = narrow[n, span, :].astype(jnp.float32)
+    for chunk in range(per_place):
+        for shift in range(seq_count):
+            out = outs[chunk * seq_count + shift]
+            head = lax.rem(lax.axis_index("seq") + shift, seq_count) * per_place + chunk
+            for n in range(3):
+                out[n * rows : (n + 1) * rows, :] = wide[
+                    n, pl.ds(head, rows, stride=heads), :
+                ].astype(jnp.bfloat16)
+            out[3 * rows :, :] = meta.astype(jnp.bfloat16)
+    copies[-1].wait()
 
 
 def half_sums(array, ones_block):
@@ -296,54 +321,64 @@
     return raised / half_sums(raised, ones_block)
 
 
-def head_kernel(seq_count, per_place, chunk, score_scale, normaliser, *refs):
-    pieces, map_ref = refs[:seq_count], refs[seq_count]
-    outs = refs[seq_count + 1 : 2 * seq_count + 1]
-    loss_ref = refs[2 * seq_count + 1]
-    q_s, k_s, v_s, t_s, s_s, qf_s, kf_s, qb_s, kb_s, dq_s, dk_s = refs[2 * seq_count + 2 :]
-    total = q_s.shape[0]
+def ones_halves():
+    row = lax.broadcasted_iota(jnp.int32, (LANES, LANES), 0) < LANES // 2
+    col = lax.broadcasted_iota(jnp.int32, (LANES, LANES), 1) < LANES // 2
+    return (row == col).astype(jnp.bfloat16)
+
+
+def block_places(first, bounds):
+    place = lax.broadcasted_iota(jnp.int32, (BLOCK, LANES), 0) + first
+    start = jnp.zeros((BLOCK, LANES), jnp.int32)
+    for value in range(DOC_VALUES - 1):
+        bound = bounds[value : value + 1, :]
+        start = jnp.maximum(start, jnp.where(bound <= place, bound, 0))
+    return place[:, :1], start[:, :1]
+
+
+def forward_kernel(seq_count, chunk, score_scale, normaliser, *refs):
+    pieces, map_ref, earlier_ref = refs[:seq_count], refs[seq_count], refs[seq_count + 1]
+    outs = refs[seq_count + 2 : 2 * seq_count + 2]
+    loss_ref, qkv_ref, feat_ref, slope_ref, bound_ref = refs[
+        2 * seq_count + 2 : 2 * seq_count + 7
+    ]
+    v_s, t_s, s_s, qb_s, kb_s = refs[2 * seq_count + 7 :]
+    q_s, k_s = qkv_ref.at[0], qkv_ref.at[1]
+    total = v_s.shape[0]
     rows = total // seq_count
     exponent = score_scale * LOG2E
 
     counts = jnp.zeros((META_ROWS, LANES), jnp.float32)
     for shift, piece in enumerate(pieces):
-        first = pl.multiple_of(place_of(shift, seq_count) * rows, 16)
-        q_s[pl.ds(first, rows), :] = piece[:rows, :]
-        k_s[pl.ds(first, rows), :] = piece[rows : 2 * rows, :]
-        v_s[pl.ds(first, rows), :LANES] = piece[2 * rows : 3 * rows, :]
+        span = pl.ds(pl.multiple_of(place_of(shift, seq_count) * rows, 16), rows)
+        for n in range(3):
+            qkv_ref[n, span, :] = piece[n * rows : (n + 1) * rows, :]
+        v_s[span, :LANES] = piece[2 * rows : 3 * rows, :]
         counts = counts + piece[3 * rows :, :].astype(jnp.float32)
     v_s[:, LANES:] = jnp.ones((total, LANES), jnp.bfloat16)
     bounds = counts.astype(jnp.int32)
+    bound_ref[...] = bounds
 
     lane = lax.broadcasted_iota(jnp.int32, (1, LANES), 1)
     left = lane < LANES // 2
-    block_row = lax.broadcasted_iota(jnp.int32, (LANES, LANES), 0)
-    block_col = lax.broadcasted_iota(jnp.int32, (LANES, LANES), 1)
-    ones_block = ((block_row < LANES // 2) == (block_col < LANES // 2)).astype(jnp.bfloat16)
-
-    weights = map_ref[lax.axis_index("seq") * per_place + chunk]
+    ones_block = ones_halves()
+    weights = map_ref[chunk]
     rolled = pltpu.roll(weights, LANES // 2, 1)
     q_feat = signed_features(q_s[...], jnp.where(left, weights, -rolled), ones_block, left)
     k_feat = signed_features(k_s[...], jnp.where(left, rolled, -weights), ones_block, left)
-    qf_s[...] = q_feat
-    kf_s[...] = k_feat
+    feat_ref[0] = q_feat
+    feat_ref[1] = k_feat
     qb_s[...] = q_feat.astype(jnp.bfloat16)
     kb_s[...] = k_feat.astype(jnp.bfloat16)
-    dk_s[...] = jnp.zeros_like(dk_s)
     loss = jnp.zeros((8, LANES), jnp.float32)
 
     for first in range(0, total, BLOCK):
         last = first + BLOCK
         near = max(0, first - LANES)
-        place = lax.broadcasted_iota(jnp.int32, (BLOCK, LANES), 0) + first
-        start = jnp.zeros((BLOCK, LANES), jnp.int32)
-        for value in range(DOC_VALUES - 1):
-            bound = bounds[value : value + 1, :]
-            start = jnp.maximum(start, jnp.where(bound <= place, bound, 0))
-        row = place[:, :1]
+        row, start = block_places(first, bounds)
         col = lax.broadcasted_iota(jnp.int32, (BLOCK, last), 1)
-        visible = (col <= row) & (col >= start[:, :1])
-        far = (col <= row - WINDOW) & (col >= start[:, :1])
+        visible = (col <= row) & (col >= start)
+        far = (col <= row - WINDOW) & (col >= start)
         window = visible[:, near:] & (col[:, near:] > row - WINDOW)
         scores = dot_nt(q_s[first:last, :], k_s[:last, :])
         shown = jnp.where(visible, scores, masked_value)
@@ -368,40 +403,61 @@
         loss = loss + jnp.sum((error * error).reshape(BLOCK // 8, 8, LANES), axis=0)
 
         slope = error * (2.0 * normaliser)
-        slope_numer = slope * inverse
         slope_denom = -jnp.sum(slope * output, axis=1, keepdims=True) * inverse
         high = slope_denom.astype(jnp.bfloat16).astype(jnp.float32)
         extra = jnp.where(lane == 0, high, jnp.where(lane == 1, slope_denom - high, 0.0))
-        slopes = jnp.concatenate(
-            [slope_numer.astype(jnp.bfloat16), extra.astype(jnp.bfloat16)], axis=1
-        )
-        slope_weight = jnp.where(far, dot_nt(slopes, v_s[:last, :]), 0.0).astype(jnp.bfloat16)
-        dq_s[first:last, :] = dot_nn(slope_weight, kb_s[:last, :])
-        dk_s[:last, :] += dot_tn(slope_weight, qb_s[first:last, :])
+        slope_ref[first:last, :LANES] = (slope * inverse).astype(jnp.bfloat16)
+        slope_ref[first:last, LANES:] = extra.astype(jnp.bfloat16)
+
+    for shift, out in enumerate(outs):
+        first = lax.rem(lax.axis_index("seq") + shift, seq_count) * rows
+        span = pl.ds(pl.multiple_of(first, 16), rows)
+        out[:rows, :] = t_s[span, :]
+        out[rows:, :] = s_s[span, :]
+    loss_ref[...] = earlier_ref[...] + jnp.sum(loss) * normaliser
+
+
+def backward_kernel(per_place, *refs):
+    saved, grad_ref = refs[: 4 * per_place], refs[4 * per_place]
+    v_s, qb_s, kb_s, dq_s, dk_s = refs[4 * per_place + 1 :]
+    total = v_s.shape[0]
+    left = lax.broadcasted_iota(jnp.int32, (1, LANES), 1) < LANES // 2
+    ones_block = ones_halves()
 
     def logits_slope(feat, slope):
         product = feat * slope
         return (product - feat * half_sums(product, ones_block)).astype(jnp.bfloat16)
 
-    from_q = dot_tn(q_s[...], logits_slope(qf_s[...], dq_s[...]))
-    from_k = dot_tn(k_s[...], logits_slope(kf_s[...], dk_s[...]))
-    grad = jnp.where(
-        left,
-        from_q - pltpu.roll(from_q, LANES // 2, 1),
-        pltpu.roll(from_k, LANES // 2, 1) - from_k,
-    ).astype(jnp.bfloat16)
-    for shift, out in enumerate(outs):
-        first = lax.rem(lax.axis_index("seq") + shift, seq_count) * rows
-        first = pl.multiple_of(first, 16)
-        out[:rows, :] = t_s[pl.ds(first, rows), :]
-        out[rows : 2 * rows, :] = s_s[pl.ds(first, rows), :]
-        out[2 * rows :, :] = grad
-    loss_ref[...] = loss * normaliser
+    for chunk in range(per_place):
+        qkv_ref, feat_ref, slope_ref, bound_ref = saved[4 * chunk : 4 * chunk + 4]
+        bounds = bound_ref[...]
+        v_s[:, :LANES] = qkv_ref[2]
+        v_s[:, LANES:] = jnp.ones((total, LANES), jnp.bfloat16)
+        qb_s[...] = feat_ref[0].astype(jnp.bfloat16)
+        kb_s[...] = feat_ref[1].astype(jnp.bfloat16)
+        dk_s[...] = jnp.zeros_like(dk_s)
+        for first in range(0, total, BLOCK):
+            last = first + BLOCK
+            row, start = block_places(first, bounds)
+            col = lax.broadcasted_iota(jnp.int32, (BLOCK, last), 1)
+            far = (col <= row - WINDOW) & (col >= start)
+            slope_weight = jnp.where(
+                far, dot_nt(slope_ref[first:last, :], v_s[:last, :]), 0.0
+            ).astype(jnp.bfloat16)
+            dq_s[first:last, :] = dot_nn(slope_weight, kb_s[:last, :])
+            dk_s[:last, :] += dot_tn(slope_weight, qb_s[first:last, :])
+        from_q = dot_tn(qkv_ref[0], logits_slope(feat_ref[0], dq_s[...]))
+        from_k = dot_tn(qkv_ref[1], logits_slope(feat_ref[1], dk_s[...]))
+        grad_ref[chunk * LANES : (chunk + 1) * LANES, :] = jnp.where(
+            left,
+            from_q - pltpu.roll(from_q, LANES // 2, 1),
+            pltpu.roll(from_k, LANES // 2, 1) - from_k,
+        ).astype(jnp.bfloat16)
 
 
 def unpack_kernel(seq_count, per_place, *refs):
     pieces = refs[: seq_count * per_place]
-    t_ref, s_ref, grad_ref, t_wide, s_wide = refs[seq_count * per_place :]
+    t_ref, s_ref, t_wide, s_wide = refs[seq_count * per_place :]
     heads = seq_count * per_place
     rows = t_ref.shape[0] // heads
     for chunk in range(per_place):
@@ -412,17 +468,51 @@
             s_wide[pl.ds(head, rows, stride=heads), :] = piece[rows : 2 * rows, :].astype(
                 jnp.float32
             )
-            grad_ref[head] = piece[2 * rows :, :].astype(jnp.float32)
     t_ref[...] = t_wide[...].astype(jnp.bfloat16)
     s_ref[...] = s_wide[...].astype(jnp.bfloat16)
 
 
-def kernel_call(kernel, out_shape, scratch_shapes, flops, moved, name):
+def join_kernel(grad_ref, *refs):
+    losses, out = refs[:-1], refs[-1]
+    size = grad_ref.shape[0]
+    loss = losses[0][...]
+    if len(losses) == 4:
+        loss = (loss + losses[2][...]) + (losses[1][...] + losses[3][...])
+    out[:size, :] = grad_ref[...]
+    row = lax.broadcasted_iota(jnp.int32, (8, LANES), 0)
+    high = loss.astype(jnp.bfloat16).astype(jnp.float32)
+    middle = (loss - high).astype(jnp.bfloat16).astype(jnp.float32)
+    low = (loss - high) - middle
+    parts = jnp.where(row == 0, high, jnp.where(row == 1, middle, jnp.where(row == 2, low, 0.0)))
+    out[size:, :] = jnp.concatenate([parts, parts], axis=0).astype(jnp.bfloat16)
+
+
+def final_kernel(seq_count, per_place, *refs):
+    pieces = refs[:seq_count]
+    grad_ref, loss_ref, parts_s = refs[seq_count:]
+    for shift, piece in enumerate(pieces):
+        source = place_of(shift, seq_count)
+        for chunk in range(per_place):
+            grad_ref[source * per_place + chunk] = piece[
+                chunk * LANES : (chunk + 1) * LANES, :
+            ].astype(jnp.float32)
+        tail = piece[per_place * LANES :, :].astype(jnp.float32)
+        parts_s[source] = tail[0:1, :] + tail[1:2, :] + tail[2:3, :]
+    loss = parts_s[0]
+    for source in range(1, seq_count):
+        loss = loss + parts_s[source]
+    loss_ref[...] = loss
+
+
+def kernel_call(
+    kernel, out_shape, scratch_shapes, flops, moved, name, vmem=48, **specs
+):
     return pl.pallas_call(
         kernel,
+        **specs,
         out_shape=out_shape,
         scratch_shapes=scratch_shapes,
-        compiler_params=pltpu.CompilerParams(vmem_limit_bytes=48 * 1024 * 1024),
+        compiler_params=pltpu.CompilerParams(vmem_limit_bytes=vmem * 1024 * 1024),
         cost_estimate=pl.CostEstimate(flops=flops, bytes_accessed=moved, transcendentals=0),
         name=name,
     )
@@ -438,67 +528,113 @@
     flat = [a.reshape(tok_rows * head_count, head_width) for a in (queries, keys, values)]
     docs = documents.reshape(1, tok_rows)
     sent_rows = 3 * tok_rows + META_ROWS
-    back_rows = 2 * tok_rows + head_width
     bf16, f32 = jnp.bfloat16, jnp.float32
 
-    held = []
-    for chunk in range(per_place):
-        packed = kernel_call(
-            functools.partial(pack_kernel, seq_count, per_place, chunk),
-            [jax.ShapeDtypeStruct((sent_rows, LANES), bf16)] * seq_count,
-            [pltpu.VMEM((3, tok_rows * head_count, LANES), f32)],
-            0,
-            12 * tok_rows * head_count * LANES,
-            "pack",
-        )(*flat, docs)
-        held.append(
-            [packed[0]] + [turned(packed[d], "seq", d) for d in range(1, seq_count)]
-        )
-
-    returned = []
+    def sizes(*rows, dtype=bf16):
+        return [jax.ShapeDtypeStruct((n, LANES), dtype) for n in rows]
+
+    def sent(blocks):
+        return [blocks[0]] + [turned(blocks[d], "seq", d) for d in range(1, seq_count)]
+
+    def after(blocks, arrived):
+        blocks, passed = lax.optimization_barrier((blocks, arrived[1:]))
+        return blocks, arrived[:1] + passed
+
+    *packed, own_map = kernel_call(
+        functools.partial(pack_kernel, seq_count, per_place),
+        sizes(*[sent_rows] * head_count)
+        + [jax.ShapeDtypeStruct((per_place,) + feature_map.shape[1:], f32)],
+        [
+            pltpu.VMEM((3, tok_rows * head_count, LANES), bf16),
+            pltpu.VMEM((3, tok_rows * head_count, LANES), f32),
+            pltpu.SemaphoreType.DMA((3 * COPIES + 1,)),
+        ],
+        0,
+        12 * tok_rows * head_count * LANES,
+        "pack",
+        vmem=PACK_VMEM,
+        in_specs=[pl.BlockSpec(memory_space=pltpu.HBM)] * 4
+        + [pl.BlockSpec(memory_space=pltpu.VMEM)],
+    )(*flat, feature_map, docs)
+    held = [
+        sent(packed[chunk * seq_count : (chunk + 1) * seq_count]) for chunk in range(per_place)
+    ]
+
+    returned, saved = [], []
     loss = jnp.zeros((8, LANES), f32)
     for chunk in range(per_place):
-        *packed, part = kernel_call(
-            functools.partial(
-                head_kernel, seq_count, per_place, chunk, score_scale, normaliser
-            ),
-            [jax.ShapeDtypeStruct((back_rows, LANES), bf16)] * seq_count
-            + [jax.ShapeDtypeStruct((8, LANES), f32)],
+        results = kernel_call(
+            functools.partial(forward_kernel, seq_count, chunk, score_scale, normaliser),
+            sizes(*[2 * tok_rows] * seq_count)
+            + sizes(8, dtype=f32)
+            + [
+                jax.ShapeDtypeStruct((3, total, LANES), bf16),
+                jax.ShapeDtypeStruct((2, total, LANES), f32),
+                jax.ShapeDtypeStruct((total, 2 * LANES), bf16),
+                jax.ShapeDtypeStruct((META_ROWS, LANES), jnp.int32),
+            ],
             [
-                pltpu.VMEM((total, LANES), bf16),
-                pltpu.VMEM((total, LANES), bf16),
                 pltpu.VMEM((total, 2 * LANES), bf16),
                 pltpu.VMEM((total, LANES), bf16),
                 pltpu.VMEM((total, LANES), bf16),
-                pltpu.VMEM((total, LANES), f32),
-                pltpu.VMEM((total, LANES), f32),
                 pltpu.VMEM((total, LANES), bf16),
                 pltpu.VMEM((total, LANES), bf16),
-                pltpu.VMEM((total, LANES), f32),
-                pltpu.VMEM((total, LANES), f32),
             ],
-            14 * total * total * LANES,
+            HEAD_COST,
             16 * total * LANES,
-            "one_head",
-        )(*held[chunk], feature_map)
-        returned += [packed[0]] + [turned(packed[d], "seq", d) for d in range(1, seq_count)]
-        loss = loss + part
-
-    loss = jnp.full((8, LANES), jnp.sum(loss), f32)
-    for axis in ("grp", "head", "seq"):
-        loss = summed_over(loss, axis)
-    teacher_out, student_out, feature_grad = kernel_call(
+            "forward",
+        )(*held[chunk], own_map, loss)
+        loss = results[seq_count]
+        saved.append(results[seq_count + 1 :])
+        returned.append(sent(results[:seq_count]))
+
+    saved, returned[0] = after(saved, returned[0])
+    grad = kernel_call(
+        functools.partial(backward_kernel, per_place),
+        sizes(per_place * LANES)[0],
+        [
+            pltpu.VMEM((total, 2 * LANES), bf16),
+            pltpu.VMEM((total, LANES), bf16),
+            pltpu.VMEM((total, LANES), bf16),
+            pltpu.VMEM((total, LANES), f32),
+            pltpu.VMEM((total, LANES), f32),
+        ],
+        HEAD_COST,
+        16 * total * LANES,
+        "backward",
+    )(*[part for parts in saved for part in parts])
+    loss = summed_over(loss, "grp")
+    if lax.axis_size("head") == 4:
+        losses = [loss] + [crossed(loss, "head", mask) for mask in range(1, 4)]
+    else:
+        losses = [summed_over(loss, "head")]
+    for n in range(1, per_place):
+        grad, returned[n] = after(grad, returned[n])
+    joined = kernel_call(
+        join_kernel,
+        sizes(per_place * LANES + META_ROWS)[0],
+        [],
+        0,
+        16 * LANES * LANES,
+        "join",
+    )(grad, *losses)
+    last = sent([joined] * seq_count)
+    teacher_out, student_out = kernel_call(
         functools.partial(unpack_kernel, seq_count, per_place),
-        [
-            jax.ShapeDtypeStruct((tok_rows * head_count, LANES), bf16),
-            jax.ShapeDtypeStruct((tok_rows * head_count, LANES), bf16),
-            jax.ShapeDtypeStruct(feature_map.shape, f32),
-        ],
+        sizes(*[tok_rows * head_count] * 2),
         [pltpu.VMEM((tok_rows * head_count, LANES), f32)] * 2,
         0,
         12 * tok_rows * head_count * LANES,
         "unpack",
-    )(*returned)
+    )(*[piece for pieces in returned for piece in pieces])
+    feature_grad, loss = kernel_call(
+        functools.partial(final_kernel, seq_count, per_place),
+        [jax.ShapeDtypeStruct(feature_map.shape, f32)] + sizes(1, dtype=f32),
+        [pltpu.VMEM((seq_count, 1, LANES), f32)],
+        0,
+        8 * head_count * LANES * LANES,
+        "final",
+    )(*last)
     return (
         teacher_out.reshape(queries.shape),
         student_out.reshape(queries.shape),

time: 77.2 us -> 65.5 us (0.85)
  waiting for transfers between devices: 23.5 us -> 14 us
  local copies, waits for them, and re-layouts: 4.82 us -> 1.82 us
  Pallas kernels: 13.9 us -> 16.8 us
  other arithmetic: 1.91 us -> 0.01 us
    ppermute x12 -> x15, waiting for transfers between devices: 22.3 us -> 12.8 us  [turned(): lax.ppermute(block, axis, [(i, (i + distance) % count) for i in range(cou...]
    ppermute x7 -> x4, starting transfers between devices: 9.04 us -> 3.49 us  [crossed(): return lax.ppermute(block, axis, [(i, i ^ mask) for i in range(count)])]
    ppermute x12 -> x15, starting transfers between devices: 23 us -> 28.4 us  [turned(): lax.ppermute(block, axis, [(i, (i + distance) % count) for i in range(cou...]
    pallas_call x5 -> x7, Pallas kernels: 13.9 us -> 16.8 us  [the longest x2 7.47 us: split_body(): kernel_call(functools.partial(forward_kernel, seq_count, chunk, score_sca...]
    unnamed x10 -> x6, local copies, waits for them, and re-layouts: 3.66 us -> 1.82 us
  transfers between devices with their start and end apart: 19 -> 19, of which waited for: 8 -> 5; matrix products, arithmetic and copies ran while one was open for 2% -> 0% of each run, Pallas kernels for 8% -> 19%
where the time goes in v2:
time: 65.5 us; the launch traced here: 65.3 us
  starting transfers between devices  31.9 us (49%)
  Pallas kernels  16.8 us (26%)
  waiting for transfers between devices  14 us (21%)
  local copies, waits for them, and re-layouts  1.82 us (3%)
  between operations  0.74 us (1%)
    ppermute x15, starting transfers between devices, turned(): lax.ppermute(block, axis, [(i, (i + distance) % count) for i in range(cou...  28.4 us
    ppermute x15, waiting for transfers between devices, turned(): lax.ppermute(block, axis, [(i, (i + distance) % count) for i in range(cou...  12.8 us
    pallas_call x2, Pallas kernels, split_body(): kernel_call(functools.partial(forward_kernel, seq_count, chunk, score_sca...  7.47 us
    pallas_call x1, Pallas kernels, split_body(): kernel_call(functools.partial(pack_kernel, seq_count, per_place), sizes(*...  3.79 us
    pallas_call x1, Pallas kernels, split_body(): kernel_call(functools.partial(backward_kernel, per_place), sizes(per_plac...  3.5 us
    ppermute x4, starting transfers between devices, crossed(): return lax.ppermute(block, axis, [(i, i ^ mask) for i in range(count)])  3.49 us
    unnamed x6, local copies, waits for them, and re-layouts  1.82 us
  transfers between devices with their start and end apart: 19, of which 5 were waited for; matrix products, arithmetic and copies ran while one was open for 0% of the time, Pallas kernels for 19%

profile of v2, /device:TPU:0, one launch (start us, length us, event | category | flops | bytes accessed | tf_op | source)
XLA Modules:
  0.0 65.3 jit_solution(17931137357984660986)
XLA Ops:
  0.6 3.8 %pack.1 = (bf16[592,128]{1,0:T(8,128)(2,1)}, bf16[592,128]{1,0:T(8,128)(2,1)}, bf16[592,128]{1,0:T(8,128)(2,1)}, bf16[592,128]{1,0:T(8,128)(2,1)}, bf16[592,128]...) custom-call(bf16[1536,128]{1,0:T(8,128)(2,1)} %bitcast.8, ...), custom_call_target="tpu_custom_call" | custom-call | bytes 2359296 | tf_op jit(solution)/shard_map/pack/pallas_call | solution.py:543
  4.4 3.1 %collective-permute-start = (bf16[592,128]{1,0:T(8,128)(2,1)}, bf16[592,128]{1,0:T(8,128)(2,1)S(1)}, u32[]{:S(2)}, u32[]{:S(2)}) collective-permute-start(bf16[592,128]{1,0:T(8,128)(2,1)} %get-tuple-element.51), channel_id=1, source_target_pairs={{0,4},{4,8},{8,12},{12,0},{1,5},{5,9},{9,13},{13,1},{2,6},{6,10},{... | collective-permute-start | bytes 454664 | tf_op jit(solution)/shard_map/ppermute | solution.py:214
  7.5 2.6 %collective-permute-start.1 = (bf16[592,128]{1,0:T(8,128)(2,1)}, bf16[592,128]{1,0:T(8,128)(2,1)S(1)}, u32[]{:S(2)}, u32[]{:S(2)}) collective-permute-start(bf16[592,128]{1,0:T(8,128)(2,1)} %get-tuple-element.52), channel_id=1, source_target_pairs={{0,8},{4,12},{8,0},{12,4},{1,9},{5,13},{9,1},{13,5},{2,10},{6,14},... | collective-permute-start | bytes 454664 | tf_op jit(solution)/shard_map/ppermute | solution.py:214
  10.1 1.3 %collective-permute-start.2 = (bf16[592,128]{1,0:T(8,128)(2,1)}, bf16[592,128]{1,0:T(8,128)(2,1)S(1)}, u32[]{:S(2)}, u32[]{:S(2)}) collective-permute-start(bf16[592,128]{1,0:T(8,128)(2,1)} %get-tuple-element.53), channel_id=1, source_target_pairs={{0,12},{4,0},{8,4},{12,8},{1,13},{5,1},{9,5},{13,9},{2,14},{6,2},{... | collective-permute-start | bytes 454664 | tf_op jit(solution)/shard_map/ppermute | solution.py:214
  11.4 0.7 %collective-permute-start.3 = (bf16[592,128]{1,0:T(8,128)(2,1)}, bf16[592,128]{1,0:T(8,128)(2,1)S(1)}, u32[]{:S(2)}, u32[]{:S(2)}) collective-permute-start(bf16[592,128]{1,0:T(8,128)(2,1)} %get-tuple-element.61), channel_id=1, source_target_pairs={{0,4},{4,8},{8,12},{12,0},{1,5},{5,9},{9,13},{13,1},{2,6},{6,10},{... | collective-permute-start | bytes 454664 | tf_op jit(solution)/shard_map/ppermute | solution.py:214
  12.1 0.3 collective-permute-start.4
  12.5 2.1 %collective-permute-done.refs_1_ = bf16[592,128]{1,0:T(8,128)(2,1)S(1)} collective-permute-done((bf16[592,128]{1,0:T(8,128)(2,1)}, bf16[592,128]{1,0:T(8,128)(2,1)S(1)}, u32[]{:S(2)}, u32[]{:S(2)}) %collective-permute-start) | collective-permute-done | bytes 151584 | tf_op jit(solution)/shard_map/ppermute | solution.py:214
  14.6 2.5 %collective-permute-start.5 = (bf16[592,128]{1,0:T(8,128)(2,1)}, bf16[592,128]{1,0:T(8,128)(2,1)S(1)}, u32[]{:S(2)}, u32[]{:S(2)}) collective-permute-start(bf16[592,128]{1,0:T(8,128)(2,1)} %get-tuple-element.63), channel_id=1, source_target_pairs={{0,12},{4,0},{8,4},{12,8},{1,13},{5,1},{9,5},{13,9},{2,14},{6,2},{... | collective-permute-start | bytes 454664 | tf_op jit(solution)/shard_map/ppermute | solution.py:214
  17.1 4.0 %collective-permute-done.1.refs_2_ = bf16[592,128]{1,0:T(8,128)(2,1)S(1)} collective-permute-done((bf16[592,128]{1,0:T(8,128)(2,1)}, bf16[592,128]{1,0:T(8,128)(2,1)S(1)}, u32[]{:S(2)}, u32[]{:S(2)}) %collective-permute-start.1) | collective-permute-done | bytes 151584 | tf_op jit(solution)/shard_map/ppermute | solution.py:214
  21.1 2.3 %collective-permute-done.2.refs_3_ = bf16[592,128]{1,0:T(8,128)(2,1)S(1)} collective-permute-done((bf16[592,128]{1,0:T(8,128)(2,1)}, bf16[592,128]{1,0:T(8,128)(2,1)S(1)}, u32[]{:S(2)}, u32[]{:S(2)}) %collective-permute-start.2) | collective-permute-done | bytes 151584 | tf_op jit(solution)/shard_map/ppermute | solution.py:214
  23.5 0.9 %copy-done.1 = bf16[592,128]{1,0:T(8,128)(2,1)S(1)} copy-done((bf16[592,128]{1,0:T(8,128)(2,1)S(1)}, bf16[592,128]{1,0:T(8,128)(2,1)}, u32[]{:S(2)}) %copy-start.1) | copy-done | bytes 151576
  24.4 0.9 %copy-done.2 = f32[2,128,128]{2,1,0:T(8,128)S(1)} copy-done((f32[2,128,128]{2,1,0:T(8,128)S(1)}, f32[2,128,128]{2,1,0:T(8,128)}, u32[]{:S(2)}) %copy-start.2) | copy-done | bytes 131096
  25.3 3.7 %forward.2 = (bf16[384,128]{1,0:T(8,128)(2,1)S(1)}, bf16[384,128]{1,0:T(8,128)(2,1)S(1)}, bf16[384,128]{1,0:T(8,128)(2,1)S(1)}, bf16[384,128]{1,0:T(8,128)(2,1)S...) custom-call(bf16[592,128]{1,0:T(8,128)(2,1)S(1)} %copy-done.1, ...), custom_call_target="tpu_custom_call" | custom-call | flops 6000000000 | bytes 1572864 | tf_op jit(solution)/shard_map/forward/pallas_call | solution.py:566
  29.1 7.2 %collective-permute-start.6 = (bf16[384,128]{1,0:T(8,128)(2,1)S(1)}, bf16[384,128]{1,0:T(8,128)(2,1)S(1)}, u32[]{:S(2)}, u32[]{:S(2)}) collective-permute-start(bf16[384,128]{1,0:T(8,128)(2,1)S(1)} %get-tuple-element.69), channel_id=1, source_target_pairs={{0,4},{4,8},{8,12},{12,0},{1,5},{5,9},{9,13},{13,1},{2,6},{6,10},{... | collective-permute-start | bytes 294920 | tf_op jit(solution)/shard_map/ppermute | solution.py:214
  36.2 2.7 %collective-permute-start.7 = (bf16[384,128]{1,0:T(8,128)(2,1)S(1)}, bf16[384,128]{1,0:T(8,128)(2,1)S(1)}, u32[]{:S(2)}, u32[]{:S(2)}) collective-permute-start(bf16[384,128]{1,0:T(8,128)(2,1)S(1)} %get-tuple-element.70), channel_id=1, source_target_pairs={{0,8},{4,12},{8,0},{12,4},{1,9},{5,13},{9,1},{13,5},{2,10},{6,14},... | collective-permute-start | bytes 294920 | tf_op jit(solution)/shard_map/ppermute | solution.py:214
  38.9 0.0 collective-permute-done.5.refs_3_
  39.0 3.7 %forward.3 = (bf16[384,128]{1,0:T(8,128)(2,1)S(1)}, bf16[384,128]{1,0:T(8,128)(2,1)S(1)}, bf16[384,128]{1,0:T(8,128)(2,1)S(1)}, bf16[384,128]{1,0:T(8,128)(2,1)S...) custom-call(bf16[592,128]{1,0:T(8,128)(2,1)S(1)} %copy-done, ...), custom_call_target="tpu_custom_call" | custom-call | flops 6000000000 | bytes 1572864 | tf_op jit(solution)/shard_map/forward/pallas_call | solution.py:566
  42.7 2.1 %collective-permute-start.9 = (bf16[384,128]{1,0:T(8,128)(2,1)S(1)}, bf16[384,128]{1,0:T(8,128)(2,1)S(1)}, u32[]{:S(2)}, u32[]{:S(2)}) collective-permute-start(bf16[384,128]{1,0:T(8,128)(2,1)S(1)} %get-tuple-element.84), channel_id=1, source_target_pairs={{0,4},{4,8},{8,12},{12,0},{1,5},{5,9},{9,13},{13,1},{2,6},{6,10},{... | collective-permute-start | bytes 294920 | tf_op jit(solution)/shard_map/ppermute | solution.py:214
  44.8 1.2 %collective-permute-done.12 = f32[8,128]{1,0:T(8,128)S(1)} collective-permute-done((f32[8,128]{1,0:T(8,128)S(1)}, f32[8,128]{1,0:T(8,128)S(1)}, u32[]{:S(2)}, u32[]{:S(2)}) %collective-permute-start.12) | collective-permute-done | bytes 4128 | tf_op jit(solution)/shard_map/ppermute | solution.py:219
  46.0 0.2 collective-permute-start.10
  46.2 0.0 collective-permute-done.6.refs_1_
  46.2 2.2 %collective-permute-start.11 = (bf16[384,128]{1,0:T(8,128)(2,1)S(1)}, bf16[384,128]{1,0:T(8,128)(2,1)S(1)}, u32[]{:S(2)}, u32[]{:S(2)}) collective-permute-start(bf16[384,128]{1,0:T(8,128)(2,1)S(1)} %get-tuple-element.86), channel_id=1, source_target_pairs={{0,12},{4,0},{8,4},{12,8},{1,13},{5,1},{9,5},{13,9},{2,14},{6,2},{... | collective-permute-start | bytes 294920 | tf_op jit(solution)/shard_map/ppermute | solution.py:214
  48.4 2.5 %collective-permute-start.15 = (f32[8,128]{1,0:T(8,128)S(1)}, f32[8,128]{1,0:T(8,128)S(1)}, u32[]{:S(2)}, u32[]{:S(2)}) collective-permute-start(f32[8,128]{1,0:T(8,128)S(1)} %add.3.refs_0_), channel_id=1, source_target_pairs={{0,3},{1,2},{2,1},{3,0},{4,7},{5,6},{6,5},{7,4},{8,11},{9,10},{10,... | collective-permute-start | bytes 12296 | tf_op jit(solution)/shard_map/ppermute | solution.py:219
  50.9 0.5 collective-permute-start.14
  51.4 0.5 collective-permute-start.13
  51.9 3.5 %backward.1.grad_ref = bf16[256,128]{1,0:T(8,128)(2,1)S(1)} custom-call(bf16[3,768,128]{2,1,0:T(8,128)(2,1)S(1)} %get-tuple-element.76.refs_0_, f32[2,768,128]{2,1,0:T(8,128)S(1)} %get-tuple-element.77.refs_1_, bf16[768,256]{1,0:T(8,128)(2,1)S(1)} %get-tuple-element.78.refs_2_, s32[16,128]{1,0:T(8,128)S(1)} %get-tuple-element.79.refs_3_, ...), custom_call_target="tpu_custom_call" | custom-call | flops 6000000000 | bytes 1572864 | tf_op jit(solution)/shard_map/backward/pallas_call | solution.py:592
  55.5 2.0 %collective-permute-start.18 = (bf16[272,128]{1,0:T(8,128)(2,1)S(1)}, bf16[272,128]{1,0:T(8,128)(2,1)S(1)}, u32[]{:S(2)}, u32[]{:S(2)}) collective-permute-start(bf16[272,128]{1,0:T(8,128)(2,1)S(1)} %join.1.refs_0_), channel_id=1, source_target_pairs={{0,12},{4,0},{8,4},{12,8},{1,13},{5,1},{9,5},{13,9},{2,14},{6,2},{... | collective-permute-start | bytes 208904 | tf_op jit(solution)/shard_map/ppermute | solution.py:214
  57.5 0.1 collective-permute-start.17
  57.6 1.3 %collective-permute-start.16 = (bf16[272,128]{1,0:T(8,128)(2,1)S(1)}, bf16[272,128]{1,0:T(8,128)(2,1)S(1)}, u32[]{:S(2)}, u32[]{:S(2)}) collective-permute-start(bf16[272,128]{1,0:T(8,128)(2,1)S(1)} %join.1.refs_0_), channel_id=1, source_target_pairs={{0,4},{4,8},{8,12},{12,0},{1,5},{5,9},{9,13},{13,1},{2,6},{6,10},{... | collective-permute-start | bytes 208904 | tf_op jit(solution)/shard_map/ppermute | solution.py:214
  59.0 1.2 %unpack.1 = (bf16[1536,128]{1,0:T(8,128)(2,1)}, bf16[1536,128]{1,0:T(8,128)(2,1)}) custom-call(bf16[384,128]{1,0:T(8,128)(2,1)S(1)} %get-tuple-element.55.refs_0_, bf16[384,128]{1,0:T(8,128)(2,1)S(1)} %collective-permute-done.6.refs_1_, bf16[384,128]{1,0:T(8,128)(2,1)S(1)} %collective-permute-done.7.refs_2_, ...), custom_call_target="tpu_custom_call" | custom-call | bytes 2359296 | tf_op jit(solution)/shard_map/unpack/pallas_call | solution.py:622
  60.1 4.3 %collective-permute-done.17.refs_2_ = bf16[272,128]{1,0:T(8,128)(2,1)S(1)} collective-permute-done((bf16[272,128]{1,0:T(8,128)(2,1)S(1)}, bf16[272,128]{1,0:T(8,128)(2,1)S(1)}, u32[]{:S(2)}, u32[]{:S(2)}) %collective-permute-start.17) | collective-permute-done | bytes 69664 | tf_op jit(solution)/shard_map/ppermute | solution.py:214
  64.5 0.8 %final.1 = (f32[8,128,128]{2,1,0:T(8,128)}, f32[1,128]{1,0:T(1,128)}) custom-call(bf16[272,128]{1,0:T(8,128)(2,1)S(1)} %join.1.refs_0_, bf16[272,128]{1,0:T(8,128)(2,1)S(1)} %collective-permute-done.16.refs_1_, bf16[272,128]{1,0:T(8,128)(2,1)S(1)} %collective-permute-done.17.refs_2_, bf16[272,128]{1,0:T(8,128)(2,1)S(1)} %collective-permute-done.18.refs_3_), custom_call_target="tpu_custom_call" | custom-call | bytes 1048576 | tf_op jit(solution)/shard_map/final/pallas_call | solution.py:630
  (21 shorter events, 0.1 us)
Async XLA Ops:
  4.4 10.2 %collective-permute-start = (bf16[592,128]{1,0:T(8,128)(2,1)}, bf16[592,128]{1,0:T(8,128)(2,1)S(1)}, u32[]{:S(2)}, u32[]{:S(2)}) collective-permute-start(bf16[592,128]{1,0:T(8,128)(2,1)} %get-tuple-element.51), channel_id=1, source_target_pairs={{0,4},{4,8},{8,12},{12,0},{1,5},{5,9},{9,13},{13,1},{2,6},{6,10},{... | collective-permute-start | bytes 454664 | tf_op jit(solution)/shard_map/ppermute | solution.py:214
  7.5 13.6 %collective-permute-start.1 = (bf16[592,128]{1,0:T(8,128)(2,1)}, bf16[592,128]{1,0:T(8,128)(2,1)S(1)}, u32[]{:S(2)}, u32[]{:S(2)}) collective-permute-start(bf16[592,128]{1,0:T(8,128)(2,1)} %get-tuple-element.52), channel_id=1, source_target_pairs={{0,8},{4,12},{8,0},{12,4},{1,9},{5,13},{9,1},{13,5},{2,10},{6,14},... | collective-permute-start | bytes 454664 | tf_op jit(solution)/shard_map/ppermute | solution.py:214
  10.1 13.4 %collective-permute-start.2 = (bf16[592,128]{1,0:T(8,128)(2,1)}, bf16[592,128]{1,0:T(8,128)(2,1)S(1)}, u32[]{:S(2)}, u32[]{:S(2)}) collective-permute-start(bf16[592,128]{1,0:T(8,128)(2,1)} %get-tuple-element.53), channel_id=1, source_target_pairs={{0,12},{4,0},{8,4},{12,8},{1,13},{5,1},{9,5},{13,9},{2,14},{6,2},{... | collective-permute-start | bytes 454664 | tf_op jit(solution)/shard_map/ppermute | solution.py:214
  11.4 27.5 %collective-permute-start.3 = (bf16[592,128]{1,0:T(8,128)(2,1)}, bf16[592,128]{1,0:T(8,128)(2,1)S(1)}, u32[]{:S(2)}, u32[]{:S(2)}) collective-permute-start(bf16[592,128]{1,0:T(8,128)(2,1)} %get-tuple-element.61), channel_id=1, source_target_pairs={{0,4},{4,8},{8,12},{12,0},{1,5},{5,9},{9,13},{13,1},{2,6},{6,10},{... | collective-permute-start | bytes 454664 | tf_op jit(solution)/shard_map/ppermute | solution.py:214
  12.1 26.8 %collective-permute-start.4 = (bf16[592,128]{1,0:T(8,128)(2,1)}, bf16[592,128]{1,0:T(8,128)(2,1)S(1)}, u32[]{:S(2)}, u32[]{:S(2)}) collective-permute-start(bf16[592,128]{1,0:T(8,128)(2,1)} %get-tuple-element.62), channel_id=1, source_target_pairs={{0,8},{4,12},{8,0},{12,4},{1,9},{5,13},{9,1},{13,5},{2,10},{6,14},... | collective-permute-start | bytes 454664 | tf_op jit(solution)/shard_map/ppermute | solution.py:214
  14.6 24.3 %collective-permute-start.5 = (bf16[592,128]{1,0:T(8,128)(2,1)}, bf16[592,128]{1,0:T(8,128)(2,1)S(1)}, u32[]{:S(2)}, u32[]{:S(2)}) collective-permute-start(bf16[592,128]{1,0:T(8,128)(2,1)} %get-tuple-element.63), channel_id=1, source_target_pairs={{0,12},{4,0},{8,4},{12,8},{1,13},{5,1},{9,5},{13,9},{2,14},{6,2},{... | collective-permute-start | bytes 454664 | tf_op jit(solution)/shard_map/ppermute | solution.py:214
  23.5 0.9 %copy-start.1 = (bf16[592,128]{1,0:T(8,128)(2,1)S(1)}, bf16[592,128]{1,0:T(8,128)(2,1)}, u32[]{:S(2)}) copy-start(bf16[592,128]{1,0:T(8,128)(2,1)} %get-tuple-element.50.refs_0_) | copy-start | bytes 454660
  24.4 0.9 %copy-start.2 = (f32[2,128,128]{2,1,0:T(8,128)S(1)}, f32[2,128,128]{2,1,0:T(8,128)}, u32[]{:S(2)}) copy-start(f32[2,128,128]{2,1,0:T(8,128)} %get-tuple-element.54.refs_4_) | copy-start | bytes 393220
  25.3 13.6 %copy-start = (bf16[592,128]{1,0:T(8,128)(2,1)S(1)}, bf16[592,128]{1,0:T(8,128)(2,1)}, u32[]{:S(2)}) copy-start(bf16[592,128]{1,0:T(8,128)(2,1)} %get-tuple-element.60.refs_0_) | copy-start | bytes 454660
  29.1 17.2 %collective-permute-start.6 = (bf16[384,128]{1,0:T(8,128)(2,1)S(1)}, bf16[384,128]{1,0:T(8,128)(2,1)S(1)}, u32[]{:S(2)}, u32[]{:S(2)}) collective-permute-start(bf16[384,128]{1,0:T(8,128)(2,1)S(1)} %get-tuple-element.69), channel_id=1, source_target_pairs={{0,4},{4,8},{8,12},{12,0},{1,5},{5,9},{9,13},{13,1},{2,6},{6,10},{... | collective-permute-start | bytes 294920 | tf_op jit(solution)/shard_map/ppermute | solution.py:214
  36.2 12.2 %collective-permute-start.7 = (bf16[384,128]{1,0:T(8,128)(2,1)S(1)}, bf16[384,128]{1,0:T(8,128)(2,1)S(1)}, u32[]{:S(2)}, u32[]{:S(2)}) collective-permute-start(bf16[384,128]{1,0:T(8,128)(2,1)S(1)} %get-tuple-element.70), channel_id=1, source_target_pairs={{0,8},{4,12},{8,0},{12,4},{1,9},{5,13},{9,1},{13,5},{2,10},{6,14},... | collective-permute-start | bytes 294920 | tf_op jit(solution)/shard_map/ppermute | solution.py:214
  38.9 11.9 %collective-permute-start.8 = (bf16[384,128]{1,0:T(8,128)(2,1)S(1)}, bf16[384,128]{1,0:T(8,128)(2,1)S(1)}, u32[]{:S(2)}, u32[]{:S(2)}) collective-permute-start(bf16[384,128]{1,0:T(8,128)(2,1)S(1)} %get-tuple-element.71), channel_id=1, source_target_pairs={{0,12},{4,0},{8,4},{12,8},{1,13},{5,1},{9,5},{13,9},{2,14},{6,2},{... | collective-permute-start | bytes 294920 | tf_op jit(solution)/shard_map/ppermute | solution.py:214
  42.7 8.7 %collective-permute-start.9 = (bf16[384,128]{1,0:T(8,128)(2,1)S(1)}, bf16[384,128]{1,0:T(8,128)(2,1)S(1)}, u32[]{:S(2)}, u32[]{:S(2)}) collective-permute-start(bf16[384,128]{1,0:T(8,128)(2,1)S(1)} %get-tuple-element.84), channel_id=1, source_target_pairs={{0,4},{4,8},{8,12},{12,0},{1,5},{5,9},{9,13},{13,1},{2,6},{6,10},{... | collective-permute-start | bytes 294920 | tf_op jit(solution)/shard_map/ppermute | solution.py:214
  44.8 1.2 %collective-permute-start.12 = (f32[8,128]{1,0:T(8,128)S(1)}, f32[8,128]{1,0:T(8,128)S(1)}, u32[]{:S(2)}, u32[]{:S(2)}) collective-permute-start(f32[8,128]{1,0:T(8,128)S(1)} %get-tuple-element.93), channel_id=1, source_target_pairs={{0,16},{16,0},{1,17},{17,1},{2,18},{18,2},{3,19},{19,3},{4,20},{20... | collective-permute-start | bytes 12296 | tf_op jit(solution)/shard_map/ppermute | solution.py:219
  46.0 9.5 %collective-permute-start.10 = (bf16[384,128]{1,0:T(8,128)(2,1)S(1)}, bf16[384,128]{1,0:T(8,128)(2,1)S(1)}, u32[]{:S(2)}, u32[]{:S(2)}) collective-permute-start(bf16[384,128]{1,0:T(8,128)(2,1)S(1)} %get-tuple-element.85), channel_id=1, source_target_pairs={{0,8},{4,12},{8,0},{12,4},{1,9},{5,13},{9,1},{13,5},{2,10},{6,14},... | collective-permute-start | bytes 294920 | tf_op jit(solution)/shard_map/ppermute | solution.py:214
  46.2 9.2 %collective-permute-start.11 = (bf16[384,128]{1,0:T(8,128)(2,1)S(1)}, bf16[384,128]{1,0:T(8,128)(2,1)S(1)}, u32[]{:S(2)}, u32[]{:S(2)}) collective-permute-start(bf16[384,128]{1,0:T(8,128)(2,1)S(1)} %get-tuple-element.86), channel_id=1, source_target_pairs={{0,12},{4,0},{8,4},{12,8},{1,13},{5,1},{9,5},{13,9},{2,14},{6,2},{... | collective-permute-start | bytes 294920 | tf_op jit(solution)/shard_map/ppermute | solution.py:214
  48.4 7.0 %collective-permute-start.15 = (f32[8,128]{1,0:T(8,128)S(1)}, f32[8,128]{1,0:T(8,128)S(1)}, u32[]{:S(2)}, u32[]{:S(2)}) collective-permute-start(f32[8,128]{1,0:T(8,128)S(1)} %add.3.refs_0_), channel_id=1, source_target_pairs={{0,3},{1,2},{2,1},{3,0},{4,7},{5,6},{6,5},{7,4},{8,11},{9,10},{10,... | collective-permute-start | bytes 12296 | tf_op jit(solution)/shard_map/ppermute | solution.py:219
  50.9 4.6 %collective-permute-start.14 = (f32[8,128]{1,0:T(8,128)S(1)}, f32[8,128]{1,0:T(8,128)S(1)}, u32[]{:S(2)}, u32[]{:S(2)}) collective-permute-start(f32[8,128]{1,0:T(8,128)S(1)} %add.3.refs_0_), channel_id=1, source_target_pairs={{0,2},{1,3},{2,0},{3,1},{4,6},{5,7},{6,4},{7,5},{8,10},{9,11},{10,... | collective-permute-start | bytes 12296 | tf_op jit(solution)/shard_map/ppermute | solution.py:219
  51.4 4.1 %collective-permute-start.13 = (f32[8,128]{1,0:T(8,128)S(1)}, f32[8,128]{1,0:T(8,128)S(1)}, u32[]{:S(2)}, u32[]{:S(2)}) collective-permute-start(f32[8,128]{1,0:T(8,128)S(1)} %add.3.refs_0_), channel_id=1, source_target_pairs={{0,1},{1,0},{2,3},{3,2},{4,5},{5,4},{6,7},{7,6},{8,9},{9,8},{10,11... | collective-permute-start | bytes 12296 | tf_op jit(solution)/shard_map/ppermute | solution.py:219
  55.5 4.7 %collective-permute-start.18 = (bf16[272,128]{1,0:T(8,128)(2,1)S(1)}, bf16[272,128]{1,0:T(8,128)(2,1)S(1)}, u32[]{:S(2)}, u32[]{:S(2)}) collective-permute-start(bf16[272,128]{1,0:T(8,128)(2,1)S(1)} %join.1.refs_0_), channel_id=1, source_target_pairs={{0,12},{4,0},{8,4},{12,8},{1,13},{5,1},{9,5},{13,9},{2,14},{6,2},{... | collective-permute-start | bytes 208904 | tf_op jit(solution)/shard_map/ppermute | solution.py:214
  57.5 7.0 %collective-permute-start.17 = (bf16[272,128]{1,0:T(8,128)(2,1)S(1)}, bf16[272,128]{1,0:T(8,128)(2,1)S(1)}, u32[]{:S(2)}, u32[]{:S(2)}) collective-permute-start(bf16[272,128]{1,0:T(8,128)(2,1)S(1)} %join.1.refs_0_), channel_id=1, source_target_pairs={{0,8},{4,12},{8,0},{12,4},{1,9},{5,13},{9,1},{13,5},{2,10},{6,14},... | collective-permute-start | bytes 208904 | tf_op jit(solution)/shard_map/ppermute | solution.py:214
  57.6 6.8 %collective-permute-start.16 = (bf16[272,128]{1,0:T(8,128)(2,1)S(1)}, bf16[272,128]{1,0:T(8,128)(2,1)S(1)}, u32[]{:S(2)}, u32[]{:S(2)}) collective-permute-start(bf16[272,128]{1,0:T(8,128)(2,1)S(1)} %join.1.refs_0_), channel_id=1, source_target_pairs={{0,4},{4,8},{8,12},{12,0},{1,5},{5,9},{9,13},{13,1},{2,6},{6,10},{... | collective-permute-start | bytes 208904 | tf_op jit(solution)/shard_map/ppermute | solution.py:214

commit v3 on v2

--- a/solution.py
+++ b/solution.py
@@ -16,7 +16,7 @@
 LOG2E = math.log2(math.e)
 COPIES = 4
 
-PACK_VMEM = 62
+PACK_VMEM = 60
 HEAD_COST = 6_000_000_000
 
 
@@ -261,12 +261,26 @@
     return lax.rem(lax.axis_index("seq") + (seq_count - shift), seq_count)
 
 
-def pack_kernel(seq_count, per_place, q_ref, k_ref, v_ref, map_ref, doc_ref, *rest):
-    outs = rest[: seq_count * per_place]
-    own_map, narrow, wide, sems = rest[seq_count * per_place :]
-    rows = doc_ref.shape[1]
+def deal(wide, docs, parts, outs, seq_count, per_place):
+    rows = docs.shape[1]
     heads = seq_count * per_place
-    part = rows * heads // COPIES
+    meta_row = lax.broadcasted_iota(jnp.int32, (META_ROWS, LANES), 0)
+    meta = jnp.zeros((META_ROWS, LANES), jnp.float32)
+    for value in range(DOC_VALUES - 1):
+        amount = jnp.sum((docs <= value).astype(jnp.float32), axis=1, keepdims=True)
+        meta = jnp.where(meta_row == value, amount, meta)
+    for (chunk, shift), out in zip(parts, outs):
+        head = lax.rem(lax.axis_index("seq") + shift, seq_count) * per_place + chunk
+        for n in range(3):
+            out[n * rows : (n + 1) * rows, :] = wide[
+                n, pl.ds(head, rows, stride=heads), :
+            ].astype(jnp.bfloat16)
+        out[3 * rows :, :] = meta.astype(jnp.bfloat16)
+
+
+def pack_kernel(seq_count, per_place, parts, q_ref, k_ref, v_ref, doc_ref, *rest):
+    outs, (narrow, wide, docs, sems) = rest[: len(parts)], rest[len(parts) :]
+    part = narrow.shape[1] // COPIES
     copies = []
     for n, ref in enumerate((q_ref, k_ref, v_ref)):
         for piece in range(COPIES):
@@ -276,31 +290,25 @@
                     ref.at[span, :], narrow.at[n, span, :], sems.at[n * COPIES + piece]
                 )
             )
-    own = pl.ds(lax.axis_index("seq") * per_place, per_place)
-    copies.append(pltpu.make_async_copy(map_ref.at[own], own_map, sems.at[3 * COPIES]))
+    copies.append(pltpu.make_async_copy(doc_ref, docs, sems.at[3 * COPIES]))
     for copy in copies:
         copy.start()
-    docs = doc_ref[...]
-    meta_row = lax.broadcasted_iota(jnp.int32, (META_ROWS, LANES), 0)
-    meta = jnp.zeros((META_ROWS, LANES), jnp.float32)
-    for value in range(DOC_VALUES - 1):
-        amount = jnp.sum((docs <= value).astype(jnp.float32), axis=1, keepdims=True)
-        meta = jnp.where(meta_row == value, amount, meta)
     for n in range(3):
         for piece in range(COPIES):
             copies[n * COPIES + piece].wait()
             span = pl.ds(piece * part, part)
             wide[n, span, :] = narrow[n, span, :].astype(jnp.float32)
+    copies[-1].wait()
+    deal(wide, docs[...], parts, outs, seq_count, per_place)
+
+
+def pack_rest_kernel(seq_count, per_place, parts, q_ref, k_ref, v_ref, doc_ref, map_ref, *rest):
+    outs, (own_map, wide) = rest[: len(parts)], rest[len(parts) :]
+    for n, ref in enumerate((q_ref, k_ref, v_ref)):
+        wide[n] = ref[...].astype(jnp.float32)
+    deal(wide, doc_ref[...], parts, outs, seq_count, per_place)
     for chunk in range(per_place):
-        for shift in range(seq_count):
-            out = outs[chunk * seq_count + shift]
-            head = lax.rem(lax.axis_index("seq") + shift, seq_count) * per_place + chunk
-            for n in range(3):
-                out[n * rows : (n + 1) * rows, :] = wide[
-                    n, pl.ds(head, rows, stride=heads), :
-                ].astype(jnp.bfloat16)
-            out[3 * rows :, :] = meta.astype(jnp.bfloat16)
-    copies[-1].wait()
+        own_map[chunk] = map_ref[lax.axis_index("seq") * per_place + chunk]
 
 
 def half_sums(array, ones_block):
@@ -540,25 +548,38 @@
         blocks, passed = lax.optimization_barrier((blocks, arrived[1:]))
         return blocks, arrived[:1] + passed
 
-    *packed, own_map = kernel_call(
-        functools.partial(pack_kernel, seq_count, per_place),
-        sizes(*[sent_rows] * head_count)
-        + [jax.ShapeDtypeStruct((per_place,) + feature_map.shape[1:], f32)],
+    first_parts = [(0, shift) for shift in range(1, seq_count)]
+    later_parts = [(0, 0)] + [
+        (chunk, shift) for chunk in range(1, per_place) for shift in range(seq_count)
+    ]
+    wide = pltpu.VMEM((3, tok_rows * head_count, LANES), f32)
+    first_packed = kernel_call(
+        functools.partial(pack_kernel, seq_count, per_place, first_parts),
+        sizes(*[sent_rows] * len(first_parts)),
         [
             pltpu.VMEM((3, tok_rows * head_count, LANES), bf16),
-            pltpu.VMEM((3, tok_rows * head_count, LANES), f32),
+            wide,
+            pltpu.VMEM((1, tok_rows), jnp.int32),
             pltpu.SemaphoreType.DMA((3 * COPIES + 1,)),
         ],
         0,
         12 * tok_rows * head_count * LANES,
         "pack",
         vmem=PACK_VMEM,
-        in_specs=[pl.BlockSpec(memory_space=pltpu.HBM)] * 4
-        + [pl.BlockSpec(memory_space=pltpu.VMEM)],
-    )(*flat, feature_map, docs)
-    held = [
-        sent(packed[chunk * seq_count : (chunk + 1) * seq_count]) for chunk in range(per_place)
-    ]
+        in_specs=[pl.BlockSpec(memory_space=pltpu.HBM)] * 4,
+    )(*flat, docs)
+    *packed, own_map = kernel_call(
+        functools.partial(pack_rest_kernel, seq_count, per_place, later_parts),
+        sizes(*[sent_rows] * len(later_parts))
+        + [jax.ShapeDtypeStruct((per_place,) + feature_map.shape[1:], f32)],
+        [wide],
+        0,
+        12 * tok_rows * head_count * LANES,
+        "pack_rest",
+    )(*flat, docs, feature_map)
+    held = [sent(packed[:1] + list(first_packed))]
+    for chunk in range(1, per_place):
+        held.append(sent(packed[1 + (chunk - 1) * seq_count : 1 + chunk * seq_count]))
 
     returned, saved = [], []
     loss = jnp.zeros((8, LANES), f32)
@@ -608,8 +629,6 @@
         losses = [loss] + [crossed(loss, "head", mask) for mask in range(1, 4)]
     else:
         losses = [summed_over(loss, "head")]
-    for n in range(1, per_place):
-        grad, returned[n] = after(grad, returned[n])
     joined = kernel_call(
         join_kernel,
         sizes(per_place * LANES + META_ROWS)[0],
@@ -618,7 +637,13 @@
         16 * LANES * LANES,
         "join",
     )(grad, *losses)
-    last = sent([joined] * seq_count)
+    last = [joined]
+    for shift in range(1, seq_count):
+        behind = [pieces[shift] for pieces in returned[1:]]
+        block, behind = lax.optimization_barrier((joined, behind))
+        for pieces, piece in zip(returned[1:], behind):
+            pieces[shift] = piece
+        last.append(turned(block, "seq", shift))
     teacher_out, student_out = kernel_call(
         functools.partial(unpack_kernel, seq_count, per_place),
         sizes(*[tok_rows * head_count] * 2),

time: 65.5 us -> 62.6 us (0.956)
  waiting for transfers between devices: 14 us -> 12.2 us
  local copies, waits for them, and re-layouts: 1.82 us -> 1.05 us
  Pallas kernels: 16.8 us -> 16.1 us
    ppermute x15, waiting for transfers between devices: 12.8 us -> 11.1 us  [turned(): lax.ppermute(block, axis, [(i, (i + distance) % count) for i in range(cou...]
    unnamed x6 -> x10, local copies, waits for them, and re-layouts: 1.82 us -> 1.05 us
    pallas_call x1 -> x2, Pallas kernels: 3.79 us -> 3.03 us  [the longest x1 2.49 us: split_body(): kernel_call(functools.partial(pack_kernel, seq_count, per_place, first_pa...]
  transfers between devices with their start and end apart: 19 -> 19, of which waited for: 5 -> 8; matrix products, arithmetic and copies ran while one was open for 0% -> 0% of each run, Pallas kernels for 19% -> 20%
where the time goes in v3:
time: 62.6 us; the launch traced here: 62.4 us
  starting transfers between devices  32.3 us (52%)
  Pallas kernels  16.1 us (26%)
  waiting for transfers between devices  12.2 us (19%)
  local copies, waits for them, and re-layouts  1.05 us (2%)
  between operations  0.76 us (1%)
    ppermute x15, starting transfers between devices, turned(): lax.ppermute(block, axis, [(i, (i + distance) % count) for i in range(cou...  29 us
    ppermute x15, waiting for transfers between devices, turned(): lax.ppermute(block, axis, [(i, (i + distance) % count) for i in range(cou...  11.1 us
    pallas_call x2, Pallas kernels, split_body(): kernel_call(functools.partial(forward_kernel, seq_count, chunk, score_sca...  7.47 us
    pallas_call x1, Pallas kernels, split_body(): kernel_call(functools.partial(backward_kernel, per_place), sizes(per_plac...  3.5 us
    ppermute x4, starting transfers between devices, crossed(): return lax.ppermute(block, axis, [(i, i ^ mask) for i in range(count)])  3.27 us
    pallas_call x1, Pallas kernels, split_body(): kernel_call(functools.partial(pack_kernel, seq_count, per_place, first_pa...  2.49 us
  transfers between devices with their start and end apart: 19, of which 8 were waited for; matrix products, arithmetic and copies ran while one was open for 0% of the time, Pallas kernels for 20%

profile of v3, /device:TPU:0, one launch (start us, length us, event | category | flops | bytes accessed | tf_op | source)
XLA Modules:
  0.0 62.4 jit_solution(17104493632240105176)
XLA Ops:
  0.7 2.5 %pack.1 = (bf16[592,128]{1,0:T(8,128)(2,1)}, bf16[592,128]{1,0:T(8,128)(2,1)}, bf16[592,128]{1,0:T(8,128)(2,1)}) custom-call(bf16[1536,128]{1,0:T(8,128)(2,1)} %bitcast.8, bf16[1536,128]{1,0:T(8,128)(2,1)} %bitcast.10, bf16[1536,128]{1,0:T(8,128)(2,1)} %bitcast.12, s32[1,192]{1,0:T(1,128)} %bitcast.14), custom_call_target="tpu_custom_call" | custom-call | bytes 2359296 | tf_op jit(solution)/shard_map/pack/pallas_call | solution.py:556
  3.2 3.1 %collective-permute-start = (bf16[592,128]{1,0:T(8,128)(2,1)}, bf16[592,128]{1,0:T(8,128)(2,1)S(1)}, u32[]{:S(2)}, u32[]{:S(2)}) collective-permute-start(bf16[592,128]{1,0:T(8,128)(2,1)} %get-tuple-element.53), channel_id=1, source_target_pairs={{0,4},{4,8},{8,12},{12,0},{1,5},{5,9},{9,13},{13,1},{2,6},{6,10},{... | collective-permute-start | bytes 454664 | tf_op jit(solution)/shard_map/ppermute | solution.py:214
  6.2 2.6 %collective-permute-start.1 = (bf16[592,128]{1,0:T(8,128)(2,1)}, bf16[592,128]{1,0:T(8,128)(2,1)S(1)}, u32[]{:S(2)}, u32[]{:S(2)}) collective-permute-start(bf16[592,128]{1,0:T(8,128)(2,1)} %get-tuple-element.54), channel_id=1, source_target_pairs={{0,8},{4,12},{8,0},{12,4},{1,9},{5,13},{9,1},{13,5},{2,10},{6,14},... | collective-permute-start | bytes 454664 | tf_op jit(solution)/shard_map/ppermute | solution.py:214
  8.8 1.3 %collective-permute-start.2 = (bf16[592,128]{1,0:T(8,128)(2,1)}, bf16[592,128]{1,0:T(8,128)(2,1)S(1)}, u32[]{:S(2)}, u32[]{:S(2)}) collective-permute-start(bf16[592,128]{1,0:T(8,128)(2,1)} %get-tuple-element.55), channel_id=1, source_target_pairs={{0,12},{4,0},{8,4},{12,8},{1,13},{5,1},{9,5},{13,9},{2,14},{6,2},{... | collective-permute-start | bytes 454664 | tf_op jit(solution)/shard_map/ppermute | solution.py:214
  10.2 1.0 %copy-done.3 = f32[8,128,128]{2,1,0:T(8,128)S(1)} copy-done((f32[8,128,128]{2,1,0:T(8,128)S(1)}, f32[8,128,128]{2,1,0:T(8,128)}, u32[]{:S(2)}) %copy-start.3) | copy-done | bytes 524312
  11.2 0.5 pack_rest.1
  11.8 0.7 %collective-permute-start.3 = (bf16[592,128]{1,0:T(8,128)(2,1)S(1)}, bf16[592,128]{1,0:T(8,128)(2,1)S(1)}, u32[]{:S(2)}, u32[]{:S(2)}) collective-permute-start(bf16[592,128]{1,0:T(8,128)(2,1)S(1)} %get-tuple-element.63), channel_id=1, source_target_pairs={{0,4},{4,8},{8,12},{12,0},{1,5},{5,9},{9,13},{13,1},{2,6},{6,10},{... | collective-permute-start | bytes 454664 | tf_op jit(solution)/shard_map/ppermute | solution.py:214
  12.8 0.5 collective-permute-done.refs_1_
  13.3 2.3 %collective-permute-start.5 = (bf16[592,128]{1,0:T(8,128)(2,1)S(1)}, bf16[592,128]{1,0:T(8,128)(2,1)S(1)}, u32[]{:S(2)}, u32[]{:S(2)}) collective-permute-start(bf16[592,128]{1,0:T(8,128)(2,1)S(1)} %get-tuple-element.65), channel_id=1, source_target_pairs={{0,12},{4,0},{8,4},{12,8},{1,13},{5,1},{9,5},{13,9},{2,14},{6,2},{... | collective-permute-start | bytes 454664 | tf_op jit(solution)/shard_map/ppermute | solution.py:214
  15.7 4.2 %collective-permute-done.1.refs_2_ = bf16[592,128]{1,0:T(8,128)(2,1)S(1)} collective-permute-done((bf16[592,128]{1,0:T(8,128)(2,1)}, bf16[592,128]{1,0:T(8,128)(2,1)S(1)}, u32[]{:S(2)}, u32[]{:S(2)}) %collective-permute-start.1) | collective-permute-done | bytes 151584 | tf_op jit(solution)/shard_map/ppermute | solution.py:214
  19.9 2.2 %collective-permute-done.2.refs_3_ = bf16[592,128]{1,0:T(8,128)(2,1)S(1)} collective-permute-done((bf16[592,128]{1,0:T(8,128)(2,1)}, bf16[592,128]{1,0:T(8,128)(2,1)S(1)}, u32[]{:S(2)}, u32[]{:S(2)}) %collective-permute-start.2) | collective-permute-done | bytes 151584 | tf_op jit(solution)/shard_map/ppermute | solution.py:214
  22.1 3.7 %forward.2 = (bf16[384,128]{1,0:T(8,128)(2,1)S(1)}, bf16[384,128]{1,0:T(8,128)(2,1)S(1)}, bf16[384,128]{1,0:T(8,128)(2,1)S(1)}, bf16[384,128]{1,0:T(8,128)(2,1)S...) custom-call(bf16[592,128]{1,0:T(8,128)(2,1)S(1)} %get-tuple-element., ...), custom_call_target="tpu_custom_call" | custom-call | flops 6000000000 | bytes 1572864 | tf_op jit(solution)/shard_map/forward/pallas_call | solution.py:587
  25.8 8.2 %collective-permute-start.6 = (bf16[384,128]{1,0:T(8,128)(2,1)S(1)}, bf16[384,128]{1,0:T(8,128)(2,1)S(1)}, u32[]{:S(2)}, u32[]{:S(2)}) collective-permute-start(bf16[384,128]{1,0:T(8,128)(2,1)S(1)} %get-tuple-element.71), channel_id=1, source_target_pairs={{0,4},{4,8},{8,12},{12,0},{1,5},{5,9},{9,13},{13,1},{2,6},{6,10},{... | collective-permute-start | bytes 294920 | tf_op jit(solution)/shard_map/ppermute | solution.py:214
  34.0 1.8 %collective-permute-start.7 = (bf16[384,128]{1,0:T(8,128)(2,1)S(1)}, bf16[384,128]{1,0:T(8,128)(2,1)S(1)}, u32[]{:S(2)}, u32[]{:S(2)}) collective-permute-start(bf16[384,128]{1,0:T(8,128)(2,1)S(1)} %get-tuple-element.72), channel_id=1, source_target_pairs={{0,8},{4,12},{8,0},{12,4},{1,9},{5,13},{9,1},{13,5},{2,10},{6,14},... | collective-permute-start | bytes 294920 | tf_op jit(solution)/shard_map/ppermute | solution.py:214
  35.8 0.6 collective-permute-start.8
  36.4 3.7 %forward.3 = (bf16[384,128]{1,0:T(8,128)(2,1)S(1)}, bf16[384,128]{1,0:T(8,128)(2,1)S(1)}, bf16[384,128]{1,0:T(8,128)(2,1)S(1)}, bf16[384,128]{1,0:T(8,128)(2,1)S...) custom-call(bf16[592,128]{1,0:T(8,128)(2,1)S(1)} %get-tuple-element., ...), custom_call_target="tpu_custom_call" | custom-call | flops 6000000000 | bytes 1572864 | tf_op jit(solution)/shard_map/forward/pallas_call | solution.py:587
  40.3 1.2 %collective-permute-done.9 = f32[8,128]{1,0:T(8,128)S(1)} collective-permute-done((f32[8,128]{1,0:T(8,128)S(1)}, f32[8,128]{1,0:T(8,128)S(1)}, u32[]{:S(2)}, u32[]{:S(2)}) %collective-permute-start.9) | collective-permute-done | bytes 4128 | tf_op jit(solution)/shard_map/ppermute | solution.py:219
  41.4 2.1 %collective-permute-start.12 = (f32[8,128]{1,0:T(8,128)S(1)}, f32[8,128]{1,0:T(8,128)S(1)}, u32[]{:S(2)}, u32[]{:S(2)}) collective-permute-start(f32[8,128]{1,0:T(8,128)S(1)} %add.3.refs_0_), channel_id=1, source_target_pairs={{0,3},{1,2},{2,1},{3,0},{4,7},{5,6},{6,5},{7,4},{8,11},{9,10},{10,... | collective-permute-start | bytes 12296 | tf_op jit(solution)/shard_map/ppermute | solution.py:219
  43.6 1.7 %collective-permute-start.13 = (bf16[384,128]{1,0:T(8,128)(2,1)S(1)}, bf16[384,128]{1,0:T(8,128)(2,1)S(1)}, u32[]{:S(2)}, u32[]{:S(2)}) collective-permute-start(bf16[384,128]{1,0:T(8,128)(2,1)S(1)} %get-tuple-element.87), channel_id=1, source_target_pairs={{0,4},{4,8},{8,12},{12,0},{1,5},{5,9},{9,13},{13,1},{2,6},{6,10},{... | collective-permute-start | bytes 294920 | tf_op jit(solution)/shard_map/ppermute | solution.py:214
  45.3 0.8 %collective-permute-start.14 = (bf16[384,128]{1,0:T(8,128)(2,1)S(1)}, bf16[384,128]{1,0:T(8,128)(2,1)S(1)}, u32[]{:S(2)}, u32[]{:S(2)}) collective-permute-start(bf16[384,128]{1,0:T(8,128)(2,1)S(1)} %get-tuple-element.89), channel_id=1, source_target_pairs={{0,8},{4,12},{8,0},{12,4},{1,9},{5,13},{9,1},{13,5},{2,10},{6,14},... | collective-permute-start | bytes 294920 | tf_op jit(solution)/shard_map/ppermute | solution.py:214
  46.1 1.7 %collective-permute-start.15 = (bf16[384,128]{1,0:T(8,128)(2,1)S(1)}, bf16[384,128]{1,0:T(8,128)(2,1)S(1)}, u32[]{:S(2)}, u32[]{:S(2)}) collective-permute-start(bf16[384,128]{1,0:T(8,128)(2,1)S(1)} %get-tuple-element.91), channel_id=1, source_target_pairs={{0,12},{4,0},{8,4},{12,8},{1,13},{5,1},{9,5},{13,9},{2,14},{6,2},{... | collective-permute-start | bytes 294920 | tf_op jit(solution)/shard_map/ppermute | solution.py:214
  47.8 0.5 collective-permute-start.11
  48.3 0.5 collective-permute-start.10
  48.8 3.5 %backward.1.grad_ref = bf16[256,128]{1,0:T(8,128)(2,1)S(1)} custom-call(bf16[3,768,128]{2,1,0:T(8,128)(2,1)S(1)} %get-tuple-element.78.refs_0_, f32[2,768,128]{2,1,0:T(8,128)S(1)} %get-tuple-element.79.refs_1_, bf16[768,256]{1,0:T(8,128)(2,1)S(1)} %get-tuple-element.80.refs_2_, s32[16,128]{1,0:T(8,128)S(1)} %get-tuple-element.81.refs_3_, ...), custom_call_target="tpu_custom_call" | custom-call | flops 6000000000 | bytes 1572864 | tf_op jit(solution)/shard_map/backward/pallas_call | solution.py:613
  52.4 0.7 %collective-permute-start.16 = (bf16[272,128]{1,0:T(8,128)(2,1)S(1)}, bf16[272,128]{1,0:T(8,128)(2,1)S(1)}, u32[]{:S(2)}, u32[]{:S(2)}) collective-permute-start(bf16[272,128]{1,0:T(8,128)(2,1)S(1)} %join.1.refs_0_), channel_id=1, source_target_pairs={{0,4},{4,8},{8,12},{12,0},{1,5},{5,9},{9,13},{13,1},{2,6},{6,10},{... | collective-permute-start | bytes 208904 | tf_op jit(solution)/shard_map/ppermute | solution.py:214
  53.1 1.2 %collective-permute-done.14.refs_6_ = bf16[384,128]{1,0:T(8,128)(2,1)S(1)} collective-permute-done((bf16[384,128]{1,0:T(8,128)(2,1)S(1)}, bf16[384,128]{1,0:T(8,128)(2,1)S(1)}, u32[]{:S(2)}, u32[]{:S(2)}) %collective-permute-start.14) | collective-permute-done | bytes 98336 | tf_op jit(solution)/shard_map/ppermute | solution.py:214
  54.3 0.7 %collective-permute-start.17 = (bf16[272,128]{1,0:T(8,128)(2,1)S(1)}, bf16[272,128]{1,0:T(8,128)(2,1)S(1)}, u32[]{:S(2)}, u32[]{:S(2)}) collective-permute-start(bf16[272,128]{1,0:T(8,128)(2,1)S(1)} %join.1.refs_0_), channel_id=1, source_target_pairs={{0,8},{4,12},{8,0},{12,4},{1,9},{5,13},{9,1},{13,5},{2,10},{6,14},... | collective-permute-start | bytes 208904 | tf_op jit(solution)/shard_map/ppermute | solution.py:214
  55.0 2.4 %collective-permute-start.18 = (bf16[272,128]{1,0:T(8,128)(2,1)S(1)}, bf16[272,128]{1,0:T(8,128)(2,1)S(1)}, u32[]{:S(2)}, u32[]{:S(2)}) collective-permute-start(bf16[272,128]{1,0:T(8,128)(2,1)S(1)} %join.1.refs_0_), channel_id=1, source_target_pairs={{0,12},{4,0},{8,4},{12,8},{1,13},{5,1},{9,5},{13,9},{2,14},{6,2},{... | collective-permute-start | bytes 208904 | tf_op jit(solution)/shard_map/ppermute | solution.py:214
  57.3 1.2 %unpack.1 = (bf16[1536,128]{1,0:T(8,128)(2,1)}, bf16[1536,128]{1,0:T(8,128)(2,1)}) custom-call(bf16[384,128]{1,0:T(8,128)(2,1)S(1)} %get-tuple-element.57.refs_0_, bf16[384,128]{1,0:T(8,128)(2,1)S(1)} %collective-permute-done.6.refs_1_, bf16[384,128]{1,0:T(8,128)(2,1)S(1)} %collective-permute-done.7.refs_2_, ...), custom_call_target="tpu_custom_call" | custom-call | bytes 2359296 | tf_op jit(solution)/shard_map/unpack/pallas_call | solution.py:647
  58.6 2.3 %collective-permute-done.17.refs_2_ = bf16[272,128]{1,0:T(8,128)(2,1)S(1)} collective-permute-done((bf16[272,128]{1,0:T(8,128)(2,1)S(1)}, bf16[272,128]{1,0:T(8,128)(2,1)S(1)}, u32[]{:S(2)}, u32[]{:S(2)}) %collective-permute-start.17) | collective-permute-done | bytes 69664 | tf_op jit(solution)/shard_map/ppermute | solution.py:214
  61.0 0.5 collective-permute-done.18.refs_3_
  61.5 0.8 %final.1 = (f32[8,128,128]{2,1,0:T(8,128)}, f32[1,128]{1,0:T(1,128)}) custom-call(bf16[272,128]{1,0:T(8,128)(2,1)S(1)} %join.1.refs_0_, bf16[272,128]{1,0:T(8,128)(2,1)S(1)} %collective-permute-done.16.refs_1_, bf16[272,128]{1,0:T(8,128)(2,1)S(1)} %collective-permute-done.17.refs_2_, bf16[272,128]{1,0:T(8,128)(2,1)S(1)} %collective-permute-done.18.refs_3_), custom_call_target="tpu_custom_call" | custom-call | bytes 1048576 | tf_op jit(solution)/shard_map/final/pallas_call | solution.py:655
  (26 shorter events, 0.6 us)
Async XLA Ops:
  0.6 9.6 %copy-start = (bf16[192,8,128]{2,1,0:T(8,128)(2,1)S(1)}, bf16[192,8,128]{2,1,0:T(8,128)(2,1)}, u32[]{:S(2)}) copy-start(bf16[192,8,128]{2,1,0:T(8,128)(2,1)} %param.5) | copy-start | bytes 1179652
  0.6 9.5 %copy-start.1 = (bf16[192,8,128]{2,1,0:T(8,128)(2,1)S(1)}, bf16[192,8,128]{2,1,0:T(8,128)(2,1)}, u32[]{:S(2)}) copy-start(bf16[192,8,128]{2,1,0:T(8,128)(2,1)} %param.6) | copy-start | bytes 1179652
  0.7 9.5 %copy-start.2 = (bf16[192,8,128]{2,1,0:T(8,128)(2,1)S(1)}, bf16[192,8,128]{2,1,0:T(8,128)(2,1)}, u32[]{:S(2)}) copy-start(bf16[192,8,128]{2,1,0:T(8,128)(2,1)} %param.7) | copy-start | bytes 1179652
  3.2 10.2 %collective-permute-start = (bf16[592,128]{1,0:T(8,128)(2,1)}, bf16[592,128]{1,0:T(8,128)(2,1)S(1)}, u32[]{:S(2)}, u32[]{:S(2)}) collective-permute-start(bf16[592,128]{1,0:T(8,128)(2,1)} %get-tuple-element.53), channel_id=1, source_target_pairs={{0,4},{4,8},{8,12},{12,0},{1,5},{5,9},{9,13},{13,1},{2,6},{6,10},{... | collective-permute-start | bytes 454664 | tf_op jit(solution)/shard_map/ppermute | solution.py:214
  6.2 4.0 %copy-start.4 = (s32[192]{0:T(256)S(1)}, s32[192]{0:T(256)}, u32[]{:S(2)}) copy-start(s32[192]{0:T(256)} %param.8) | copy-start | bytes 2308
  6.2 13.6 %collective-permute-start.1 = (bf16[592,128]{1,0:T(8,128)(2,1)}, bf16[592,128]{1,0:T(8,128)(2,1)S(1)}, u32[]{:S(2)}, u32[]{:S(2)}) collective-permute-start(bf16[592,128]{1,0:T(8,128)(2,1)} %get-tuple-element.54), channel_id=1, source_target_pairs={{0,8},{4,12},{8,0},{12,4},{1,9},{5,13},{9,1},{13,5},{2,10},{6,14},... | collective-permute-start | bytes 454664 | tf_op jit(solution)/shard_map/ppermute | solution.py:214
  8.8 13.2 %collective-permute-start.2 = (bf16[592,128]{1,0:T(8,128)(2,1)}, bf16[592,128]{1,0:T(8,128)(2,1)S(1)}, u32[]{:S(2)}, u32[]{:S(2)}) collective-permute-start(bf16[592,128]{1,0:T(8,128)(2,1)} %get-tuple-element.55), channel_id=1, source_target_pairs={{0,12},{4,0},{8,4},{12,8},{1,13},{5,1},{9,5},{13,9},{2,14},{6,2},{... | collective-permute-start | bytes 454664 | tf_op jit(solution)/shard_map/ppermute | solution.py:214
  10.2 1.0 %copy-start.3 = (f32[8,128,128]{2,1,0:T(8,128)S(1)}, f32[8,128,128]{2,1,0:T(8,128)}, u32[]{:S(2)}) copy-start(f32[8,128,128]{2,1,0:T(8,128)} %map_ref.1) | copy-start | bytes 1572868
  11.8 24.1 %collective-permute-start.3 = (bf16[592,128]{1,0:T(8,128)(2,1)S(1)}, bf16[592,128]{1,0:T(8,128)(2,1)S(1)}, u32[]{:S(2)}, u32[]{:S(2)}) collective-permute-start(bf16[592,128]{1,0:T(8,128)(2,1)S(1)} %get-tuple-element.63), channel_id=1, source_target_pairs={{0,4},{4,8},{8,12},{12,0},{1,5},{5,9},{9,13},{13,1},{2,6},{6,10},{... | collective-permute-start | bytes 454664 | tf_op jit(solution)/shard_map/ppermute | solution.py:214
  12.5 23.9 %collective-permute-start.4 = (bf16[592,128]{1,0:T(8,128)(2,1)S(1)}, bf16[592,128]{1,0:T(8,128)(2,1)S(1)}, u32[]{:S(2)}, u32[]{:S(2)}) collective-permute-start(bf16[592,128]{1,0:T(8,128)(2,1)S(1)} %get-tuple-element.64), channel_id=1, source_target_pairs={{0,8},{4,12},{8,0},{12,4},{1,9},{5,13},{9,1},{13,5},{2,10},{6,14},... | collective-permute-start | bytes 454664 | tf_op jit(solution)/shard_map/ppermute | solution.py:214
  13.3 23.1 %collective-permute-start.5 = (bf16[592,128]{1,0:T(8,128)(2,1)S(1)}, bf16[592,128]{1,0:T(8,128)(2,1)S(1)}, u32[]{:S(2)}, u32[]{:S(2)}) collective-permute-start(bf16[592,128]{1,0:T(8,128)(2,1)S(1)} %get-tuple-element.65), channel_id=1, source_target_pairs={{0,12},{4,0},{8,4},{12,8},{1,13},{5,1},{9,5},{13,9},{2,14},{6,2},{... | collective-permute-start | bytes 454664 | tf_op jit(solution)/shard_map/ppermute | solution.py:214
  25.8 19.5 %collective-permute-start.6 = (bf16[384,128]{1,0:T(8,128)(2,1)S(1)}, bf16[384,128]{1,0:T(8,128)(2,1)S(1)}, u32[]{:S(2)}, u32[]{:S(2)}) collective-permute-start(bf16[384,128]{1,0:T(8,128)(2,1)S(1)} %get-tuple-element.71), channel_id=1, source_target_pairs={{0,4},{4,8},{8,12},{12,0},{1,5},{5,9},{9,13},{13,1},{2,6},{6,10},{... | collective-permute-start | bytes 294920 | tf_op jit(solution)/shard_map/ppermute | solution.py:214
  34.0 12.1 %collective-permute-start.7 = (bf16[384,128]{1,0:T(8,128)(2,1)S(1)}, bf16[384,128]{1,0:T(8,128)(2,1)S(1)}, u32[]{:S(2)}, u32[]{:S(2)}) collective-permute-start(bf16[384,128]{1,0:T(8,128)(2,1)S(1)} %get-tuple-element.72), channel_id=1, source_target_pairs={{0,8},{4,12},{8,0},{12,4},{1,9},{5,13},{9,1},{13,5},{2,10},{6,14},... | collective-permute-start | bytes 294920 | tf_op jit(solution)/shard_map/ppermute | solution.py:214
  35.8 11.9 %collective-permute-start.8 = (bf16[384,128]{1,0:T(8,128)(2,1)S(1)}, bf16[384,128]{1,0:T(8,128)(2,1)S(1)}, u32[]{:S(2)}, u32[]{:S(2)}) collective-permute-start(bf16[384,128]{1,0:T(8,128)(2,1)S(1)} %get-tuple-element.73), channel_id=1, source_target_pairs={{0,12},{4,0},{8,4},{12,8},{1,13},{5,1},{9,5},{13,9},{2,14},{6,2},{... | collective-permute-start | bytes 294920 | tf_op jit(solution)/shard_map/ppermute | solution.py:214
  40.2 1.2 %collective-permute-start.9 = (f32[8,128]{1,0:T(8,128)S(1)}, f32[8,128]{1,0:T(8,128)S(1)}, u32[]{:S(2)}, u32[]{:S(2)}) collective-permute-start(f32[8,128]{1,0:T(8,128)S(1)} %get-tuple-element.86), channel_id=1, source_target_pairs={{0,16},{16,0},{1,17},{17,1},{2,18},{18,2},{3,19},{19,3},{4,20},{20... | collective-permute-start | bytes 12296 | tf_op jit(solution)/shard_map/ppermute | solution.py:219
  41.4 6.8 %collective-permute-start.12 = (f32[8,128]{1,0:T(8,128)S(1)}, f32[8,128]{1,0:T(8,128)S(1)}, u32[]{:S(2)}, u32[]{:S(2)}) collective-permute-start(f32[8,128]{1,0:T(8,128)S(1)} %add.3.refs_0_), channel_id=1, source_target_pairs={{0,3},{1,2},{2,1},{3,0},{4,7},{5,6},{6,5},{7,4},{8,11},{9,10},{10,... | collective-permute-start | bytes 12296 | tf_op jit(solution)/shard_map/ppermute | solution.py:219
  43.6 8.8 %collective-permute-start.13 = (bf16[384,128]{1,0:T(8,128)(2,1)S(1)}, bf16[384,128]{1,0:T(8,128)(2,1)S(1)}, u32[]{:S(2)}, u32[]{:S(2)}) collective-permute-start(bf16[384,128]{1,0:T(8,128)(2,1)S(1)} %get-tuple-element.87), channel_id=1, source_target_pairs={{0,4},{4,8},{8,12},{12,0},{1,5},{5,9},{9,13},{13,1},{2,6},{6,10},{... | collective-permute-start | bytes 294920 | tf_op jit(solution)/shard_map/ppermute | solution.py:214
  45.3 8.9 %collective-permute-start.14 = (bf16[384,128]{1,0:T(8,128)(2,1)S(1)}, bf16[384,128]{1,0:T(8,128)(2,1)S(1)}, u32[]{:S(2)}, u32[]{:S(2)}) collective-permute-start(bf16[384,128]{1,0:T(8,128)(2,1)S(1)} %get-tuple-element.89), channel_id=1, source_target_pairs={{0,8},{4,12},{8,0},{12,4},{1,9},{5,13},{9,1},{13,5},{2,10},{6,14},... | collective-permute-start | bytes 294920 | tf_op jit(solution)/shard_map/ppermute | solution.py:214
  46.1 8.9 %collective-permute-start.15 = (bf16[384,128]{1,0:T(8,128)(2,1)S(1)}, bf16[384,128]{1,0:T(8,128)(2,1)S(1)}, u32[]{:S(2)}, u32[]{:S(2)}) collective-permute-start(bf16[384,128]{1,0:T(8,128)(2,1)S(1)} %get-tuple-element.91), channel_id=1, source_target_pairs={{0,12},{4,0},{8,4},{12,8},{1,13},{5,1},{9,5},{13,9},{2,14},{6,2},{... | collective-permute-start | bytes 294920 | tf_op jit(solution)/shard_map/ppermute | solution.py:214
  47.8 4.6 %collective-permute-start.11 = (f32[8,128]{1,0:T(8,128)S(1)}, f32[8,128]{1,0:T(8,128)S(1)}, u32[]{:S(2)}, u32[]{:S(2)}) collective-permute-start(f32[8,128]{1,0:T(8,128)S(1)} %add.3.refs_0_), channel_id=1, source_target_pairs={{0,2},{1,3},{2,0},{3,1},{4,6},{5,7},{6,4},{7,5},{8,10},{9,11},{10,... | collective-permute-start | bytes 12296 | tf_op jit(solution)/shard_map/ppermute | solution.py:219
  48.3 4.1 %collective-permute-start.10 = (f32[8,128]{1,0:T(8,128)S(1)}, f32[8,128]{1,0:T(8,128)S(1)}, u32[]{:S(2)}, u32[]{:S(2)}) collective-permute-start(f32[8,128]{1,0:T(8,128)S(1)} %add.3.refs_0_), channel_id=1, source_target_pairs={{0,1},{1,0},{2,3},{3,2},{4,5},{5,4},{6,7},{7,6},{8,9},{9,8},{10,11... | collective-permute-start | bytes 12296 | tf_op jit(solution)/shard_map/ppermute | solution.py:219
  52.4 6.3 %collective-permute-start.16 = (bf16[272,128]{1,0:T(8,128)(2,1)S(1)}, bf16[272,128]{1,0:T(8,128)(2,1)S(1)}, u32[]{:S(2)}, u32[]{:S(2)}) collective-permute-start(bf16[272,128]{1,0:T(8,128)(2,1)S(1)} %join.1.refs_0_), channel_id=1, source_target_pairs={{0,4},{4,8},{8,12},{12,0},{1,5},{5,9},{9,13},{13,1},{2,6},{6,10},{... | collective-permute-start | bytes 208904 | tf_op jit(solution)/shard_map/ppermute | solution.py:214
  54.3 6.7 %collective-permute-start.17 = (bf16[272,128]{1,0:T(8,128)(2,1)S(1)}, bf16[272,128]{1,0:T(8,128)(2,1)S(1)}, u32[]{:S(2)}, u32[]{:S(2)}) collective-permute-start(bf16[272,128]{1,0:T(8,128)(2,1)S(1)} %join.1.refs_0_), channel_id=1, source_target_pairs={{0,8},{4,12},{8,0},{12,4},{1,9},{5,13},{9,1},{13,5},{2,10},{6,14},... | collective-permute-start | bytes 208904 | tf_op jit(solution)/shard_map/ppermute | solution.py:214
  55.0 6.6 %collective-permute-start.18 = (bf16[272,128]{1,0:T(8,128)(2,1)S(1)}, bf16[272,128]{1,0:T(8,128)(2,1)S(1)}, u32[]{:S(2)}, u32[]{:S(2)}) collective-permute-start(bf16[272,128]{1,0:T(8,128)(2,1)S(1)} %join.1.refs_0_), channel_id=1, source_target_pairs={{0,12},{4,0},{8,4},{12,8},{1,13},{5,1},{9,5},{13,9},{2,14},{6,2},{... | collective-permute-start | bytes 208904 | tf_op jit(solution)/shard_map/ppermute | solution.py:214

commit v4 on v3

--- a/solution.py
+++ b/solution.py
@@ -305,24 +305,24 @@
 def pack_rest_kernel(seq_count, per_place, parts, q_ref, k_ref, v_ref, doc_ref, map_ref, *rest):
     outs, (own_map, wide) = rest[: len(parts)], rest[len(parts) :]
     for n, ref in enumerate((q_ref, k_ref, v_ref)):
-        wide[n] = ref[...].astype(jnp.float32)
+        wide[n, : ref.shape[0], :] = ref[...].astype(jnp.float32)
     deal(wide, doc_ref[...], parts, outs, seq_count, per_place)
     for chunk in range(per_place):
         own_map[chunk] = map_ref[lax.axis_index("seq") * per_place + chunk]
 
 
-def half_sums(array, ones_block):
+def two_parts(array, axis):
     high = array.astype(jnp.bfloat16)
     low = (array - high.astype(jnp.float32)).astype(jnp.bfloat16)
-    return dot_nn(high, ones_block) + dot_nn(low, ones_block)
+    return jnp.concatenate([high, low], axis=axis)
+
+
+def half_sums(array, ones_block):
+    return dot_nn(two_parts(array, 1), ones_block)
 
 
 def signed_features(inputs, weights, ones_block, left):
-    first = weights.astype(jnp.bfloat16)
-    left_over = weights - first.astype(jnp.float32)
-    second = left_over.astype(jnp.bfloat16)
-    third = (left_over - second.astype(jnp.float32)).astype(jnp.bfloat16)
-    logits = dot_nn(inputs, first) + dot_nn(inputs, second) + dot_nn(inputs, third)
+    logits = dot_nn(jnp.concatenate([inputs, inputs], axis=1), two_parts(weights, 0))
     left_most = jnp.max(jnp.where(left, logits, -jnp.inf), axis=1, keepdims=True)
     right_most = jnp.max(jnp.where(left, -jnp.inf, logits), axis=1, keepdims=True)
     raised = jnp.exp2((logits - jnp.where(left, left_most, right_most)) * LOG2E)
@@ -330,8 +330,8 @@
 
 
 def ones_halves():
-    row = lax.broadcasted_iota(jnp.int32, (LANES, LANES), 0) < LANES // 2
-    col = lax.broadcasted_iota(jnp.int32, (LANES, LANES), 1) < LANES // 2
+    row = lax.broadcasted_iota(jnp.int32, (2 * LANES, LANES), 0) % LANES < LANES // 2
+    col = lax.broadcasted_iota(jnp.int32, (2 * LANES, LANES), 1) < LANES // 2
     return (row == col).astype(jnp.bfloat16)
 
 
@@ -425,9 +425,9 @@
     loss_ref[...] = earlier_ref[...] + jnp.sum(loss) * normaliser
 
 
-def backward_kernel(per_place, *refs):
-    saved, grad_ref = refs[: 4 * per_place], refs[4 * per_place]
-    v_s, qb_s, kb_s, dq_s, dk_s = refs[4 * per_place + 1 :]
+def backward_kernel(qkv_ref, feat_ref, slope_ref, bound_ref, *refs):
+    *blocks, v_s, qb_s, kb_s, dq_s, dk_s = refs
+    results, outs = blocks[: len(blocks) // 2], blocks[len(blocks) // 2 :]
     total = v_s.shape[0]
     left = lax.broadcasted_iota(jnp.int32, (1, LANES), 1) < LANES // 2
     ones_block = ones_halves()
@@ -436,31 +436,33 @@
         product = feat * slope
         return (product - feat * half_sums(product, ones_block)).astype(jnp.bfloat16)
 
-    for chunk in range(per_place):
-        qkv_ref, feat_ref, slope_ref, bound_ref = saved[4 * chunk : 4 * chunk + 4]
-        bounds = bound_ref[...]
-        v_s[:, :LANES] = qkv_ref[2]
-        v_s[:, LANES:] = jnp.ones((total, LANES), jnp.bfloat16)
-        qb_s[...] = feat_ref[0].astype(jnp.bfloat16)
-        kb_s[...] = feat_ref[1].astype(jnp.bfloat16)
-        dk_s[...] = jnp.zeros_like(dk_s)
-        for first in range(0, total, BLOCK):
-            last = first + BLOCK
-            row, start = block_places(first, bounds)
-            col = lax.broadcasted_iota(jnp.int32, (BLOCK, last), 1)
-            far = (col <= row - WINDOW) & (col >= start)
-            slope_weight = jnp.where(
-                far, dot_nt(slope_ref[first:last, :], v_s[:last, :]), 0.0
-            ).astype(jnp.bfloat16)
-            dq_s[first:last, :] = dot_nn(slope_weight, kb_s[:last, :])
-            dk_s[:last, :] += dot_tn(slope_weight, qb_s[first:last, :])
-        from_q = dot_tn(qkv_ref[0], logits_slope(feat_ref[0], dq_s[...]))
-        from_k = dot_tn(qkv_ref[1], logits_slope(feat_ref[1], dk_s[...]))
-        grad_ref[chunk * LANES : (chunk + 1) * LANES, :] = jnp.where(
-            left,
-            from_q - pltpu.roll(from_q, LANES // 2, 1),
-            pltpu.roll(from_k, LANES // 2, 1) - from_k,
+    bounds = bound_ref[...]
+    v_s[:, :LANES] = qkv_ref[2]
+    v_s[:, LANES:] = jnp.ones((total, LANES), jnp.bfloat16)
+    qb_s[...] = feat_ref[0].astype(jnp.bfloat16)
+    kb_s[...] = feat_ref[1].astype(jnp.bfloat16)
+    dk_s[...] = jnp.zeros_like(dk_s)
+    for first in range(0, total, BLOCK):
+        last = first + BLOCK
+        row, start = block_places(first, bounds)
+        col = lax.broadcasted_iota(jnp.int32, (BLOCK, last), 1)
+        far = (col <= row - WINDOW) & (col >= start)
+        slope_weight = jnp.where(
+            far, dot_nt(slope_ref[first:last, :], v_s[:last, :]), 0.0
         ).astype(jnp.bfloat16)
+        dq_s[first:last, :] = dot_nn(slope_weight, kb_s[:last, :])
+        dk_s[:last, :] += dot_tn(slope_weight, qb_s[first:last, :])
+    from_q = dot_tn(qkv_ref[0], logits_slope(feat_ref[0], dq_s[...]))
+    from_k = dot_tn(qkv_ref[1], logits_slope(feat_ref[1], dk_s[...]))
+    grad = jnp.where(
+        left,
+        from_q - pltpu.roll(from_q, LANES // 2, 1),
+        pltpu.roll(from_k, LANES // 2, 1) - from_k,
+    ).astype(jnp.bfloat16)
+    for out in outs:
+        out[out.shape[0] - LANES :, :] = grad
+    for result, out in zip(results, outs):
+        out[: result.shape[0], :] = result[...]
 
 
 def unpack_kernel(seq_count, per_place, *refs):
@@ -476,35 +478,37 @@
             s_wide[pl.ds(head, rows, stride=heads), :] = piece[rows : 2 * rows, :].astype(
                 jnp.float32
             )
-    t_ref[...] = t_wide[...].astype(jnp.bfloat16)
-    s_ref[...] = s_wide[...].astype(jnp.bfloat16)
+    t_ref[...] = t_wide[: rows * heads, :].astype(jnp.bfloat16)
+    s_ref[...] = s_wide[: rows * heads, :].astype(jnp.bfloat16)
 
 
 def join_kernel(grad_ref, *refs):
     losses, out = refs[:-1], refs[-1]
-    size = grad_ref.shape[0]
     loss = losses[0][...]
     if len(losses) == 4:
         loss = (loss + losses[2][...]) + (losses[1][...] + losses[3][...])
-    out[:size, :] = grad_ref[...]
+    out[:LANES, :] = grad_ref[...]
     row = lax.broadcasted_iota(jnp.int32, (8, LANES), 0)
     high = loss.astype(jnp.bfloat16).astype(jnp.float32)
     middle = (loss - high).astype(jnp.bfloat16).astype(jnp.float32)
     low = (loss - high) - middle
     parts = jnp.where(row == 0, high, jnp.where(row == 1, middle, jnp.where(row == 2, low, 0.0)))
-    out[size:, :] = jnp.concatenate([parts, parts], axis=0).astype(jnp.bfloat16)
+    out[LANES:, :] = jnp.concatenate([parts, parts], axis=0).astype(jnp.bfloat16)
 
 
 def final_kernel(seq_count, per_place, *refs):
-    pieces = refs[:seq_count]
-    grad_ref, loss_ref, parts_s = refs[seq_count:]
-    for shift, piece in enumerate(pieces):
+    pieces = refs[: seq_count * per_place]
+    grad_ref, loss_ref, parts_s = refs[seq_count * per_place :]
+    for shift in range(seq_count):
         source = place_of(shift, seq_count)
-        for chunk in range(per_place):
+        for chunk in range(per_place - 1):
+            piece = pieces[chunk * seq_count + shift]
             grad_ref[source * per_place + chunk] = piece[
-                chunk * LANES : (chunk + 1) * LANES, :
+                piece.shape[0] - LANES :, :
             ].astype(jnp.float32)
-        tail = piece[per_place * LANES :, :].astype(jnp.float32)
+        piece = pieces[(per_place - 1) * seq_count + shift]
+        grad_ref[source * per_place + per_place - 1] = piece[:LANES, :].astype(jnp.float32)
+        tail = piece[LANES:, :].astype(jnp.float32)
         parts_s[source] = tail[0:1, :] + tail[1:2, :] + tail[2:3, :]
     loss = parts_s[0]
     for source in range(1, seq_count):
@@ -552,7 +556,7 @@
     later_parts = [(0, 0)] + [
         (chunk, shift) for chunk in range(1, per_place) for shift in range(seq_count)
     ]
-    wide = pltpu.VMEM((3, tok_rows * head_count, LANES), f32)
+    wide = pltpu.VMEM((3, (tok_rows + 1) * head_count, LANES), f32)
     first_packed = kernel_call(
         functools.partial(pack_kernel, seq_count, per_place, first_parts),
         sizes(*[sent_rows] * len(first_parts)),
@@ -581,7 +585,7 @@
     for chunk in range(1, per_place):
         held.append(sent(packed[1 + (chunk - 1) * seq_count : 1 + chunk * seq_count]))
 
-    returned, saved = [], []
+    returned = []
     loss = jnp.zeros((8, LANES), f32)
     for chunk in range(per_place):
         results = kernel_call(
@@ -605,25 +609,34 @@
             16 * total * LANES,
             "forward",
         )(*held[chunk], own_map, loss)
-        loss = results[seq_count]
-        saved.append(results[seq_count + 1 :])
-        returned.append(sent(results[:seq_count]))
-
-    saved, returned[0] = after(saved, returned[0])
-    grad = kernel_call(
-        functools.partial(backward_kernel, per_place),
-        sizes(per_place * LANES)[0],
-        [
-            pltpu.VMEM((total, 2 * LANES), bf16),
-            pltpu.VMEM((total, LANES), bf16),
-            pltpu.VMEM((total, LANES), bf16),
-            pltpu.VMEM((total, LANES), f32),
-            pltpu.VMEM((total, LANES), f32),
-        ],
-        HEAD_COST,
-        16 * total * LANES,
-        "backward",
-    )(*[part for parts in saved for part in parts])
+        loss, *saved = results[seq_count:]
+        blocks = results[:seq_count]
+        if chunk:
+            saved, returned[chunk - 1] = after(saved, returned[chunk - 1])
+        if chunk + 1 < per_place:
+            given, rows = blocks, [2 * tok_rows + LANES] * seq_count
+        else:
+            returned.append(sent(blocks))
+            given, rows = [], [LANES]
+        grad = kernel_call(
+            backward_kernel,
+            sizes(*rows),
+            [
+                pltpu.VMEM((total, 2 * LANES), bf16),
+                pltpu.VMEM((total, LANES), bf16),
+                pltpu.VMEM((total, LANES), bf16),
+                pltpu.VMEM((total, LANES), f32),
+                pltpu.VMEM((total, LANES), f32),
+            ],
+            HEAD_COST,
+            16 * total * LANES,
+            "backward",
+        )(*saved, *given)
+        if chunk + 1 < per_place:
+            grad, own_map = lax.optimization_barrier((grad, own_map))
+            returned.append(sent(grad))
+
+
     loss = summed_over(loss, "grp")
     if lax.axis_size("head") == 4:
         losses = [loss] + [crossed(loss, "head", mask) for mask in range(1, 4)]
@@ -631,23 +644,23 @@
         losses = [summed_over(loss, "head")]
     joined = kernel_call(
         join_kernel,
-        sizes(per_place * LANES + META_ROWS)[0],
+        sizes(LANES + META_ROWS)[0],
         [],
         0,
         16 * LANES * LANES,
         "join",
-    )(grad, *losses)
+    )(*grad, *losses)
     last = [joined]
     for shift in range(1, seq_count):
-        behind = [pieces[shift] for pieces in returned[1:]]
+        behind = [pieces[shift] for pieces in returned[-1:]]
         block, behind = lax.optimization_barrier((joined, behind))
-        for pieces, piece in zip(returned[1:], behind):
+        for pieces, piece in zip(returned[-1:], behind):
             pieces[shift] = piece
         last.append(turned(block, "seq", shift))
     teacher_out, student_out = kernel_call(
         functools.partial(unpack_kernel, seq_count, per_place),
         sizes(*[tok_rows * head_count] * 2),
-        [pltpu.VMEM((tok_rows * head_count, LANES), f32)] * 2,
+        [pltpu.VMEM(((tok_rows + 1) * head_count, LANES), f32)] * 2,
         0,
         12 * tok_rows * head_count * LANES,
         "unpack",
@@ -659,7 +672,7 @@
         0,
         8 * head_count * LANES * LANES,
         "final",
-    )(*last)
+    )(*[piece for pieces in returned[:-1] for piece in pieces], *last)
     return (
         teacher_out.reshape(queries.shape),
         student_out.reshape(queries.shape),

time: 62.6 us -> 62.6 us (level)
  starting transfers between devices: 32.3 us -> 36.7 us
  waiting for transfers between devices: 12.2 us -> 9.33 us
  Pallas kernels: 16.1 us -> 14.5 us
    ppermute x4, starting transfers between devices: 3.27 us -> 6.66 us  [crossed(): return lax.ppermute(block, axis, [(i, i ^ mask) for i in range(count)])]
    ppermute x15, waiting for transfers between devices: 11.1 us -> 8.17 us  [turned(): lax.ppermute(block, axis, [(i, (i + distance) % count) for i in range(cou...]
    pallas_call x2, Pallas kernels: 7.47 us -> 5.89 us  [split_body(): kernel_call(functools.partial(forward_kernel, seq_count, chunk, score_sca...]
    ppermute x15, starting transfers between devices: 29 us -> 30.1 us  [turned(): lax.ppermute(block, axis, [(i, (i + distance) % count) for i in range(cou...]
    pallas_call x2 -> x3, Pallas kernels: 3.52 us -> 3.55 us  [the longest x2 3.53 us: split_body(): kernel_call(backward_kernel, sizes(*rows), [pltpu.VMEM((total, 2 * LANES)...]
  transfers between devices with their start and end apart: 19 -> 19, of which waited for: 8 -> 6; matrix products, arithmetic and copies ran while one was open for 0% -> 0% of each run, Pallas kernels for 20% -> 18%
where the time goes in v4:
time: 62.6 us; the launch traced here: 62.4 us
  starting transfers between devices  36.7 us (59%)
  Pallas kernels  14.5 us (23%)
  waiting for transfers between devices  9.33 us (15%)
  local copies, waits for them, and re-layouts  1.05 us (2%)
  between operations  0.78 us (1%)
    ppermute x15, starting transfers between devices, turned(): lax.ppermute(block, axis, [(i, (i + distance) % count) for i in range(cou...  30.1 us
    ppermute x15, waiting for transfers between devices, turned(): lax.ppermute(block, axis, [(i, (i + distance) % count) for i in range(cou...  8.17 us
    ppermute x4, starting transfers between devices, crossed(): return lax.ppermute(block, axis, [(i, i ^ mask) for i in range(count)])  6.66 us
    pallas_call x2, Pallas kernels, split_body(): kernel_call(functools.partial(forward_kernel, seq_count, chunk, score_sca...  5.89 us
    pallas_call x2, Pallas kernels, split_body(): kernel_call(backward_kernel, sizes(*rows), [pltpu.VMEM((total, 2 * LANES)...  3.53 us
    pallas_call x1, Pallas kernels, split_body(): kernel_call(functools.partial(pack_kernel, seq_count, per_place, first_pa...  2.49 us
  transfers between devices with their start and end apart: 19, of which 6 were waited for; matrix products, arithmetic and copies ran while one was open for 0% of the time, Pallas kernels for 18%

profile of v4, /device:TPU:0, one launch (start us, length us, event | category | flops | bytes accessed | tf_op | source)
XLA Modules:
  0.0 62.4 jit_solution(9792215821750052901)
XLA Ops:
  0.7 2.5 %pack.1 = (bf16[592,128]{1,0:T(8,128)(2,1)}, bf16[592,128]{1,0:T(8,128)(2,1)}, bf16[592,128]{1,0:T(8,128)(2,1)}) custom-call(bf16[1536,128]{1,0:T(8,128)(2,1)} %bitcast.8, bf16[1536,128]{1,0:T(8,128)(2,1)} %bitcast.10, bf16[1536,128]{1,0:T(8,128)(2,1)} %bitcast.12, s32[1,192]{1,0:T(1,128)} %bitcast.14), custom_call_target="tpu_custom_call" | custom-call | bytes 2359296 | tf_op jit(solution)/shard_map/pack/pallas_call | solution.py:560
  3.2 3.1 %collective-permute-start = (bf16[592,128]{1,0:T(8,128)(2,1)}, bf16[592,128]{1,0:T(8,128)(2,1)S(1)}, u32[]{:S(2)}, u32[]{:S(2)}) collective-permute-start(bf16[592,128]{1,0:T(8,128)(2,1)} %get-tuple-element.58), channel_id=1, source_target_pairs={{0,4},{4,8},{8,12},{12,0},{1,5},{5,9},{9,13},{13,1},{2,6},{6,10},{... | collective-permute-start | bytes 454664 | tf_op jit(solution)/shard_map/ppermute | solution.py:214
  6.2 2.6 %collective-permute-start.1 = (bf16[592,128]{1,0:T(8,128)(2,1)}, bf16[592,128]{1,0:T(8,128)(2,1)S(1)}, u32[]{:S(2)}, u32[]{:S(2)}) collective-permute-start(bf16[592,128]{1,0:T(8,128)(2,1)} %get-tuple-element.59), channel_id=1, source_target_pairs={{0,8},{4,12},{8,0},{12,4},{1,9},{5,13},{9,1},{13,5},{2,10},{6,14},... | collective-permute-start | bytes 454664 | tf_op jit(solution)/shard_map/ppermute | solution.py:214
  8.8 1.3 %collective-permute-start.2 = (bf16[592,128]{1,0:T(8,128)(2,1)}, bf16[592,128]{1,0:T(8,128)(2,1)S(1)}, u32[]{:S(2)}, u32[]{:S(2)}) collective-permute-start(bf16[592,128]{1,0:T(8,128)(2,1)} %get-tuple-element.60), channel_id=1, source_target_pairs={{0,12},{4,0},{8,4},{12,8},{1,13},{5,1},{9,5},{13,9},{2,14},{6,2},{... | collective-permute-start | bytes 454664 | tf_op jit(solution)/shard_map/ppermute | solution.py:214
  10.2 1.0 %copy-done.3 = f32[8,128,128]{2,1,0:T(8,128)S(1)} copy-done((f32[8,128,128]{2,1,0:T(8,128)S(1)}, f32[8,128,128]{2,1,0:T(8,128)}, u32[]{:S(2)}) %copy-start.3) | copy-done | bytes 524312
  11.2 0.5 pack_rest.1
  11.8 0.7 %collective-permute-start.3 = (bf16[592,128]{1,0:T(8,128)(2,1)S(1)}, bf16[592,128]{1,0:T(8,128)(2,1)S(1)}, u32[]{:S(2)}, u32[]{:S(2)}) collective-permute-start(bf16[592,128]{1,0:T(8,128)(2,1)S(1)} %get-tuple-element.76), channel_id=1, source_target_pairs={{0,4},{4,8},{8,12},{12,0},{1,5},{5,9},{9,13},{13,1},{2,6},{6,10},{... | collective-permute-start | bytes 454664 | tf_op jit(solution)/shard_map/ppermute | solution.py:214
  12.5 0.3 collective-permute-start.4
  12.8 0.5 collective-permute-done.refs_1_
  13.3 2.3 %collective-permute-start.5 = (bf16[592,128]{1,0:T(8,128)(2,1)S(1)}, bf16[592,128]{1,0:T(8,128)(2,1)S(1)}, u32[]{:S(2)}, u32[]{:S(2)}) collective-permute-start(bf16[592,128]{1,0:T(8,128)(2,1)S(1)} %get-tuple-element.78), channel_id=1, source_target_pairs={{0,12},{4,0},{8,4},{12,8},{1,13},{5,1},{9,5},{13,9},{2,14},{6,2},{... | collective-permute-start | bytes 454664 | tf_op jit(solution)/shard_map/ppermute | solution.py:214
  15.7 4.2 %collective-permute-done.1.refs_2_ = bf16[592,128]{1,0:T(8,128)(2,1)S(1)} collective-permute-done((bf16[592,128]{1,0:T(8,128)(2,1)}, bf16[592,128]{1,0:T(8,128)(2,1)S(1)}, u32[]{:S(2)}, u32[]{:S(2)}) %collective-permute-start.1) | collective-permute-done | bytes 151584 | tf_op jit(solution)/shard_map/ppermute | solution.py:214
  19.9 2.2 %collective-permute-done.2.refs_3_ = bf16[592,128]{1,0:T(8,128)(2,1)S(1)} collective-permute-done((bf16[592,128]{1,0:T(8,128)(2,1)}, bf16[592,128]{1,0:T(8,128)(2,1)S(1)}, u32[]{:S(2)}, u32[]{:S(2)}) %collective-permute-start.2) | collective-permute-done | bytes 151584 | tf_op jit(solution)/shard_map/ppermute | solution.py:214
  22.1 2.9 %forward.2 = (bf16[384,128]{1,0:T(8,128)(2,1)S(1)}, bf16[384,128]{1,0:T(8,128)(2,1)S(1)}, bf16[384,128]{1,0:T(8,128)(2,1)S(1)}, bf16[384,128]{1,0:T(8,128)(2,1)S...) custom-call(bf16[592,128]{1,0:T(8,128)(2,1)S(1)} %get-tuple-element., ...), custom_call_target="tpu_custom_call" | custom-call | flops 6000000000 | bytes 1572864 | tf_op jit(solution)/shard_map/forward/pallas_call | solution.py:591
  25.0 1.8 %backward.2 = (bf16[512,128]{1,0:T(8,128)(2,1)S(1)}, bf16[512,128]{1,0:T(8,128)(2,1)S(1)}, bf16[512,128]{1,0:T(8,128)(2,1)S(1)}, bf16[512,128]{1,0:T(8,128)(2,1)S(1)}) custom-call(bf16[3,768,128]{2,1,0:T(8,128)(2,1)S(1)} %get-tuple-element.62.qkv_ref, f32[2,768,128]{2,1,0:T(8,128)S(1)} %get-tuple-element.63.feat_ref, ...), custom_call_target="tpu_custom_call" | custom-call | flops 6000000000 | bytes 1572864 | tf_op jit(solution)/shard_map/backward/pallas_call | solution.py:621
  26.8 7.3 %collective-permute-start.6 = (bf16[512,128]{1,0:T(8,128)(2,1)S(1)}, bf16[512,128]{1,0:T(8,128)(2,1)S(1)}, u32[]{:S(2)}, u32[]{:S(2)}) collective-permute-start(bf16[512,128]{1,0:T(8,128)(2,1)S(1)} %get-tuple-element.85), channel_id=1, source_target_pairs={{0,4},{4,8},{8,12},{12,0},{1,5},{5,9},{9,13},{13,1},{2,6},{6,10},{... | collective-permute-start | bytes 393224 | tf_op jit(solution)/shard_map/ppermute | solution.py:214
  34.1 2.7 %collective-permute-start.7 = (bf16[512,128]{1,0:T(8,128)(2,1)S(1)}, bf16[512,128]{1,0:T(8,128)(2,1)S(1)}, u32[]{:S(2)}, u32[]{:S(2)}) collective-permute-start(bf16[512,128]{1,0:T(8,128)(2,1)S(1)} %get-tuple-element.86), channel_id=1, source_target_pairs={{0,8},{4,12},{8,0},{12,4},{1,9},{5,13},{9,1},{13,5},{2,10},{6,14},... | collective-permute-start | bytes 393224 | tf_op jit(solution)/shard_map/ppermute | solution.py:214
  36.9 2.9 %forward.3 = (bf16[384,128]{1,0:T(8,128)(2,1)S(1)}, bf16[384,128]{1,0:T(8,128)(2,1)S(1)}, bf16[384,128]{1,0:T(8,128)(2,1)S(1)}, bf16[384,128]{1,0:T(8,128)(2,1)S...) custom-call(bf16[592,128]{1,0:T(8,128)(2,1)S(1)} %get-tuple-element., ...), custom_call_target="tpu_custom_call" | custom-call | flops 6000000000 | bytes 1572864 | tf_op jit(solution)/shard_map/forward/pallas_call | solution.py:591
  39.8 0.1 collective-permute-start.9
  39.9 1.2 %collective-permute-done.9 = f32[8,128]{1,0:T(8,128)S(1)} collective-permute-done((f32[8,128]{1,0:T(8,128)S(1)}, f32[8,128]{1,0:T(8,128)S(1)}, u32[]{:S(2)}, u32[]{:S(2)}) %collective-permute-start.9) | collective-permute-done | bytes 4128 | tf_op jit(solution)/shard_map/ppermute | solution.py:219
  41.1 2.4 %collective-permute-start.12 = (f32[8,128]{1,0:T(8,128)S(1)}, f32[8,128]{1,0:T(8,128)S(1)}, u32[]{:S(2)}, u32[]{:S(2)}) collective-permute-start(f32[8,128]{1,0:T(8,128)S(1)} %add.3.refs_0_), channel_id=1, source_target_pairs={{0,3},{1,2},{2,1},{3,0},{4,7},{5,6},{6,5},{7,4},{8,11},{9,10},{10,... | collective-permute-start | bytes 12296 | tf_op jit(solution)/shard_map/ppermute | solution.py:219
  43.5 2.0 %collective-permute-start.13 = (bf16[384,128]{1,0:T(8,128)(2,1)S(1)}, bf16[384,128]{1,0:T(8,128)(2,1)S(1)}, u32[]{:S(2)}, u32[]{:S(2)}) collective-permute-start(bf16[384,128]{1,0:T(8,128)(2,1)S(1)} %get-tuple-element.97), channel_id=1, source_target_pairs={{0,4},{4,8},{8,12},{12,0},{1,5},{5,9},{9,13},{13,1},{2,6},{6,10},{... | collective-permute-start | bytes 294920 | tf_op jit(solution)/shard_map/ppermute | solution.py:214
  45.5 0.2 collective-permute-start.14
  45.8 2.8 %collective-permute-start.15 = (bf16[384,128]{1,0:T(8,128)(2,1)S(1)}, bf16[384,128]{1,0:T(8,128)(2,1)S(1)}, u32[]{:S(2)}, u32[]{:S(2)}) collective-permute-start(bf16[384,128]{1,0:T(8,128)(2,1)S(1)} %get-tuple-element.101), channel_id=1, source_target_pairs={{0,12},{4,0},{8,4},{12,8},{1,13},{5,1},{9,5},{13,9},{2,14},{6,2},{... | collective-permute-start | bytes 294920 | tf_op jit(solution)/shard_map/ppermute | solution.py:214
  48.6 2.2 %collective-permute-start.11 = (f32[8,128]{1,0:T(8,128)S(1)}, f32[8,128]{1,0:T(8,128)S(1)}, u32[]{:S(2)}, u32[]{:S(2)}) collective-permute-start(f32[8,128]{1,0:T(8,128)S(1)} %add.3.refs_0_), channel_id=1, source_target_pairs={{0,2},{1,3},{2,0},{3,1},{4,6},{5,7},{6,4},{7,5},{8,10},{9,11},{10,... | collective-permute-start | bytes 12296 | tf_op jit(solution)/shard_map/ppermute | solution.py:219
  50.8 2.0 %collective-permute-start.10 = (f32[8,128]{1,0:T(8,128)S(1)}, f32[8,128]{1,0:T(8,128)S(1)}, u32[]{:S(2)}, u32[]{:S(2)}) collective-permute-start(f32[8,128]{1,0:T(8,128)S(1)} %add.3.refs_0_), channel_id=1, source_target_pairs={{0,1},{1,0},{2,3},{3,2},{4,5},{5,4},{6,7},{7,6},{8,9},{9,8},{10,11... | collective-permute-start | bytes 12296 | tf_op jit(solution)/shard_map/ppermute | solution.py:219
  52.8 1.8 %backward.3.grad_ref = bf16[128,128]{1,0:T(8,128)(2,1)S(1)} custom-call(bf16[3,768,128]{2,1,0:T(8,128)(2,1)S(1)} %get-tuple-element.92.qkv_ref, f32[2,768,128]{2,1,0:T(8,128)S(1)} %get-tuple-element.93.feat_ref, bf16[768,256]{1,0:T(8,128)(2,1)S(1)} %get-tuple-element.94.slope_ref, s32[16,128]{1,0:T(8,128)S(1)} %get-tuple-element.95.bound_ref), custom_call_target="tpu_custom_call" | custom-call | flops 6000000000 | bytes 1572864 | tf_op jit(solution)/shard_map/backward/pallas_call | solution.py:621
  54.6 2.1 %collective-permute-start.16 = (bf16[144,128]{1,0:T(8,128)(2,1)S(1)}, bf16[144,128]{1,0:T(8,128)(2,1)S(1)}, u32[]{:S(2)}, u32[]{:S(2)}) collective-permute-start(bf16[144,128]{1,0:T(8,128)(2,1)S(1)} %join.1.refs_4_), channel_id=1, source_target_pairs={{0,4},{4,8},{8,12},{12,0},{1,5},{5,9},{9,13},{13,1},{2,6},{6,10},{... | collective-permute-start | bytes 110600 | tf_op jit(solution)/shard_map/ppermute | solution.py:214
  56.7 2.4 %collective-permute-start.18 = (bf16[144,128]{1,0:T(8,128)(2,1)S(1)}, bf16[144,128]{1,0:T(8,128)(2,1)S(1)}, u32[]{:S(2)}, u32[]{:S(2)}) collective-permute-start(bf16[144,128]{1,0:T(8,128)(2,1)S(1)} %join.1.refs_4_), channel_id=1, source_target_pairs={{0,12},{4,0},{8,4},{12,8},{1,13},{5,1},{9,5},{13,9},{2,14},{6,2},{... | collective-permute-start | bytes 110600 | tf_op jit(solution)/shard_map/ppermute | solution.py:214
  59.1 1.2 %unpack.1 = (bf16[1536,128]{1,0:T(8,128)(2,1)}, bf16[1536,128]{1,0:T(8,128)(2,1)}) custom-call(bf16[512,128]{1,0:T(8,128)(2,1)S(1)} %get-tuple-element.74.refs_0_, bf16[512,128]{1,0:T(8,128)(2,1)S(1)} %collective-permute-done.6.refs_1_, bf16[512,128]{1,0:T(8,128)(2,1)S(1)} %collective-permute-done.7.refs_2_, ...), custom_call_target="tpu_custom_call" | custom-call | bytes 2359296 | tf_op jit(solution)/shard_map/unpack/pallas_call | solution.py:660
  60.3 0.2 collective-permute-done.16.refs_5_
  60.5 1.0 %collective-permute-done.17.refs_6_ = bf16[144,128]{1,0:T(8,128)(2,1)S(1)} collective-permute-done((bf16[144,128]{1,0:T(8,128)(2,1)S(1)}, bf16[144,128]{1,0:T(8,128)(2,1)S(1)}, u32[]{:S(2)}, u32[]{:S(2)}) %collective-permute-start.17) | collective-permute-done | bytes 36896 | tf_op jit(solution)/shard_map/ppermute | solution.py:214
  61.6 0.8 %final.1 = (f32[8,128,128]{2,1,0:T(8,128)}, f32[1,128]{1,0:T(1,128)}) custom-call(bf16[512,128]{1,0:T(8,128)(2,1)S(1)} %get-tuple-element.74.refs_0_, bf16[512,128]{1,0:T(8,128)(2,1)S(1)} %collective-permute-done.6.refs_1_, bf16[512,128]{1,0:T(8,128)(2,1)S(1)} %collective-permute-done.7.refs_2_, bf16[512,128]{1,0:T(8,128)(2,1)S(1)} %collective-permute-done.8.refs_3_, ...), custom_call_target="tpu_custom_call" | custom-call | bytes 1048576 | tf_op jit(solution)/shard_map/final/pallas_call | solution.py:668
  (27 shorter events, 0.1 us)
Async XLA Ops:
  0.6 9.6 %copy-start = (bf16[192,8,128]{2,1,0:T(8,128)(2,1)S(1)}, bf16[192,8,128]{2,1,0:T(8,128)(2,1)}, u32[]{:S(2)}) copy-start(bf16[192,8,128]{2,1,0:T(8,128)(2,1)} %param.5) | copy-start | bytes 1179652
  0.6 9.5 %copy-start.1 = (bf16[192,8,128]{2,1,0:T(8,128)(2,1)S(1)}, bf16[192,8,128]{2,1,0:T(8,128)(2,1)}, u32[]{:S(2)}) copy-start(bf16[192,8,128]{2,1,0:T(8,128)(2,1)} %param.6) | copy-start | bytes 1179652
  0.7 9.5 %copy-start.2 = (bf16[192,8,128]{2,1,0:T(8,128)(2,1)S(1)}, bf16[192,8,128]{2,1,0:T(8,128)(2,1)}, u32[]{:S(2)}) copy-start(bf16[192,8,128]{2,1,0:T(8,128)(2,1)} %param.7) | copy-start | bytes 1179652
  3.2 10.2 %collective-permute-start = (bf16[592,128]{1,0:T(8,128)(2,1)}, bf16[592,128]{1,0:T(8,128)(2,1)S(1)}, u32[]{:S(2)}, u32[]{:S(2)}) collective-permute-start(bf16[592,128]{1,0:T(8,128)(2,1)} %get-tuple-element.58), channel_id=1, source_target_pairs={{0,4},{4,8},{8,12},{12,0},{1,5},{5,9},{9,13},{13,1},{2,6},{6,10},{... | collective-permute-start | bytes 454664 | tf_op jit(solution)/shard_map/ppermute | solution.py:214
  6.2 4.0 %copy-start.4 = (s32[192]{0:T(256)S(1)}, s32[192]{0:T(256)}, u32[]{:S(2)}) copy-start(s32[192]{0:T(256)} %param.8) | copy-start | bytes 2308
  6.2 13.6 %collective-permute-start.1 = (bf16[592,128]{1,0:T(8,128)(2,1)}, bf16[592,128]{1,0:T(8,128)(2,1)S(1)}, u32[]{:S(2)}, u32[]{:S(2)}) collective-permute-start(bf16[592,128]{1,0:T(8,128)(2,1)} %get-tuple-element.59), channel_id=1, source_target_pairs={{0,8},{4,12},{8,0},{12,4},{1,9},{5,13},{9,1},{13,5},{2,10},{6,14},... | collective-permute-start | bytes 454664 | tf_op jit(solution)/shard_map/ppermute | solution.py:214
  8.8 13.2 %collective-permute-start.2 = (bf16[592,128]{1,0:T(8,128)(2,1)}, bf16[592,128]{1,0:T(8,128)(2,1)S(1)}, u32[]{:S(2)}, u32[]{:S(2)}) collective-permute-start(bf16[592,128]{1,0:T(8,128)(2,1)} %get-tuple-element.60), channel_id=1, source_target_pairs={{0,12},{4,0},{8,4},{12,8},{1,13},{5,1},{9,5},{13,9},{2,14},{6,2},{... | collective-permute-start | bytes 454664 | tf_op jit(solution)/shard_map/ppermute | solution.py:214
  10.2 1.0 %copy-start.3 = (f32[8,128,128]{2,1,0:T(8,128)S(1)}, f32[8,128,128]{2,1,0:T(8,128)}, u32[]{:S(2)}) copy-start(f32[8,128,128]{2,1,0:T(8,128)} %map_ref.1) | copy-start | bytes 1572868
  11.8 25.1 %collective-permute-start.3 = (bf16[592,128]{1,0:T(8,128)(2,1)S(1)}, bf16[592,128]{1,0:T(8,128)(2,1)S(1)}, u32[]{:S(2)}, u32[]{:S(2)}) collective-permute-start(bf16[592,128]{1,0:T(8,128)(2,1)S(1)} %get-tuple-element.76), channel_id=1, source_target_pairs={{0,4},{4,8},{8,12},{12,0},{1,5},{5,9},{9,13},{13,1},{2,6},{6,10},{... | collective-permute-start | bytes 454664 | tf_op jit(solution)/shard_map/ppermute | solution.py:214
  12.5 24.3 %collective-permute-start.4 = (bf16[592,128]{1,0:T(8,128)(2,1)S(1)}, bf16[592,128]{1,0:T(8,128)(2,1)S(1)}, u32[]{:S(2)}, u32[]{:S(2)}) collective-permute-start(bf16[592,128]{1,0:T(8,128)(2,1)S(1)} %get-tuple-element.77), channel_id=1, source_target_pairs={{0,8},{4,12},{8,0},{12,4},{1,9},{5,13},{9,1},{13,5},{2,10},{6,14},... | collective-permute-start | bytes 454664 | tf_op jit(solution)/shard_map/ppermute | solution.py:214
  13.3 23.5 %collective-permute-start.5 = (bf16[592,128]{1,0:T(8,128)(2,1)S(1)}, bf16[592,128]{1,0:T(8,128)(2,1)S(1)}, u32[]{:S(2)}, u32[]{:S(2)}) collective-permute-start(bf16[592,128]{1,0:T(8,128)(2,1)S(1)} %get-tuple-element.78), channel_id=1, source_target_pairs={{0,12},{4,0},{8,4},{12,8},{1,13},{5,1},{9,5},{13,9},{2,14},{6,2},{... | collective-permute-start | bytes 454664 | tf_op jit(solution)/shard_map/ppermute | solution.py:214
  26.8 18.7 %collective-permute-start.6 = (bf16[512,128]{1,0:T(8,128)(2,1)S(1)}, bf16[512,128]{1,0:T(8,128)(2,1)S(1)}, u32[]{:S(2)}, u32[]{:S(2)}) collective-permute-start(bf16[512,128]{1,0:T(8,128)(2,1)S(1)} %get-tuple-element.85), channel_id=1, source_target_pairs={{0,4},{4,8},{8,12},{12,0},{1,5},{5,9},{9,13},{13,1},{2,6},{6,10},{... | collective-permute-start | bytes 393224 | tf_op jit(solution)/shard_map/ppermute | solution.py:214
  34.1 11.6 %collective-permute-start.7 = (bf16[512,128]{1,0:T(8,128)(2,1)S(1)}, bf16[512,128]{1,0:T(8,128)(2,1)S(1)}, u32[]{:S(2)}, u32[]{:S(2)}) collective-permute-start(bf16[512,128]{1,0:T(8,128)(2,1)S(1)} %get-tuple-element.86), channel_id=1, source_target_pairs={{0,8},{4,12},{8,0},{12,4},{1,9},{5,13},{9,1},{13,5},{2,10},{6,14},... | collective-permute-start | bytes 393224 | tf_op jit(solution)/shard_map/ppermute | solution.py:214
  36.8 11.8 %collective-permute-start.8 = (bf16[512,128]{1,0:T(8,128)(2,1)S(1)}, bf16[512,128]{1,0:T(8,128)(2,1)S(1)}, u32[]{:S(2)}, u32[]{:S(2)}) collective-permute-start(bf16[512,128]{1,0:T(8,128)(2,1)S(1)} %get-tuple-element.87), channel_id=1, source_target_pairs={{0,12},{4,0},{8,4},{12,8},{1,13},{5,1},{9,5},{13,9},{2,14},{6,2},{... | collective-permute-start | bytes 393224 | tf_op jit(solution)/shard_map/ppermute | solution.py:214
  39.8 1.2 %collective-permute-start.9 = (f32[8,128]{1,0:T(8,128)S(1)}, f32[8,128]{1,0:T(8,128)S(1)}, u32[]{:S(2)}, u32[]{:S(2)}) collective-permute-start(f32[8,128]{1,0:T(8,128)S(1)} %get-tuple-element.96), channel_id=1, source_target_pairs={{0,16},{16,0},{1,17},{17,1},{2,18},{18,2},{3,19},{19,3},{4,20},{20... | collective-permute-start | bytes 12296 | tf_op jit(solution)/shard_map/ppermute | solution.py:219
  41.1 9.7 %collective-permute-start.12 = (f32[8,128]{1,0:T(8,128)S(1)}, f32[8,128]{1,0:T(8,128)S(1)}, u32[]{:S(2)}, u32[]{:S(2)}) collective-permute-start(f32[8,128]{1,0:T(8,128)S(1)} %add.3.refs_0_), channel_id=1, source_target_pairs={{0,3},{1,2},{2,1},{3,0},{4,7},{5,6},{6,5},{7,4},{8,11},{9,10},{10,... | collective-permute-start | bytes 12296 | tf_op jit(solution)/shard_map/ppermute | solution.py:219
  43.5 11.1 %collective-permute-start.13 = (bf16[384,128]{1,0:T(8,128)(2,1)S(1)}, bf16[384,128]{1,0:T(8,128)(2,1)S(1)}, u32[]{:S(2)}, u32[]{:S(2)}) collective-permute-start(bf16[384,128]{1,0:T(8,128)(2,1)S(1)} %get-tuple-element.97), channel_id=1, source_target_pairs={{0,4},{4,8},{8,12},{12,0},{1,5},{5,9},{9,13},{13,1},{2,6},{6,10},{... | collective-permute-start | bytes 294920 | tf_op jit(solution)/shard_map/ppermute | solution.py:214
  45.5 11.1 %collective-permute-start.14 = (bf16[384,128]{1,0:T(8,128)(2,1)S(1)}, bf16[384,128]{1,0:T(8,128)(2,1)S(1)}, u32[]{:S(2)}, u32[]{:S(2)}) collective-permute-start(bf16[384,128]{1,0:T(8,128)(2,1)S(1)} %get-tuple-element.99), channel_id=1, source_target_pairs={{0,8},{4,12},{8,0},{12,4},{1,9},{5,13},{9,1},{13,5},{2,10},{6,14},... | collective-permute-start | bytes 294920 | tf_op jit(solution)/shard_map/ppermute | solution.py:214
  45.8 10.9 %collective-permute-start.15 = (bf16[384,128]{1,0:T(8,128)(2,1)S(1)}, bf16[384,128]{1,0:T(8,128)(2,1)S(1)}, u32[]{:S(2)}, u32[]{:S(2)}) collective-permute-start(bf16[384,128]{1,0:T(8,128)(2,1)S(1)} %get-tuple-element.101), channel_id=1, source_target_pairs={{0,12},{4,0},{8,4},{12,8},{1,13},{5,1},{9,5},{13,9},{2,14},{6,2},{... | collective-permute-start | bytes 294920 | tf_op jit(solution)/shard_map/ppermute | solution.py:214
  48.6 5.9 %collective-permute-start.11 = (f32[8,128]{1,0:T(8,128)S(1)}, f32[8,128]{1,0:T(8,128)S(1)}, u32[]{:S(2)}, u32[]{:S(2)}) collective-permute-start(f32[8,128]{1,0:T(8,128)S(1)} %add.3.refs_0_), channel_id=1, source_target_pairs={{0,2},{1,3},{2,0},{3,1},{4,6},{5,7},{6,4},{7,5},{8,10},{9,11},{10,... | collective-permute-start | bytes 12296 | tf_op jit(solution)/shard_map/ppermute | solution.py:219
  50.8 3.8 %collective-permute-start.10 = (f32[8,128]{1,0:T(8,128)S(1)}, f32[8,128]{1,0:T(8,128)S(1)}, u32[]{:S(2)}, u32[]{:S(2)}) collective-permute-start(f32[8,128]{1,0:T(8,128)S(1)} %add.3.refs_0_), channel_id=1, source_target_pairs={{0,1},{1,0},{2,3},{3,2},{4,5},{5,4},{6,7},{7,6},{8,9},{9,8},{10,11... | collective-permute-start | bytes 12296 | tf_op jit(solution)/shard_map/ppermute | solution.py:219
  54.6 5.9 %collective-permute-start.16 = (bf16[144,128]{1,0:T(8,128)(2,1)S(1)}, bf16[144,128]{1,0:T(8,128)(2,1)S(1)}, u32[]{:S(2)}, u32[]{:S(2)}) collective-permute-start(bf16[144,128]{1,0:T(8,128)(2,1)S(1)} %join.1.refs_4_), channel_id=1, source_target_pairs={{0,4},{4,8},{8,12},{12,0},{1,5},{5,9},{9,13},{13,1},{2,6},{6,10},{... | collective-permute-start | bytes 110600 | tf_op jit(solution)/shard_map/ppermute | solution.py:214
  56.7 4.9 %collective-permute-start.17 = (bf16[144,128]{1,0:T(8,128)(2,1)S(1)}, bf16[144,128]{1,0:T(8,128)(2,1)S(1)}, u32[]{:S(2)}, u32[]{:S(2)}) collective-permute-start(bf16[144,128]{1,0:T(8,128)(2,1)S(1)} %join.1.refs_4_), channel_id=1, source_target_pairs={{0,8},{4,12},{8,0},{12,4},{1,9},{5,13},{9,1},{13,5},{2,10},{6,14},... | collective-permute-start | bytes 110600 | tf_op jit(solution)/shard_map/ppermute | solution.py:214
  56.7 4.9 %collective-permute-start.18 = (bf16[144,128]{1,0:T(8,128)(2,1)S(1)}, bf16[144,128]{1,0:T(8,128)(2,1)S(1)}, u32[]{:S(2)}, u32[]{:S(2)}) collective-permute-start(bf16[144,128]{1,0:T(8,128)(2,1)S(1)} %join.1.refs_4_), channel_id=1, source_target_pairs={{0,12},{4,0},{8,4},{12,8},{1,13},{5,1},{9,5},{13,9},{2,14},{6,2},{... | collective-permute-start | bytes 110600 | tf_op jit(solution)/shard_map/ppermute | solution.py:214
